TPU v7x, 32 devices: a whole 2x2x4 slice. The times are simulated.
32 devices in a mesh: dp: 16 (over z, y, core), mp: 2 (over x).
Axes of the slice: x: 2, y: 2, z: 4, core: 2. Of those that a mesh axis runs over, the one named last changes fastest.
Arguments:
- tokens: float32 [128, 256, 1152], P(('dp', 'mp')), may hold values from -6 to 6
- cotangent: float32 [128, 256, 1152], P(('dp', 'mp')), may hold values from -6 to 6
- bucket: int32 [128], P('dp'), may hold values from 0 to 63
- counts: int32 [16], replicated, may hold values from 1 to 8, as said below
- first_gain: float32 [1152], replicated, may hold values from 0.5 to 1.5
- first_shift: float32 [1152], replicated, may hold values from -1.75 to 1.75
- attend_weight: float32 [3, 1152, 1152], P(None, None, 'mp'), may hold values from -0.1875 to 0.1875
- time_weight: float32 [3, 1152, 1152], P(None, None, 'mp'), may hold values from -0.1875 to 0.1875
- time_table: float32 [64, 1152], replicated, may hold values from -6 to 6
- bias_table: float32 [16, 961], P('mp'), may hold values from -3 to 3
- output_weight: float32 [1152, 1152], P('mp'), may hold values from -0.5 to 0.5
- output_bias: float32 [1152], replicated, may hold values from -1.75 to 1.75
- second_gain: float32 [1152], replicated, may hold values from 0.5 to 1.5
- second_shift: float32 [1152], replicated, may hold values from -1.75 to 1.75
- hidden_weight: float32 [1152, 4608], P(None, 'mp'), may hold values from -0.1875 to 0.1875
- hidden_bias: float32 [4608], P('mp'), may hold values from -3 to 3
- return_weight: float32 [4608, 1152], P('mp'), may hold values from -0.09375 to 0.09375
- return_bias: float32 [1152], replicated, may hold values from -1.75 to 1.75
Outputs:
- result: float32 [128, 256, 1152], P(('dp', 'mp'))
- tokens_grad: float32 [128, 256, 1152], P(('dp', 'mp'))
- first_gain_grad: float32 [1152], replicated
- first_shift_grad: float32 [1152], replicated
- attend_weight_grad: float32 [3, 1152, 1152], P(None, None, 'mp')
- time_weight_grad: float32 [3, 1152, 1152], P(None, None, 'mp')
- time_table_grad: float32 [64, 1152], replicated
- bias_table_grad: float32 [16, 961], P('mp')
- output_weight_grad: float32 [1152, 1152], P('mp')
- output_bias_grad: float32 [1152], replicated
- second_gain_grad: float32 [1152], replicated
- second_shift_grad: float32 [1152], replicated
- hidden_weight_grad: float32 [1152, 4608], P(None, 'mp')
- hidden_bias_grad: float32 [4608], P('mp')
- return_weight_grad: float32 [4608, 1152], P('mp')
- return_bias_grad: float32 [1152], replicated
Inputs may be any that keep to these rules, and one draw needn't show every extreme that they name: Group g holds its live images in its first counts[g] slots; some group has all 8 slots live.
All inputs are finite; a program needn't handle non-finite values.
Results may differ from a plain program's by a relative error of at most 0.0003.
Values sent between devices are 32-bit elements; how exact they have to be, the bound alone decides.
No kernel may reach another device: no remote copies, remote signals or barrier semaphores. Data moves between devices by JAX's collectives and lax.ppermute only.
A program may use at most 384 MiB of HBM per device.

v0:
```python
import math

import jax
import jax.numpy as jnp
from jax import lax
from jax.sharding import PartitionSpec as P

HEAD_DIM = 72
SIDE = 16


HIGH = lax.Precision.HIGHEST
EPS = 1e-05


def standardize(values):
    centre = values - jnp.mean(values, -1, keepdims=True)
    inverse = lax.rsqrt(jnp.mean(centre * centre, -1, keepdims=True) + EPS)
    return (centre * inverse, inverse)


def norm_back(grad_hat, scaled, inverse):
    return inverse * (
        grad_hat
        - jnp.mean(grad_hat, -1, keepdims=True)
        - scaled * jnp.mean(grad_hat * scaled, -1, keepdims=True)
    )


def relative_index(side):
    place = jnp.arange(side * side, dtype=jnp.int32)
    rows = place // side
    cols = place % side
    return (
        (rows[:, None] - rows[None, :] + side - 1) * (2 * side - 1)
        + cols[:, None]
        - cols[None, :]
        + side
        - 1
    )


def attention_scores(query, keys, bias):
    scores = jnp.einsum("sphe,sqhe->shpq", query, keys, precision=HIGH) * HEAD_DIM ** (-0.5)
    return scores + bias[None]


def body(
    tokens,
    cotangent,
    bucket,
    counts,
    first_gain,
    first_shift,
    attend_weight,
    time_weight,
    time_table,
    bias_table,
    output_weight,
    output_bias,
    second_gain,
    second_shift,
    hidden_weight,
    hidden_bias,
    return_weight,
    return_bias,
):
    own_images = tokens.shape[0]
    images = bucket.shape[0]
    patches = SIDE * SIDE
    heads_local = bias_table.shape[0]
    width_local = attend_weight.shape[2]
    group = lax.axis_index("dp")
    offset_start = lax.axis_index("mp") * own_images
    live = (offset_start + jnp.arange(own_images) < counts[group]).astype(jnp.float32)
    inv_total = 1.0 / jnp.sum(counts).astype(jnp.float32)
    scaled_first, inverse_first = standardize(tokens)
    normed_part = scaled_first * first_gain + first_shift
    normed_first = lax.all_gather(normed_part, "mp", axis=0, tiled=True)
    onehot = (bucket[:, None] == jnp.arange(time_table.shape[0])[None, :]).astype(jnp.float32)
    time_vec = jnp.dot(onehot, time_table, precision=HIGH)
    proj = jnp.einsum("spd,cde->cspe", normed_first, attend_weight, precision=HIGH)
    proj = proj + jnp.einsum("sd,cde->cse", time_vec, time_weight, precision=HIGH)[:, :, None, :]
    split = proj.reshape(3, images, patches, heads_local, HEAD_DIM)
    query, keys, values = (split[0], split[1], split[2])
    offsets = relative_index(SIDE)
    bias, bias_pull = jax.vjp(lambda table: table[:, offsets], bias_table)
    scores = attention_scores(query, keys, bias)
    peak = jnp.max(scores, -1, keepdims=True)
    log_total = peak + jnp.log(jnp.sum(jnp.exp(scores - peak), -1, keepdims=True))
    prob = jnp.exp(scores - log_total)
    mixed_heads = jnp.einsum("shpq,sqhe->sphe", prob, values, precision=HIGH)
    mixed = mixed_heads.reshape(images, patches, width_local)
    attend_terms = jnp.einsum("spe,ed->spd", mixed, output_weight, precision=HIGH)
    middle = (
        tokens + lax.psum_scatter(attend_terms, "mp", scatter_dimension=0, tiled=True) + output_bias
    )
    scaled_second, inverse_second = standardize(middle)
    second_part = scaled_second * second_gain + second_shift
    normed_second = lax.all_gather(second_part, "mp", axis=0, tiled=True)
    hidden = jnp.einsum("spd,df->spf", normed_second, hidden_weight, precision=HIGH) + hidden_bias
    cumul = 0.5 * (1.0 + lax.erf(hidden * 2.0 ** (-0.5)))
    active = hidden * cumul
    mixer_terms = jnp.einsum("spf,fd->spd", active, return_weight, precision=HIGH)
    result = (
        middle + lax.psum_scatter(mixer_terms, "mp", scatter_dimension=0, tiled=True) + return_bias
    )
    grad_out = cotangent * live[:, None, None]
    grad_full = lax.all_gather(grad_out, "mp", axis=0, tiled=True)
    return_weight_grad = jnp.einsum("spf,spd->fd", active, grad_full, precision=HIGH)
    return_bias_grad = jnp.sum(grad_out, (0, 1))
    d_active = jnp.einsum("spd,fd->spf", grad_full, return_weight, precision=HIGH)
    density = hidden * jnp.exp(-0.5 * hidden * hidden) / math.sqrt(2.0 * math.pi)
    d_hidden = d_active * (cumul + density)
    hidden_weight_grad = jnp.einsum("spd,spf->df", normed_second, d_hidden, precision=HIGH)
    hidden_bias_grad = jnp.sum(d_hidden, (0, 1))
    second_terms = jnp.einsum("spf,df->spd", d_hidden, hidden_weight, precision=HIGH)
    d_second = lax.psum_scatter(second_terms, "mp", scatter_dimension=0, tiled=True)
    second_gain_grad = jnp.sum(d_second * scaled_second, (0, 1))
    second_shift_grad = jnp.sum(d_second, (0, 1))
    d_middle = grad_out + norm_back(d_second * second_gain, scaled_second, inverse_second)
    output_bias_grad = jnp.sum(d_middle, (0, 1))
    middle_full = lax.all_gather(d_middle, "mp", axis=0, tiled=True)
    output_weight_grad = jnp.einsum("spe,spd->ed", mixed, middle_full, precision=HIGH)
    d_mixed = jnp.einsum("spd,ed->spe", middle_full, output_weight, precision=HIGH)
    d_heads = d_mixed.reshape(images, patches, heads_local, HEAD_DIM)
    again = jnp.exp(attention_scores(query, keys, bias) - log_total)
    d_prob = jnp.einsum("sphe,sqhe->shpq", d_heads, values, precision=HIGH)
    delta = jnp.transpose(jnp.sum(d_heads * mixed_heads, -1), (0, 2, 1))[..., None]
    d_scores = again * (d_prob - delta)
    d_values = jnp.einsum("shpq,sphe->sqhe", again, d_heads, precision=HIGH)
    d_query = jnp.einsum("shpq,sqhe->sphe", d_scores, keys, precision=HIGH) * HEAD_DIM ** (-0.5)
    d_keys = jnp.einsum("shpq,sphe->sqhe", d_scores, query, precision=HIGH) * HEAD_DIM ** (-0.5)
    (bias_table_grad,) = bias_pull(jnp.sum(d_scores, 0))
    d_proj = jnp.stack([d_query, d_keys, d_values]).reshape(3, images, patches, width_local)
    attend_weight_grad = jnp.einsum("spd,cspe->cde", normed_first, d_proj, precision=HIGH)
    d_time = jnp.sum(d_proj, 2)
    time_weight_grad = jnp.einsum("sd,cse->cde", time_vec, d_time, precision=HIGH)
    d_time_vec = jnp.einsum("cse,cde->sd", d_time, time_weight, precision=HIGH)
    time_table_grad = jnp.dot(onehot.T, d_time_vec, precision=HIGH)
    first_terms = jnp.einsum("cspe,cde->spd", d_proj, attend_weight, precision=HIGH)
    d_first = lax.psum_scatter(first_terms, "mp", scatter_dimension=0, tiled=True)
    first_gain_grad = jnp.sum(d_first * scaled_first, (0, 1))
    first_shift_grad = jnp.sum(d_first, (0, 1))
    tokens_grad = d_middle + norm_back(d_first * first_gain, scaled_first, inverse_first)
    (
        attend_weight_sum,
        time_weight_sum,
        bias_table_sum,
        output_weight_sum,
        hidden_weight_sum,
        hidden_bias_sum,
        return_weight_sum,
    ) = lax.psum(
        (
            attend_weight_grad * inv_total,
            time_weight_grad * inv_total,
            bias_table_grad * inv_total,
            output_weight_grad * inv_total,
            hidden_weight_grad * inv_total,
            hidden_bias_grad * inv_total,
            return_weight_grad * inv_total,
        ),
        "dp",
    )
    (
        first_gain_sum,
        first_shift_sum,
        time_table_sum,
        output_bias_sum,
        second_gain_sum,
        second_shift_sum,
        return_bias_sum,
    ) = lax.psum(
        (
            first_gain_grad * inv_total,
            first_shift_grad * inv_total,
            time_table_grad * inv_total,
            output_bias_grad * inv_total,
            second_gain_grad * inv_total,
            second_shift_grad * inv_total,
            return_bias_grad * inv_total,
        ),
        ("dp", "mp"),
    )
    return (
        result,
        tokens_grad,
        first_gain_sum,
        first_shift_sum,
        attend_weight_sum,
        time_weight_sum,
        time_table_sum,
        bias_table_sum,
        output_weight_sum,
        output_bias_sum,
        second_gain_sum,
        second_shift_sum,
        hidden_weight_sum,
        hidden_bias_sum,
        return_weight_sum,
        return_bias_sum,
    )


def solution(mesh):
    in_specs = (
        P(("dp", "mp"), None, None),
        P(("dp", "mp"), None, None),
        P("dp"),
        P(),
        P(),
        P(),
        P(None, None, "mp"),
        P(None, None, "mp"),
        P(),
        P("mp", None),
        P("mp", None),
        P(),
        P(),
        P(),
        P(None, "mp"),
        P("mp"),
        P("mp", None),
        P(),
    )
    out_specs = (
        P(("dp", "mp"), None, None),
        P(("dp", "mp"), None, None),
        P(),
        P(),
        P(None, None, "mp"),
        P(None, None, "mp"),
        P(),
        P("mp", None),
        P("mp", None),
        P(),
        P(),
        P(),
        P(None, "mp"),
        P("mp"),
        P("mp", None),
        P(),
    )
    return jax.shard_map(body, mesh=mesh, in_specs=in_specs, out_specs=out_specs, check_vma=False)
```

profile of v0, /device:TPU:0, one launch (start us, length us, event | category | flops | bytes accessed | tf_op | source)
XLA Modules:
  0.0 2527.4 jit_solution(2900430065042946791)
XLA Ops:
  17.1 8.6 convolution_bitcast_fusion.5
  28.0 215.5 %gather_fusion = f32[65536,8]{1,0:T(8,128)} fusion(f32[8,961]{0,1:T(8,128)S(1)} %copy.81, s32[65536]{0:T(1024)S(1)} %broadcast_clamp_fusion), kind=kCustom, calls=%fused_computation | custom fusion | bytes 4456448 | tf_op jit(solution)/shard_map/jvp()/gather | solution.py:87
  243.5 19.5 copy.82
  263.1 61.4 %bitcast_add_fusion = f32[3,8,256,576]{2,3,0,1:T(8,128)} fusion(f32[8,256,1152]{2,1,0:T(8,128)} %all-gather.5.cloned.1.call-done, f32[3,1152,576]{1,2,0:T(8,128)} %param.24, f32[3,8,576]{2,0,1:T(4,128)S(1)} %copy.80), kind=kOutput, calls=%fused_computation.15 | convolution fusion | flops 48925900800 | bytes 31610880 | tf_op jit(solution)/shard_map/spd,cde->cspe/dot_general | solution.py:82
  324.4 10.5 fusion.64
  334.9 21.8 fusion.7
  356.7 10.6 exponential_reduce_fusion
  367.4 23.0 fusion.25
  390.4 28.7 %fusion.46 = f32[8,256,1152]{2,1,0:T(8,128)} fusion(f32[8,256,576]{1,2,0:T(8,128)} %bitcast.154, f32[576,1152]{1,0:T(8,128)S(1)} %copy-done), kind=kOutput, calls=%fused_computation.71 | convolution fusion | flops 16307453952 | bytes 16809984 | tf_op jit(solution)/shard_map/spe,ed->spd/dot_general | solution.py:94
  419.3 113.3 %reduce-scatter.5.cloned.1.call-done = f32[4,256,1152]{2,1,0:T(8,128)} async-done(((f32[8,256,1152]{2,1,0:T(8,128)}), f32[4,256,1152]{2,1,0:T(8,128)}) %reduce-scatter.5.cloned.1.call-update) | async-done | bytes 4718608 | tf_op jit(solution)/shard_map/reduce_scatter | solution.py:96
  532.6 4.4 fusion.63
  543.4 5.6 fusion.61
  549.1 111.2 %all-gather.7.cloned.1.call-done = f32[8,256,1152]{2,1,0:T(8,128)} async-done(((f32[4,256,1152]{2,1,0:T(8,128)}), f32[8,256,1152]{2,1,0:T(8,128)}) %all-gather.7.cloned.1.call-update) | async-done | bytes 9437200 | tf_op jit(solution)/shard_map/all_gather | solution.py:100
  660.3 92.3 %fusion.14 = f32[8,256,2304]{2,1,0:T(8,128)} fusion(f32[8,256,1152]{2,1,0:T(8,128)} %all-gather.7.cloned.1.call-done, f32[1152,2304]{1,0:T(8,128)} %param.32), kind=kOutput, calls=%fused_computation.27 | convolution fusion | flops 65229815808 | bytes 38928384 | tf_op jit(solution)/shard_map/spd,df->spf/dot_general | solution.py:101
  752.6 27.7 %all-gather.9.cloned.1.call-done = f32[8,256,1152]{2,1,0:T(8,128)} async-done(((f32[4,256,1152]{2,1,0:T(8,128)}), f32[8,256,1152]{2,1,0:T(8,128)}) %all-gather.9.cloned.1.call-update) | async-done | bytes 9437200 | tf_op jit(solution)/shard_map/all_gather | solution.py:109
  780.3 92.3 %fusion.66 = (f32[2304]{0:T(1024)}, f32[8,256,2304]{2,1,0:T(8,128)}) fusion(f32[8,256,2304]{2,1,0:T(8,128)} %fusion.14, f32[2304]{0:T(1024)S(1)} %copy-done.32, f32[8,256,1152]{2,1,0:T(8,128)} %all-gather.9.cloned.1.call-done, f32[2304,1152]{1,0:T(8,128)} %param.34), kind=kOutput, calls=%fused_computation.124 | convolution fusion | flops 65281720320 | bytes 57821184 | tf_op jit(solution)/shard_map/spd,fd->spf/dot_general | solution.py:112
  872.6 82.6 %fusion.12 = f32[8,256,1152]{2,1,0:T(8,128)} fusion(f32[8,256,2304]{2,1,0:T(8,128)} %get-tuple-element.116, f32[1152,2304]{1,0:T(8,128)} %param.32), kind=kOutput, calls=%fused_computation.25 | convolution fusion | flops 65229815808 | bytes 38928384 | tf_op jit(solution)/shard_map/spf,df->spd/dot_general | solution.py:117
  955.3 86.5 %fusion.10 = f32[8,256,1152]{2,1,0:T(8,128)} fusion(f32[2304,1152]{1,0:T(8,128)} %param.34, f32[8,256,2304]{2,1,0:T(8,128)} %fusion.14, f32[2304]{0:T(1024)S(1)} %copy-done.32), kind=kOutput, calls=%fused_computation.23 | convolution fusion | flops 65253408768 | bytes 38937600 | tf_op jit(solution)/shard_map/spf,fd->spd/dot_general | solution.py:104
  1041.8 24.1 reduce-scatter.9.cloned.1.call-done
  1066.0 5.4 multiply_reduce_fusion
  1071.3 107.9 %reduce-scatter.7.cloned.1.call-done = f32[4,256,1152]{2,1,0:T(8,128)} async-done(((f32[8,256,1152]{2,1,0:T(8,128)}), f32[4,256,1152]{2,1,0:T(8,128)}) %reduce-scatter.7.cloned.1.call-update) | async-done | bytes 4718608 | tf_op jit(solution)/shard_map/reduce_scatter | solution.py:106
  1179.3 11.8 fusion.62
  1191.2 118.1 %all-gather.11.cloned.1.call-done = f32[8,256,1152]{2,1,0:T(8,128)} async-done(((f32[4,256,1152]{2,1,0:T(8,128)}), f32[8,256,1152]{2,1,0:T(8,128)}) %all-gather.11.cloned.1.call-update) | async-done | bytes 9437200 | tf_op jit(solution)/shard_map/all_gather | solution.py:123
  1309.3 21.8 fusion.44
  1333.4 3.4 fusion.42
  1336.9 27.5 %fusion.24 = f32[8,8,72,256]{3,2,1,0:T(8,128)} fusion(f32[8,256,8,72]{1,3,2,0:T(8,128)} %bitcast.149, f32[8,8,256,256]{2,3,1,0:T(8,128)} %get-tuple-element.112, f32[8,8,256]{2,1,0:T(8,128)S(1)} %log_add_fusion, f32[8,256,256]{1,2,0:T(8,128)S(1)} %bitcast.140), kind=kOutput, calls=%fused_computation.33 | convolution fusion | flops 3636461568 | bytes 28377088 | tf_op jit(solution)/shard_map/shpq,sphe->sqhe/dot_general | solution.py:131
  1364.4 28.6 %fusion.65 = (f32[8,256,256]{1,2,0:T(8,128)}, f32[8,8,256,256]{2,3,1,0:T(8,128)}) fusion(f32[8,8,256]{2,1,0:T(8,128)S(1)} %bitcast.171, f32[8,256,8,72]{1,3,2,0:T(8,128)} %bitcast.150, f32[8,256,8,72]{1,3,2,0:T(8,128)} %bitcast.147, f32[8,8,256]{2,1,0:T(8,128)S(1)} %log_add_fusion, f32[8,256,256]{1,2,0:T(8,128)S(1)} %bitcast.141, ...), kind=kOutput, calls=%fused_computation.123 | convolution fusion | flops 3648520192 | bytes 47316992 | tf_op jit(solution)/shard_map/sphe,sqhe->shpq/dot_general | solution.py:128
  1393.0 26.2 %broadcast_multiply_fusion = f32[8,8,72,256]{3,2,1,0:T(8,128)} fusion(f32[8,256,8,72]{1,3,2,0:T(8,128)} %bitcast.145, f32[8,8,256,256]{2,3,1,0:T(8,128)} %get-tuple-element.114), kind=kOutput, calls=%fused_computation.74 | convolution fusion | flops 3625058304 | bytes 26214400 | tf_op jit(solution)/shard_map/shpq,sphe->sqhe/dot_general | solution.py:133
  1419.2 20.1 broadcast_multiply_fusion.1
  1439.3 66.6 %fusion.36 = f32[8,256,1152]{2,1,0:T(8,128)} fusion(f32[3,1152,576]{1,2,0:T(8,128)} %param.24, f32[1,8,256,576]{2,3,0,1:T(8,128)} %bitcast.156, f32[1,8,256,576]{2,3,0,1:T(8,128)} %bitcast.159, f32[1,8,256,576]{2,3,0,1:T(8,128)} %bitcast.162), kind=kOutput, calls=%fused_computation.47 | convolution fusion | flops 48929439744 | bytes 31555584 | tf_op jit(solution)/shard_map/cspe,cde->spd/dot_general | solution.py:141
  1507.9 75.8 %fusion.5 = f32[1152,2304]{1,0:T(8,128)} fusion(f32[8,256,1152]{2,1,0:T(8,128)} %all-gather.7.cloned.1.call-done, f32[8,256,2304]{2,1,0:T(8,128)} %get-tuple-element.116, f32[]{:T(128)S(6)} %div.55), kind=kOutput, calls=%fused_computation.17 | convolution fusion | flops 65232470016 | bytes 38928388 | tf_op jit(solution)/shard_map/spd,spf->df/dot_general | solution.py:115
  1583.8 85.5 %fusion.6 = f32[2304,1152]{1,0:T(8,128)} fusion(f32[8,256,1152]{2,1,0:T(8,128)} %all-gather.9.cloned.1.call-done, f32[8,256,2304]{2,1,0:T(8,128)} %fusion.14, f32[2304]{0:T(1024)S(1)} %copy-done.32, f32[]{:T(128)S(6)} %div.55), kind=kOutput, calls=%fused_computation.19 | convolution fusion | flops 65256062976 | bytes 38937604 | tf_op jit(solution)/shard_map/spf,spd->fd/dot_general | solution.py:110
  1669.2 6.5 fusion.39
  1675.7 3.9 convolution_bitcast_fusion.3
  1680.8 27.2 %fusion.43 = f32[576,1152]{1,0:T(8,128)} fusion(f32[8,256,576]{1,2,0:T(8,128)} %bitcast.155, f32[8,256,1152]{2,1,0:T(8,128)} %all-gather.11.cloned.1.call-done, f32[]{:T(128)S(6)} %div.55), kind=kOutput, calls=%fused_computation.68 | convolution fusion | flops 16308117504 | bytes 16809988 | tf_op jit(solution)/shard_map/spe,spd->ed/dot_general | solution.py:124
  1708.0 63.1 %fusion.32 = f32[3,1152,576]{1,2,0:T(8,128)} fusion(f32[8,256,1152]{2,1,0:T(8,128)} %all-gather.5.cloned.1.call-done, f32[1,8,256,576]{2,3,0,1:T(8,128)} %bitcast.158, f32[1,8,256,576]{2,3,0,1:T(8,128)} %bitcast.161, f32[1,8,256,576]{2,3,0,1:T(8,128)} %bitcast.164, f32[]{:T(128)S(6)} %div.55), kind=kOutput, calls=%fused_computation.42 | convolution fusion | flops 48931430400 | bytes 31555588 | tf_op jit(solution)/shard_map/spd,cspe->cde/dot_general | solution.py:136
  1771.1 8.6 multiply_bitcast_fusion
  1783.3 16.4 copy.94
  1799.7 347.5 %scatter_custom_fusion = f32[8,961]{0,1:T(8,128)S(1)} fusion(s32[65536]{0:T(1024)} %bitcast.170, f32[65536,8]{1,0:T(8,128)} %copy.94, f32[]{:T(128)} %constant.70.clone.1), kind=kCustom, calls=%fused_computation.83 | custom fusion | flops 524288 | bytes 31264 | tf_op jit(solution)/shard_map/transpose(jvp())/scatter-add | solution.py:87
  2147.2 75.7 %all-reduce.1 = (f32[8,961]{0,1:T(8,128)S(1)}, f32[2304]{0:T(1024)}) all-reduce(f32[8,961]{0,1:T(8,128)S(1)} %broadcast_multiply_fusion.3, f32[2304]{0:T(1024)S(1)} %broadcast_multiply_fusion.4), channel_id=1, replica_groups=mesh['dp'=16,'mp'=2] {'dp'}, use_global_device_ids=true, to_apply=%region_26.27 | all-reduce | flops 9992 | bytes 79936 | tf_op jit(solution)/shard_map/psum | solution.py:154
  2223.7 4.8 multiply_reduce_fusion.1
  2228.6 40.3 %all-reduce = (f32[1152]{0:T(1024)}, f32[1152]{0:T(1024)}, f32[1152]{0:T(1024)}, f32[1152]{0:T(1024)}, f32[1152]{0:T(1024)}, /*index=5*/f32[1152]{0:T(1024)}) all-reduce(f32[1152]{0:T(1024)S(1)} %broadcast_multiply_fusion.10, f32[1152]{0:T(1024)S(1)} %broadcast_multiply_fusion.9, ...), channel_id=1, replica_groups=mesh['dp'=16,'mp'=2] {'dp','mp'}, use_global_device_ids=true, to_apply=%region_17.18 | all-reduce | flops 6912 | bytes 55296 | tf_op jit(solution)/shard_map/psum | solution.py:174
  2268.9 8.2 multiply_add_fusion.1
  2277.1 215.9 %all-reduce.8.cloned.1.call-done = (f32[3,1152,576]{1,2,0:T(8,128)}, f32[3,1152,576]{1,2,0:T(8,128)}, f32[576,1152]{1,0:T(8,128)}, f32[1152,2304]{1,0:T(8,128)}, f32[2304,1152]{1,0:T(8,128)}) async-done(((f32[3,1152,576]{1,2,0:T(8,128)}, f32[3,1152,576]{1,2,0:T(8,128)}, f32[576,1152]{1,0:T(8,128)}, f32[1152,2304]{1,0:T(8,128)}, f32[2304,1152]{1,0:T(8,128)}), (f32[3,1152,576]{1,2,0:T(8,128)}, ...) | async-done | bytes 39813136 | tf_op jit(solution)/shard_map/psum | solution.py:154
  2493.0 7.3 copy.118
  2500.3 3.7 copy.119
  2506.2 10.0 copy.122
  2516.2 4.1 copy.123
  (142 shorter events, 30.2 us)
Async XLA Ops:
  7.2 383.2 %copy-start = (f32[576,1152]{1,0:T(8,128)S(1)}, f32[576,1152]{1,0:T(8,128)}, u32[]{:S(2)}) copy-start(f32[576,1152]{1,0:T(8,128)} %param.28) | copy-start | bytes 7962628
  7.2 6.6 copy-start.15
  7.2 6.6 copy-start.28
  7.2 255.8 %all-gather.5.cloned.1.call-start = ((), (), s32[]{:S(2)}) async-start(), calls=%async_computation.4 | async-start | bytes 14155776 | tf_op jit(solution)/shard_map/all_gather | solution.py:79
  10.0 3.8 copy-start.2
  10.1 3.1 copy-start.13
  13.2 3.7 copy-start.12
  13.2 3.7 copy-start.30
  16.8 10.0 copy-start.21
  16.8 515.8 %reduce-scatter.5.cloned.1.call-start = ((), (), s32[]{:S(2)}) async-start(), calls=%async_computation.5 | async-start | bytes 14155776 | tf_op jit(solution)/shard_map/reduce_scatter | solution.py:96
  17.1 8.8 copy-start.9
  419.1 113.5 %copy-start.26 = (f32[1152]{0:T(1024)S(1)}, f32[1152]{0:T(1024)}, u32[]{:S(2)}) copy-start(f32[1152]{0:T(1024)} %param.29) | copy-start | bytes 13828
  419.2 119.9 %copy-start.17 = (f32[1152]{0:T(1024)S(1)}, f32[1152]{0:T(1024)}, u32[]{:S(2)}) copy-start(f32[1152]{0:T(1024)} %param.30) | copy-start | bytes 13828
  419.2 119.9 %copy-start.29 = (f32[1152]{0:T(1024)S(1)}, f32[1152]{0:T(1024)}, u32[]{:S(2)}) copy-start(f32[1152]{0:T(1024)} %param.31) | copy-start | bytes 13828
  419.2 241.1 %all-gather.7.cloned.1.call-start = ((), (), s32[]{:S(2)}) async-start(), calls=%async_computation.6 | async-start | bytes 14155776 | tf_op jit(solution)/shard_map/all_gather | solution.py:100
  537.0 2.1 copy-start.3
  537.6 4.5 copy-start.33
  542.1 238.2 %all-gather.9.cloned.1.call-start = ((), (), s32[]{:S(2)}) async-start(), calls=%async_computation.8 | async-start | bytes 14155776 | tf_op jit(solution)/shard_map/all_gather | solution.py:109
  549.0 231.3 %copy-start.32 = (f32[2304]{0:T(1024)S(1)}, f32[2304]{0:T(1024)}, u32[]{:S(2)}) copy-start(f32[2304]{0:T(1024)} %param.33) | copy-start | bytes 27652
  549.0 517.0 %reduce-scatter.9.cloned.1.call-start = ((), (), s32[]{:S(2)}) async-start(), calls=%async_computation.9 | async-start | bytes 14155776 | tf_op jit(solution)/shard_map/reduce_scatter | solution.py:118
  955.3 224.0 %reduce-scatter.7.cloned.1.call-start = ((), (), s32[]{:S(2)}) async-start(), calls=%async_computation.7 | async-start | bytes 14155776 | tf_op jit(solution)/shard_map/reduce_scatter | solution.py:106
  1041.8 137.5 %copy-start.27 = (f32[1152]{0:T(1024)S(1)}, f32[1152]{0:T(1024)}, u32[]{:S(2)}) copy-start(f32[1152]{0:T(1024)} %param.35) | copy-start | bytes 13828
  1041.8 267.5 %all-gather.11.cloned.1.call-start = ((), (), s32[]{:S(2)}) async-start(), calls=%async_computation.10 | async-start | bytes 14155776 | tf_op jit(solution)/shard_map/all_gather | solution.py:123
  1191.1 1032.6 %reduce-scatter.11.cloned.1.call-start = ((), (), s32[]{:S(2)}) async-start(), calls=%async_computation.11 | async-start | bytes 14155776 | tf_op jit(solution)/shard_map/reduce_scatter | solution.py:142
  1331.1 2.3 copy-start.5
  1331.1 5.8 copy-start.4
  1506.0 771.1 %all-reduce.6.cloned.1.call-start = ((), (), s32[]{:S(2)}) async-start(), calls=%async_computation.12 | async-start | bytes 589824 | tf_op jit(solution)/shard_map/psum | solution.py:174
  1507.9 167.8 %slice-start = ((s8[7962624]{0:T(1024)(128)(4,1)}), s8[4194304]{0:T(1024)(128)(4,1)S(1)}, s32[]{:S(2)}) async-start(s8[7962624]{0:T(1024)(128)(4,1)} %bitcast.152), calls=%async_computation.14 | async-start | bytes 8388608
  1583.8 91.9 %slice-start.1 = ((s8[7962624]{0:T(1024)(128)(4,1)}), s8[3768320]{0:T(1024)(128)(4,1)S(1)}, s32[]{:S(2)}) async-start(s8[7962624]{0:T(1024)(128)(4,1)} %bitcast.152), calls=%async_computation.15 | async-start | bytes 7536640
  1669.2 10.4 copy-start.31
  1680.7 812.3 %all-reduce.8.cloned.1.call-start = ((), (), s32[]{:S(2)}) async-start(), calls=%async_computation.13 | async-start | bytes 79626240 | tf_op jit(solution)/shard_map/psum | solution.py:154
  1708.0 63.1 %copy-start.10 = (f32[8,1152,1]{1,0,2:T(8,128)S(1)}, f32[8,1152,1]{1,0,2:T(8,128)}, u32[]{:S(2)}) copy-start(f32[8,1152,1]{1,0,2:T(8,128)} %copy-done.9) | copy-start | bytes 110596
  1779.6 0.7 copy-start.22
  1779.6 0.7 copy-start.25
  1779.6 0.7 copy-start.24
  1779.6 0.7 copy-start.20
  1779.6 0.8 copy-start.23
  1779.6 1.6 copy-start.6
  1783.2 440.5 %copy-start.14 = (f32[4,256]{1,0:T(4,128)S(1)}, f32[4,256]{1,0:T(4,128)}, u32[]{:S(2)}) copy-start(f32[4,256]{1,0:T(4,128)} %copy-done.13) | copy-start | bytes 12292
  1783.2 440.5 %copy-start.16 = (f32[1152]{0:T(1024)S(1)}, f32[1152]{0:T(1024)}, u32[]{:S(2)}) copy-start(f32[1152]{0:T(1024)} %param.22) | copy-start | bytes 13828
  1783.3 440.5 %copy-start.19 = (f32[4,256]{1,0:T(4,128)S(1)}, f32[4,256]{1,0:T(4,128)}, u32[]{:S(2)}) copy-start(f32[4,256]{1,0:T(4,128)} %copy-done.18) | copy-start | bytes 12292
  2493.0 7.3 copy-start.7
  2500.3 3.7 copy-start.11
  2500.3 4.4 copy-start.8
  2504.7 11.5 slice-start.2
  2506.2 10.0 slice-start.3
  2506.2 10.0 slice-start.4
  2506.2 14.2 copy-start.1
  (2 other events, 1.3 us)
Sparse Core Ops, SparseCore 0:
  16.9 120.6 all-gather.4
  419.3 113.2 reduce-scatter.4
  542.2 118.0 all-gather.6
  662.3 117.9 all-gather.8
  955.4 110.5 reduce-scatter.8
  1068.7 110.5 reduce-scatter.6
  1191.3 117.9 all-gather.10
  1506.1 110.5 reduce-scatter.10
  1680.9 125.6 all-reduce.5
  1813.8 679.1 all-reduce.7
where the time goes:
time: 2530 us
  matrix products  953 us (38%)
  waiting for transfers between devices  719 us (28%)
  other arithmetic  423 us (17%)
  local copies, waits for them, and re-layouts  300 us (12%)
  blocking collectives  116 us (5%)
    scatter-add x1, other arithmetic, body(): bias, bias_pull = jax.vjp(lambda table: table[:, offsets], bias_table)  347 us
    gather x2, local copies, waits for them, and re-layouts, body(): bias, bias_pull = jax.vjp(lambda table: table[:, offsets], bias_table)  235 us
    psum x1, waiting for transfers between devices, body(): lax.psum((attend_weight_grad * inv_total, time_weight_grad * inv_total, b...  216 us
    all_gather x1, waiting for transfers between devices, body(): middle_full = lax.all_gather(d_middle, 'mp', axis=0, tiled=True)  118 us
    reduce_scatter x1, waiting for transfers between devices, body(): lax.psum_scatter(attend_terms, 'mp', scatter_dimension=0, tiled=True)  113 us
    all_gather x1, waiting for transfers between devices, body(): normed_second = lax.all_gather(second_part, 'mp', axis=0, tiled=True)  111 us
    reduce_scatter x1, waiting for transfers between devices, body(): lax.psum_scatter(mixer_terms, 'mp', scatter_dimension=0, tiled=True)  108 us
    dot_general x1, matrix products, body(): jnp.einsum('spd,df->spf', normed_second, hidden_weight, precision=HIGH)  92.3 us
  transfers between devices with their start and end apart: 10, of which 7 were waited for; matrix products, arithmetic and copies ran while one was open for 43% of the time, Pallas kernels for 0%

commit v1 on v0

v1 whole, which is shorter than its diff:
```python
import functools
import math

import jax
import jax.numpy as jnp
from jax import lax
from jax.experimental import pallas as pl
from jax.experimental.pallas import tpu as pltpu
from jax.sharding import PartitionSpec as P

HEAD_DIM = 72
SIDE = 16
PATCHES = SIDE * SIDE
STRIP = 2 * SIDE - 1
EPS = 1e-05
SCALE = HEAD_DIM ** (-0.5)
MIB = 1024 * 1024
HIGHEST = lax.Precision.HIGHEST
HIGH = lax.Precision.HIGH


def dot_nn(a, b):
    return lax.dot_general(a, b, (((1,), (0,)), ((), ())), precision=HIGH, preferred_element_type=jnp.float32)


def dot_nt(a, b):
    return lax.dot_general(a, b, (((1,), (1,)), ((), ())), precision=HIGH, preferred_element_type=jnp.float32)


def dot_tn(a, b):
    return lax.dot_general(a, b, (((0,), (0,)), ((), ())), precision=HIGH, preferred_element_type=jnp.float32)


def standardize(values):
    centre = values - jnp.mean(values, -1, keepdims=True)
    inverse = lax.rsqrt(jnp.mean(centre * centre, -1, keepdims=True) + EPS)
    return centre * inverse, inverse


def norm_back(grad_hat, scaled, inverse):
    return inverse * (
        grad_hat
        - jnp.mean(grad_hat, -1, keepdims=True)
        - scaled * jnp.mean(grad_hat * scaled, -1, keepdims=True)
    )


def head_window(head, width):
    first = head * HEAD_DIM
    start = first // 128 * 128
    stop = min(-(-(first + HEAD_DIM) // 128) * 128, width)
    return start, stop, first - start


def head_mask(head, width):
    start, stop, offset = head_window(head, width)
    lane = lax.broadcasted_iota(jnp.int32, (1, stop - start), 1)
    return (lane >= offset) & (lane < offset + HEAD_DIM)


def fixed(shape, **kw):
    return pl.BlockSpec(shape, lambda i: (0,) * len(shape), pipeline_mode=pl.Buffered(1), **kw)


def rows(count, width):
    return pl.BlockSpec((count, width), lambda i: (i, 0))


def params(limit):
    return pltpu.CompilerParams(dimension_semantics=("arbitrary",), vmem_limit_bytes=limit * MIB)


def cost(flops, nbytes, trans=0):
    return pl.CostEstimate(flops=int(flops) // 1000, bytes_accessed=int(nbytes) // 1000, transcendentals=0)


def halves(value):
    high = value.astype(jnp.bfloat16)
    return high, (value - high.astype(jnp.float32)).astype(jnp.bfloat16)


def mul(a, b, left, right):
    return lax.dot_general(a, b, (((left,), (right,)), ((), ())), preferred_element_type=jnp.float32)


def scalars():
    return pl.BlockSpec(memory_space=pltpu.SMEM)


def build_bias(strip_ref, bias_ref, heads):
    def one(head, carry):
        strip = strip_ref[head]
        for row in range(SIDE):
            shift = (SIDE - 1 - row) * SIDE
            bias_ref[head, row * SIDE : (row + 1) * SIDE, :] = strip[:, shift : shift + PATCHES]
        return carry

    lax.fori_loop(0, heads, one, 0)


def attend_forward_kernel(
    heads, tokens_ref, gain_ref, shift_ref, weight_ref, time_ref, strip_ref,
    query_ref, keys_ref, values_ref, mixed_ref, flipped_ref, lse_ref, normed_ref, bias_ref,
):
    width = query_ref.shape[1]

    @pl.when(pl.program_id(0) == 0)
    def _():
        build_bias(strip_ref, bias_ref, heads)

    scaled, _ = standardize(tokens_ref[...])
    normed = scaled * gain_ref[...] + shift_ref[...]
    normed_ref[...] = normed
    proj = dot_nt(normed, weight_ref[...]) + time_ref[0]
    query_ref[...] = proj[:, :width] * SCALE
    keys_ref[...] = proj[:, width : 2 * width]
    values_ref[...] = proj[:, 2 * width :]
    mixed_ref[...] = jnp.zeros_like(mixed_ref)
    columns = lax.broadcasted_iota(jnp.int32, (1, heads), 1)
    stats = jnp.zeros((PATCHES, heads), jnp.float32)
    for head in range(heads):
        start, stop, _ = head_window(head, width)
        mask = head_mask(head, width)
        query = jnp.where(mask, query_ref[:, start:stop], 0.0)
        scores = dot_nt(query, keys_ref[:, start:stop]) + bias_ref[head]
        peak = jnp.max(scores, -1, keepdims=True)
        weights = jnp.exp(scores - peak)
        total = jnp.sum(weights, -1, keepdims=True)
        values = jnp.where(mask, values_ref[:, start:stop], 0.0)
        mixed_ref[:, start:stop] += dot_nn(weights, values) * (1.0 / total)
        stats = jnp.where(columns == head, peak + jnp.log(total), stats)
    lse_ref[...] = stats
    flipped_ref[...] = mixed_ref[...].T


def attend_forward(tokens, gain, shift, weight, time_proj, strips):
    count, dim = tokens.shape
    heads = strips.shape[0]
    width = weight.shape[0] // 3
    images = count // PATCHES
    piece = jax.ShapeDtypeStruct((count, width), jnp.float32)
    return pl.pallas_call(
        functools.partial(attend_forward_kernel, heads),
        grid=(images,),
        in_specs=[
            rows(PATCHES, dim),
            fixed((1, dim)),
            fixed((1, dim)),
            fixed((3 * width, dim)),
            pl.BlockSpec((1, 1, 3 * width), lambda i: (i, 0, 0)),
            fixed(strips.shape),
        ],
        out_specs=[rows(PATCHES, width)] * 4
        + [pl.BlockSpec((width, PATCHES), lambda i: (0, i)), rows(PATCHES, heads), rows(PATCHES, dim)],
        out_shape=[piece] * 4
        + [
            jax.ShapeDtypeStruct((width, count), jnp.float32),
            jax.ShapeDtypeStruct((count, heads), jnp.float32),
            jax.ShapeDtypeStruct((count, dim), jnp.float32),
        ],
        scratch_shapes=[pltpu.VMEM((heads, PATCHES, PATCHES), jnp.float32)],
        compiler_params=params(56),
        cost_estimate=cost(6 * count * dim * width * 3 + 24 * count * PATCHES * 256 * heads // 2, 4 * (weight.size + 6 * count * width)),
    )(tokens, gain, shift, weight, time_proj, strips)


def output_kernel(parts, *refs):
    live_ref, tokens_ref, cotangent_ref = refs[:3]
    mixed_refs = refs[3 : 3 + parts]
    weight_refs = refs[3 + parts : 3 + 2 * parts]
    bias_ref, gain_ref, shift_ref, middle_ref, pair_ref, flip_ref, grad_pair_ref, grad_flip_ref = refs[3 + 2 * parts :]
    dim = tokens_ref.shape[1]
    middle = tokens_ref[...] + bias_ref[...]
    for mixed_ref, weight_ref in zip(mixed_refs, weight_refs):
        middle = middle + dot_nn(mixed_ref[...], weight_ref[...])
    middle_ref[...] = middle
    scaled, _ = standardize(middle)
    normed = scaled * gain_ref[...] + shift_ref[...]
    grad = cotangent_ref[...] * live_ref[pl.program_id(0)]
    for value, pair_out, flip_out in ((normed, pair_ref, flip_ref), (grad, grad_pair_ref, grad_flip_ref)):
        pair_out[:, :dim], pair_out[:, dim:] = halves(value)
        flip_out[:dim], flip_out[dim:] = halves(value.T)


def output_forward(live, tokens, cotangent, mixed, weights, bias, gain, shift):
    count, dim = tokens.shape
    parts = len(mixed)
    pair = jax.ShapeDtypeStruct((count, 2 * dim), jnp.bfloat16)
    return pl.pallas_call(
        functools.partial(output_kernel, parts),
        grid=(count // PATCHES,),
        in_specs=[scalars()]
        + [rows(PATCHES, dim)] * 2
        + [rows(PATCHES, m.shape[1]) for m in mixed]
        + [fixed(w.shape) for w in weights]
        + [fixed((1, dim))] * 3,
        out_specs=[rows(PATCHES, dim)]
        + [rows(PATCHES, 2 * dim), pl.BlockSpec((2 * dim, PATCHES), lambda i: (0, i))] * 2,
        out_shape=[jax.ShapeDtypeStruct((count, dim), jnp.float32)]
        + [
            jax.ShapeDtypeStruct((count, 2 * dim), jnp.bfloat16),
            jax.ShapeDtypeStruct((2 * dim, count), jnp.bfloat16),
        ]
        * 2,
        compiler_params=params(48),
        cost_estimate=cost(6 * count * dim * dim, 4 * (dim * dim + 5 * count * dim)),
    )(live, tokens, cotangent, *mixed, *weights, bias, gain, shift)


BLOCK = 256
PIECE = BLOCK // 16


def feed_kernel(
    split, core_ref, pair_ref, flip_ref, grad_pair_ref, grad_flip_ref, hidden_ref, bias_ref, return_ref, *refs
):
    result_ref, second_ref, d_bias_ref = refs[:3]
    outs = refs[3:-7]
    up_ref, down_ref, hidden3_ref, return3_ref, active3_ref, slope3_ref, block_ref = refs[-7:]
    count = pair_ref.shape[0]
    dim = pair_ref.shape[1] // 2
    chunk = min(512, count)

    @pl.when(pl.program_id(0) == 0)
    def _():
        result_ref[...] = jnp.zeros_like(result_ref)
        second_ref[...] = jnp.zeros_like(second_ref)

    d_bias_ref[...] = jnp.zeros_like(d_bias_ref)

    def triple_columns(ref, value, size):
        high, low = halves(value)
        ref[:, :size] = high
        ref[:, size : 2 * size] = high
        ref[:, 2 * size :] = low

    def triple_rows(ref, part, value):
        high, low = halves(value)
        ref[:BLOCK, part] = high
        ref[BLOCK : 2 * BLOCK, part] = low
        ref[2 * BLOCK :, part] = high

    triple_columns(down_ref, return_ref[...], dim)
    triple_columns(up_ref, hidden_ref[...].T, dim)
    triple_columns(hidden3_ref, hidden_ref[...], BLOCK)
    triple_columns(return3_ref, return_ref[...].T, BLOCK)

    def tokens_step(step, carry):
        part = pl.ds(pl.multiple_of(step * chunk, chunk), chunk)
        d_active = mul(down_ref[:, : 2 * dim], grad_flip_ref[:, part], 1, 0) + mul(
            down_ref[:, 2 * dim :], grad_flip_ref[:dim, part], 1, 0
        )
        hidden = (
            mul(up_ref[:, : 2 * dim], flip_ref[:, part], 1, 0)
            + mul(up_ref[:, 2 * dim :], flip_ref[:dim, part], 1, 0)
            + bias_ref[...]
        )
        cumul = 0.5 * (1.0 + lax.erf(hidden * 2.0 ** (-0.5)))
        triple_rows(active3_ref, part, hidden * cumul)
        density = hidden * jnp.exp(-0.5 * hidden * hidden) * (1.0 / math.sqrt(2.0 * math.pi))
        d_hidden = d_active * (cumul + density)
        triple_rows(slope3_ref, part, d_hidden)
        d_bias_ref[...] += jnp.sum(d_hidden, 1, keepdims=True)
        result_ref[:, part] += mul(return3_ref[...], active3_ref[:, part], 1, 0)
        second_ref[:, part] += mul(hidden3_ref[...], slope3_ref[:, part], 1, 0)
        return carry

    lax.fori_loop(0, count // chunk, tokens_step, 0)

    def weight_grad(left_ref, right_ref):
        wide = mul(left_ref[:BLOCK], right_ref[...], 1, 0)
        return wide[:, :dim] + wide[:, dim:] + mul(left_ref[BLOCK : 2 * BLOCK], right_ref[:, :dim], 1, 0)

    if split:
        hidden_keep, hidden_send, return_keep, return_send = outs
        block_ref[...] = weight_grad(active3_ref, grad_pair_ref)

        def place_return(even_ref, odd_ref):
            for pair in range(8):
                even_ref[0, pair] = block_ref[2 * pair * PIECE : (2 * pair + 1) * PIECE]
                odd_ref[0, pair] = block_ref[(2 * pair + 1) * PIECE : (2 * pair + 2) * PIECE]

        pl.when(core_ref[0] == 0)(lambda: place_return(return_keep, return_send))
        pl.when(core_ref[0] == 1)(lambda: place_return(return_send, return_keep))
        value = weight_grad(slope3_ref, pair_ref).T
        piece = dim // 16

        def place_hidden(even_ref, odd_ref):
            for pair in range(8):
                even_ref[pair] = value[2 * pair * piece : (2 * pair + 1) * piece]
                odd_ref[pair] = value[(2 * pair + 1) * piece : (2 * pair + 2) * piece]

        pl.when(core_ref[0] == 0)(lambda: place_hidden(hidden_keep, hidden_send))
        pl.when(core_ref[0] == 1)(lambda: place_hidden(hidden_send, hidden_keep))
    else:
        outs[1][...] = weight_grad(active3_ref, grad_pair_ref)
        outs[0][...] = weight_grad(slope3_ref, pair_ref).T


def feed(split, core, tokens_forms, hidden_weight, hidden_bias, return_weight, first, blocks):
    pair, flip = tokens_forms[:2]
    count = pair.shape[0]
    dim = pair.shape[1] // 2
    units = blocks * BLOCK
    whole = jax.ShapeDtypeStruct((dim, count), jnp.float32)
    if split:
        hidden_out = jax.ShapeDtypeStruct((8, dim // 16, units), jnp.float32)
        return_out = jax.ShapeDtypeStruct((blocks, 8, PIECE, dim), jnp.float32)
        out_specs = [pl.BlockSpec((8, dim // 16, BLOCK), lambda i: (0, 0, i))] * 2 + [
            pl.BlockSpec((1, 8, PIECE, dim), lambda i: (i, 0, 0, 0))
        ] * 2
        out_shape = [hidden_out] * 2 + [return_out] * 2
    else:
        out_specs = [pl.BlockSpec((dim, BLOCK), lambda i: (0, i)), rows(BLOCK, dim)]
        out_shape = [
            jax.ShapeDtypeStruct((dim, units), jnp.float32),
            jax.ShapeDtypeStruct((units, dim), jnp.float32),
        ]
    wide = pltpu.VMEM((BLOCK, 3 * dim), jnp.bfloat16)
    tall = pltpu.VMEM((dim, 3 * BLOCK), jnp.bfloat16)
    return pl.pallas_call(
        functools.partial(feed_kernel, split),
        grid=(blocks,),
        in_specs=[scalars()]
        + [fixed(form.shape) for form in tokens_forms]
        + [
            pl.BlockSpec((dim, BLOCK), lambda i: (0, first + i)),
            pl.BlockSpec((BLOCK, 1), lambda i: (first + i, 0)),
            pl.BlockSpec((BLOCK, dim), lambda i: (first + i, 0)),
        ],
        out_specs=[fixed((dim, count)), fixed((dim, count)), rows(BLOCK, 1)] + out_specs,
        out_shape=[whole, whole, jax.ShapeDtypeStruct((units, 1), jnp.float32)] + out_shape,
        scratch_shapes=[
            wide,
            wide,
            tall,
            tall,
            pltpu.VMEM((3 * BLOCK, count), jnp.bfloat16),
            pltpu.VMEM((3 * BLOCK, count), jnp.bfloat16),
            pltpu.VMEM((BLOCK, dim), jnp.float32),
        ],
        compiler_params=params(62),
        cost_estimate=cost(36 * count * dim * units, 4 * (4 * dim * units + 5 * count * dim), 2 * count * units),
    )(core, *tokens_forms, hidden_weight, hidden_bias, return_weight)


def middle_kernel(parts, feeds, *refs):
    live_ref, middle_ref, cotangent_ref, gain_ref, bias_ref = refs[:5]
    result_parts = refs[5 : 5 + feeds]
    second_parts = refs[5 + feeds : 5 + 2 * feeds]
    weight_refs = refs[5 + 2 * feeds : 5 + 2 * feeds + parts]
    result_ref, d_middle_ref, sums_ref = refs[5 + 2 * feeds + parts : 8 + 2 * feeds + parts]
    mix_refs = refs[8 + 2 * feeds + parts :]
    middle = middle_ref[...]
    grad = cotangent_ref[...] * live_ref[pl.program_id(0)]
    result = result_parts[0][...]
    second = second_parts[0][...]
    for part in result_parts[1:]:
        result = result + part[...]
    for part in second_parts[1:]:
        second = second + part[...]
    result_ref[...] = middle + bias_ref[...] + result.T
    second = second.T
    scaled, inverse = standardize(middle)
    d_middle = grad + norm_back(second * gain_ref[...], scaled, inverse)
    d_middle_ref[...] = d_middle

    @pl.when(pl.program_id(0) == 0)
    def _():
        sums_ref[...] = jnp.zeros_like(sums_ref)

    sums_ref[0:1, :] += jnp.sum(second * scaled, 0, keepdims=True)
    sums_ref[1:2, :] += jnp.sum(second, 0, keepdims=True)
    sums_ref[2:3, :] += jnp.sum(d_middle, 0, keepdims=True)
    sums_ref[3:4, :] += jnp.sum(grad, 0, keepdims=True)
    for weight_ref, mix_ref in zip(weight_refs, mix_refs):
        mix_ref[...] = dot_nt(d_middle, weight_ref[...])


def middle_backward(live, middle, cotangent, gain, bias, results, seconds, weights):
    count, dim = middle.shape
    parts = len(weights)
    block = jax.ShapeDtypeStruct((count, dim), jnp.float32)
    return pl.pallas_call(
        functools.partial(middle_kernel, parts, len(results)),
        grid=(count // PATCHES,),
        in_specs=[scalars()]
        + [rows(PATCHES, dim)] * 2
        + [fixed((1, dim))] * 2
        + [pl.BlockSpec((dim, PATCHES), lambda i: (0, i))] * (2 * len(results))
        + [fixed(w.shape) for w in weights],
        out_specs=[rows(PATCHES, dim)] * 2 + [fixed((8, dim))] + [rows(PATCHES, w.shape[0]) for w in weights],
        out_shape=[block, block, jax.ShapeDtypeStruct((8, dim), jnp.float32)]
        + [jax.ShapeDtypeStruct((count, w.shape[0]), jnp.float32) for w in weights],
        compiler_params=params(60),
        cost_estimate=cost(6 * count * dim * dim, 4 * (dim * dim + 9 * count * dim)),
    )(live, middle, cotangent, gain, bias, *results, *seconds, *weights)


def attend_backward_kernel(
    heads, query_ref, keys_ref, values_ref, mixed_ref, grad_ref, lse_ref, strip_ref,
    d_proj_ref, flipped_ref, d_strip_ref, d_time_ref, bias_ref, total_ref, d_query_ref, d_keys_ref, d_values_ref,
):
    width = query_ref.shape[1]
    image = pl.program_id(0)

    @pl.when(image == 0)
    def _():
        build_bias(strip_ref, bias_ref, heads)
        total_ref[...] = jnp.zeros_like(total_ref)

    d_query_ref[...] = jnp.zeros_like(d_query_ref)
    d_keys_ref[...] = jnp.zeros_like(d_keys_ref)
    d_values_ref[...] = jnp.zeros_like(d_values_ref)
    for head in range(heads):
        start, stop, _ = head_window(head, width)
        mask = head_mask(head, width)
        query = jnp.where(mask, query_ref[:, start:stop], 0.0)
        keys = jnp.where(mask, keys_ref[:, start:stop], 0.0)
        grad = jnp.where(mask, grad_ref[:, start:stop], 0.0)
        scores = dot_nt(query, keys) + bias_ref[head]
        prob = jnp.exp(scores - lse_ref[:, head : head + 1])
        d_prob = dot_nt(grad, values_ref[:, start:stop])
        delta = jnp.sum(grad * mixed_ref[:, start:stop], -1, keepdims=True)
        d_scores = prob * (d_prob - delta)
        total_ref[head] += d_scores
        d_values_ref[:, start:stop] += dot_tn(prob, grad)
        d_query_ref[:, start:stop] += dot_nn(d_scores, keys)
        d_keys_ref[:, start:stop] += dot_tn(d_scores, query)
    d_proj_ref[:, :width] = d_query_ref[...] * SCALE
    d_proj_ref[:, width : 2 * width] = d_keys_ref[...]
    d_proj_ref[:, 2 * width :] = d_values_ref[...]
    d_time_ref[0] = jnp.sum(d_proj_ref[...], 0, keepdims=True)
    flipped_ref[:width] = (d_query_ref[...] * SCALE).T
    flipped_ref[width : 2 * width] = d_keys_ref[...].T
    flipped_ref[2 * width :] = d_values_ref[...].T

    @pl.when(image == pl.num_programs(0) - 1)
    def _():
        d_strip_ref[...] = jnp.zeros_like(d_strip_ref)

        def one(head, carry):
            for row in range(SIDE):
                shift = (SIDE - 1 - row) * SIDE
                d_strip_ref[head, :, shift : shift + PATCHES] += total_ref[head, row * SIDE : (row + 1) * SIDE, :]
            return carry

        lax.fori_loop(0, heads, one, 0)


def attend_backward(query, keys, values, mixed, grad, lse, strips):
    count, width = query.shape
    heads = strips.shape[0]
    images = count // PATCHES
    return pl.pallas_call(
        functools.partial(attend_backward_kernel, heads),
        grid=(images,),
        in_specs=[rows(PATCHES, width)] * 5 + [rows(PATCHES, heads), fixed(strips.shape)],
        out_specs=[
            rows(PATCHES, 3 * width),
            pl.BlockSpec((3 * width, PATCHES), lambda i: (0, i)),
            fixed(strips.shape),
            pl.BlockSpec((1, 1, 3 * width), lambda i: (i, 0, 0)),
        ],
        out_shape=[
            jax.ShapeDtypeStruct((count, 3 * width), jnp.float32),
            jax.ShapeDtypeStruct((3 * width, count), jnp.float32),
            jax.ShapeDtypeStruct(strips.shape, jnp.float32),
            jax.ShapeDtypeStruct((images, 1, 3 * width), jnp.float32),
        ],
        scratch_shapes=[pltpu.VMEM((heads, PATCHES, PATCHES), jnp.float32)] * 2
        + [pltpu.VMEM((PATCHES, width), jnp.float32)] * 3,
        compiler_params=params(56),
        cost_estimate=cost(30 * count * PATCHES * 256 * heads, 4 * 9 * count * width),
    )(query, keys, values, mixed, grad, lse, strips)


STEP = 576


def attend_weights_kernel(split, steps, core_ref, *refs):
    lefts, rights = refs[: len(steps)], refs[len(steps) : 2 * len(steps)]
    outs = refs[2 * len(steps) :]
    step = pl.program_id(0)
    piece = STEP // 8
    begin = 0
    for left_ref, right_ref, count in zip(lefts, rights, steps):

        @pl.when((step >= begin) & (step < begin + count))
        def _(left_ref=left_ref, right_ref=right_ref):
            value = dot_nn(left_ref[...], right_ref[...])
            if split:

                def store(even_ref, odd_ref):
                    for pair in range(4):
                        even_ref[pair] = value[2 * pair * piece : (2 * pair + 1) * piece]
                        odd_ref[pair] = value[(2 * pair + 1) * piece : (2 * pair + 2) * piece]

                pl.when(core_ref[0] == 0)(lambda: store(outs[0], outs[1]))
                pl.when(core_ref[0] == 1)(lambda: store(outs[1], outs[0]))
            else:
                outs[0][...] = value

        begin += count


def attend_weights(split, core, lefts, rights, firsts, steps):
    count, dim = rights[0].shape
    total = sum(steps)
    starts = [sum(steps[:i]) for i in range(len(steps))]

    def left_spec(start, first, size):
        return pl.BlockSpec((STEP, count), lambda i: (first + jnp.clip(i - start, 0, size - 1), 0))

    if split:
        out_specs = [pl.BlockSpec((4, STEP // 8, dim), lambda i: (i, 0, 0))] * 2
        out_shape = [jax.ShapeDtypeStruct((4 * total, STEP // 8, dim), jnp.float32)] * 2
    else:
        out_specs = [rows(STEP, dim)]
        out_shape = [jax.ShapeDtypeStruct((STEP * total, dim), jnp.float32)]
    return pl.pallas_call(
        functools.partial(attend_weights_kernel, split, steps),
        grid=(total,),
        in_specs=[scalars()]
        + [left_spec(a, b, c) for a, b, c in zip(starts, firsts, steps)]
        + [fixed((count, dim)) for _ in rights],
        out_specs=out_specs,
        out_shape=out_shape,
        compiler_params=params(60),
        cost_estimate=cost(6 * count * dim * STEP * total, 4 * (dim * STEP * total + count * 3 * dim)),
    )(core, *lefts, *rights)


def first_kernel(parts, *refs):
    tokens_ref, d_middle_ref, gain_ref = refs[:3]
    d_proj_refs = refs[3 : 3 + parts]
    weight_refs = refs[3 + parts : 3 + 2 * parts]
    out_ref, sums_ref = refs[3 + 2 * parts :]
    first = dot_nn(d_proj_refs[0][...], weight_refs[0][...])
    for d_proj_ref, weight_ref in zip(d_proj_refs[1:], weight_refs[1:]):
        first = first + dot_nn(d_proj_ref[...], weight_ref[...])
    scaled, inverse = standardize(tokens_ref[...])
    out_ref[...] = d_middle_ref[...] + norm_back(first * gain_ref[...], scaled, inverse)

    @pl.when(pl.program_id(0) == 0)
    def _():
        sums_ref[...] = jnp.zeros_like(sums_ref)

    sums_ref[0:1, :] += jnp.sum(first * scaled, 0, keepdims=True)
    sums_ref[1:2, :] += jnp.sum(first, 0, keepdims=True)


def first_backward(tokens, d_middle, gain, d_projs, weights, begin, images):
    dim = tokens.shape[1]
    count = images * PATCHES

    def some(width):
        return pl.BlockSpec((PATCHES, width), lambda i: (begin + i, 0))

    parts = len(d_projs)
    return pl.pallas_call(
        functools.partial(first_kernel, parts),
        grid=(count // PATCHES,),
        in_specs=[some(dim)] * 2
        + [fixed((1, dim))]
        + [some(d.shape[1]) for d in d_projs]
        + [fixed(w.shape) for w in weights],
        out_specs=[rows(PATCHES, dim), fixed((8, dim))],
        out_shape=[jax.ShapeDtypeStruct((count, dim), jnp.float32), jax.ShapeDtypeStruct((8, dim), jnp.float32)],
        compiler_params=params(60),
        cost_estimate=cost(18 * count * dim * dim, 4 * (3 * dim * dim + 6 * count * dim)),
    )(tokens, d_middle, gain, *d_projs, *weights)


def offset_matrix():
    place = jnp.arange(PATCHES)
    offset = place // SIDE - place % SIDE + SIDE - 1
    return (jnp.arange(STRIP)[:, None] == offset[None, :]).astype(jnp.float32)


def make_strips(table):
    heads = table.shape[0]
    grid = table.reshape(heads, STRIP, STRIP)[:, ::-1]
    wide = jnp.einsum("hmo,op->hmp", grid, offset_matrix(), precision=HIGHEST)
    wide = wide.reshape(heads, STRIP, SIDE, SIDE).transpose(0, 2, 1, 3).reshape(heads, SIDE, STRIP * SIDE)
    return jnp.pad(wide, ((0, 0), (0, 0), (0, 512 - STRIP * SIDE)))


def table_gradient(d_strips):
    heads = d_strips.shape[0]
    wide = d_strips[:, :, : STRIP * SIDE].reshape(heads, SIDE, STRIP, SIDE).transpose(0, 2, 1, 3)
    grid = jnp.einsum("hmp,op->hmo", wide.reshape(heads, STRIP, PATCHES), offset_matrix(), precision=HIGHEST)
    return grid[:, ::-1].reshape(heads, STRIP * STRIP)


def pick(array, index, axis):
    return lax.dynamic_index_in_dim(array, index, axis, keepdims=False)


def join(*values):
    return lax.optimization_barrier(values)


class Ring:
    def __init__(self):
        place = lax.axis_index("dp")
        self.place = place
        self.bits = [place & 1, (place >> 1) & 1, (place >> 2) & 1, (place >> 3) & 1]

    def across(self, value):
        return lax.ppermute(value, "mp", [(0, 1), (1, 0)])

    def along(self, value, bit):
        return lax.ppermute(value, "dp", [(i, i ^ (1 << bit)) for i in range(16)])

    def ordered(self, mine, theirs, bit, axis=0):
        flag = self.bits[bit] == 0
        return jnp.concatenate([jnp.where(flag, mine, theirs), jnp.where(flag, theirs, mine)], axis)

    def core_half(self, weight, base, count):
        half = count // 2
        return lax.dynamic_slice(weight, (base + self.bits[0] * half, 0), (half, weight.shape[1]))

    def share(self, weight, count, first, width):
        part = count // 16
        return lax.dynamic_slice(weight, (self.place * part, first), (part, width))

    def spread(self, part):
        return lax.all_gather(part, "dp", axis=0, tiled=True)

    def all_sum(self, value):
        value = value + self.along(value, 0)
        value = value + self.across(value)
        for bit in (1, 2, 3):
            value = value + self.along(value, bit)
        return value

    def all_rows(self, value):
        for bit in range(4):
            value = self.ordered(value, self.along(value, bit), bit)
        return value


class Reduction:
    def __init__(self, ring, axis):
        self.ring = ring
        self.axis = axis
        self.terms = {}
        self.level = {}

    def begin(self, side, keep, send):
        self.terms[side] = [keep, self.ring.along(send, 0)]
        self.level[side] = 1

    def value(self, side):
        out = self.terms[side][0]
        for term in self.terms[side][1:]:
            out = out + term
        return out

    def send(self, side):
        bit = self.ring.bits[self.level[side]]
        kept = []
        out = 0.0
        for term in self.terms[side]:
            shape = term.shape
            axis = self.axis
            cut = term.reshape(shape[:axis] + (shape[axis] // 2, 2) + shape[axis + 1 :])
            kept.append(pick(cut, bit, axis + 1))
            out = out + pick(cut, 1 - bit, axis + 1)
        self.terms[side] = kept
        return out

    def pass_on(self, side, value):
        self.terms[side].append(self.ring.along(value, self.level[side]))
        self.level[side] += 1

    def cross(self, value):
        self.terms["own"].append(self.ring.across(value))

    def gather(self, value):
        return lax.all_gather(value, "dp", axis=self.axis, tiled=True)

    def back(self, value, bit):
        axis = self.axis
        got = self.ring.along(value, bit)
        value, got = (v.reshape(v.shape[: axis + 1] + (1,) + v.shape[axis + 1 :]) for v in (value, got))
        out = self.ring.ordered(value, got, bit, axis + 1)
        return out.reshape(out.shape[:axis] + (-1,) + out.shape[axis + 2 :])


def body(split, *args):
    (
        tokens, cotangent, bucket, counts, first_gain, first_shift, attend_weight, time_weight, time_table,
        bias_table, output_weight, output_bias, second_gain, second_shift, hidden_weight, hidden_bias,
        return_weight, return_bias,
    ) = args
    own_images, patches, dim = tokens.shape
    images = bucket.shape[0]
    buckets = time_table.shape[0]
    heads_local = bias_table.shape[0]
    width = attend_weight.shape[2]
    units = hidden_bias.shape[0]
    group = lax.axis_index("dp")
    rank = lax.axis_index("mp")
    first_own = rank * own_images
    live = (first_own + jnp.arange(own_images) < counts[group]).astype(jnp.float32)
    inv_total = 1.0 / jnp.sum(counts).astype(jnp.float32)
    core = (group & 1).reshape(1)

    def row(vector):
        return vector.reshape(1, -1)

    def column(vector):
        return vector.reshape(-1, 1)

    tokens2 = tokens.reshape(own_images * patches, dim)
    cotangent2 = cotangent.reshape(own_images * patches, dim)
    onehot = (bucket[:, None] == jnp.arange(buckets)[None, :]).astype(jnp.float32)
    time_vec = jnp.dot(onehot, time_table, precision=HIGHEST)
    time_proj = jnp.einsum("sd,ced->sce", time_vec, time_weight.transpose(0, 2, 1), precision=HIGH)
    attend_own = attend_weight.transpose(0, 2, 1).reshape(3 * width, dim)
    norm_first = (row(first_gain), row(first_shift))
    norm_second = (row(second_gain), row(second_shift))

    def times_of(value):
        return value.reshape(own_images, 1, -1)

    if split:
        ring = Ring()
        more = (units // BLOCK + 1) // 2
        cuts = [(0, more), (more, units // BLOCK - more)]
        qk = ring.across(ring.share(attend_own, 2 * width, 0, dim))
        qk_full = ring.spread(qk)
        values_half = ring.core_half(attend_own, 2 * width, width)
        values_half, qk = join(values_half, qk)
        values_mine = ring.across(values_half)
        time_mine = lax.dynamic_slice_in_dim(time_proj, first_own, own_images, 0)
        time_theirs = lax.dynamic_slice_in_dim(time_proj, (1 - rank) * own_images, own_images, 0)
        strips_own = make_strips(bias_table)
        tokens_a, qk, time_theirs = join(tokens2, qk, time_theirs)
        own = attend_forward(tokens_a, *norm_first, attend_own, times_of(time_mine), strips_own)
        own, values_mine, time_theirs, bias_table_b = join(own, values_mine, time_theirs, bias_table)
        time_other = ring.across(time_theirs)
        table_other = ring.across(bias_table_b)
        bias_other = column(ring.across(hidden_bias))
        output_mine = ring.across(ring.core_half(output_weight, 0, width))
        values_theirs = ring.along(values_mine, 0)
        hidden_other = []
        for first, blocks in cuts:
            part = ring.share(hidden_weight, dim, first * BLOCK, blocks * BLOCK)
            part, values_mine = join(part, values_mine)
            hidden_other.append(ring.spread(ring.across(part)))
        attend_other = jnp.concatenate([qk_full, ring.ordered(values_mine, values_theirs, 0)], 0)
        attend_other, output_mine = join(attend_other, output_mine)
        first_half = ring.core_half(return_weight, 0, cuts[0][1] * BLOCK)
        first_half, output_mine = join(first_half, output_mine)
        return_mine = ring.across(first_half)
        output_other = ring.ordered(output_mine, ring.along(output_mine, 0), 0)
        other = attend_forward(
            tokens2, *norm_first, attend_other, times_of(time_other), make_strips(table_other)
        )
        strips_other = make_strips(table_other)
        attend = [attend_own, attend_other]
        output = [output_weight, output_other]
        middle, *forms = output_forward(
            live, tokens2, cotangent2, [own[3], other[3]], output, row(output_bias), *norm_second
        )
        second_half = ring.core_half(return_weight, cuts[1][0] * BLOCK, cuts[1][1] * BLOCK)
        return_1, second_half = join(ring.ordered(return_mine, ring.along(return_mine, 0), 0), second_half)
        return_mine = ring.across(second_half)

        def feed_other(forms, index, hidden, back):
            first, blocks = cuts[index]
            bias = bias_other[first * BLOCK : (first + blocks) * BLOCK]
            return feed(True, core, forms, hidden, bias, back, 0, blocks)

        def feed_own(forms, index):
            return feed(True, core, forms, hidden_weight, column(hidden_bias), return_weight, *cuts[index])

        h1, h2, r1, r2, qa, qb = (Reduction(ring, axis) for axis in (0, 0, 1, 1, 0, 0))
        other_1 = feed_other(forms, 0, hidden_other[0], return_1)
        forms, other_1, return_mine = join(forms, other_1, return_mine)
        h1.begin("other", *other_1[3:5])
        r1.begin("other", *other_1[5:7])
        return_2 = ring.ordered(return_mine, ring.along(return_mine, 0), 0)
        other_2 = feed_other(forms, 1, hidden_other[1], return_2)
        forms, other_2, a, b = join(forms, other_2, h1.value("other"), r1.send("other"))
        h1_cross, r1_y = a, b
        h2.begin("other", *other_2[3:5])
        r2.begin("other", *other_2[5:7])
        h1_crossed = ring.across(h1_cross)
        r1.pass_on("other", r1_y)
        own_1 = feed_own(forms, 0)
        forms, own_1, a, b, h1_crossed, r1.terms["other"] = join(
            forms, own_1, h2.value("other"), r2.send("other"), h1_crossed, r1.terms["other"]
        )
        h1.begin("own", *own_1[3:5])
        r1.begin("own", *own_1[5:7])
        h1.terms["own"].append(h1_crossed)
        h2_crossed = ring.across(a)
        r2.pass_on("other", b)
        own_2 = feed_own(forms, 1)
        middle, own_2, a, b, h2_crossed = join(middle, own_2, r1.send("own"), r1.value("other"), h2_crossed)
        h2.begin("own", *own_2[3:5])
        r2.begin("own", *own_2[5:7])
        h2.terms["own"].append(h2_crossed)
        r1.pass_on("own", a)
        r1.cross(b)
        fed = [other_1, own_1, other_2, own_2]
        result, d_middle, second_sums, d_mixed_own, d_mixed_other = middle_backward(
            live, middle, cotangent2, row(second_gain), row(return_bias), [f[0] for f in fed], [f[1] for f in fed], output
        )
        d_mixed_other, a, b, c = join(d_mixed_other, h1.send("own"), r2.value("other"), r1.send("own"))
        h1.pass_on("own", a)
        r2_crossed = ring.across(b)
        r1.pass_on("own", c)
        attended_other = attend_backward(*other[:4], d_mixed_other, other[5], strips_other)
        attended_other, a, b, c, r2_crossed = join(
            attended_other, h1.send("own"), r1.send("own"), h2.send("own"), r2_crossed
        )
        h1.pass_on("own", a)
        r1.pass_on("own", b)
        h2.pass_on("own", c)

        def weights_a(attended, normed):
            return attend_weights(True, core, [attended[1]], [normed], [0], [2])

        def weights_b(attended, normed, flipped_mixed):
            return attend_weights(True, core, [attended[1], flipped_mixed], [normed, d_middle], [2, 0], [1, 1])

        normed_first = own[6]
        part = weights_a(attended_other, normed_first)
        part, normed_first = join(part, normed_first)
        qa.begin("other", *part)
        part = weights_b(attended_other, normed_first, other[4])
        part, d_mixed_own, a, b, c, d, e = join(
            part, d_mixed_own, qa.value("other"), h1.send("own"), r2.send("own"), h2.send("own"), r1.value("own")
        )
        qb.begin("other", *part)
        qa_first = ring.across(a[:4])
        h1.pass_on("own", b)
        r2.pass_on("own", c)
        r2.terms["own"].append(r2_crossed)
        h2.pass_on("own", d)
        return_1 = r1.gather(e)
        attended_own = attend_backward(*own[:4], d_mixed_own, own[5], strips_own)
        attended_own, a, b, c, d, e, qa_first = join(
            attended_own, qb.send("other"), h1.value("own"), r2.send("own"), h2.send("own"), a[4:], qa_first
        )
        qb.pass_on("other", a)
        hidden_1 = h1.gather(b)
        r2.pass_on("own", c)
        h2.pass_on("own", d)
        qa_second = ring.across(e)
        part = weights_b(attended_own, normed_first, own[4])
        part, normed_first = join(part, normed_first)
        qb.begin("own", *part)
        part = weights_a(attended_own, normed_first)
        part, d_projs, a, b, c, d, qa_second = join(
            part, [attended_own[0], attended_other[0]], qb.send("own"), qb.value("other"), r2.send("own"),
            h2.value("own"), qa_second,
        )
        qa.begin("own", *part)
        qa.terms["own"].append(jnp.concatenate([qa_first, qa_second], 0))
        qb.pass_on("own", a)
        qb.cross(b)
        r2.pass_on("own", c)
        hidden_2 = h2.back(d, 3)
        half = own_images // 2
        tokens_a, sums_a = first_backward(tokens2, d_middle, row(first_gain), d_projs, attend, 0, half)
        tokens_a, d_projs, a, b, c, hidden_2 = join(
            tokens_a, d_projs, qa.send("own"), qb.send("own"), r2.value("own"), hidden_2
        )
        qa.pass_on("own", a)
        qb.pass_on("own", b)
        return_2 = r2.back(c, 3)
        hidden_2 = h2.back(hidden_2, 2)
        tokens_b, sums_b = first_backward(
            tokens2, d_middle, row(first_gain), d_projs, attend, half, own_images - half
        )
        tokens_b, a, b, hidden_2, return_2 = join(tokens_b, qa.send("own"), qb.send("own"), hidden_2, return_2)
        qa.pass_on("own", a)
        qb.pass_on("own", b)
        hidden_2 = h2.back(hidden_2, 1)
        return_2 = r2.back(return_2, 2)
        a, b, hidden_2, return_2 = join(qa.send("own"), qb.value("own"), hidden_2, return_2)
        qa.pass_on("own", a)
        attend_b = qb.gather(b)
        hidden_2 = h2.back(hidden_2, 0)
        return_2 = r2.back(return_2, 1)
        a, hidden_2, return_2 = join(qa.value("own"), hidden_2, return_2)
        attend_a = qa.back(a, 3)
        return_2 = r2.back(return_2, 0)
        hidden_grad = jnp.concatenate([g.reshape(dim, -1) for g in (hidden_1, hidden_2)], 1) * inv_total
        attend_a, hidden_grad, return_2 = join(attend_a, hidden_grad, return_2)
        attend_a = qa.back(attend_a, 2)
        return_grad = jnp.concatenate([g.reshape(-1, dim) for g in (return_1, return_2)], 0) * inv_total
        attend_a, return_grad = join(attend_a, return_grad)
        attend_a = qa.back(qa.back(attend_a, 1), 0)
        tokens_grad = jnp.concatenate([tokens_a, tokens_b], 0)
        first_sums = sums_a + sums_b
        attend_a = attend_a.reshape(2, width, dim)
        attend_b = attend_b.reshape(2, width, dim)
        attend_weight_grad = (jnp.concatenate([attend_a, attend_b[:1]], 0) * inv_total).transpose(0, 2, 1)
        output_weight_grad = attend_b[1] * inv_total

        def absolute(own, other):
            flag = rank == 0
            return jnp.concatenate([jnp.where(flag, own, other), jnp.where(flag, other, own)], 0)

        table_full = absolute(table_gradient(attended_own[2]), table_gradient(attended_other[2]))
        bias_own = jnp.concatenate([own_1[2][:, 0], own_2[2][:, 0]])
        hidden_bias_full = absolute(bias_own, jnp.concatenate([other_1[2][:, 0], other_2[2][:, 0]]))
        d_time_got = ring.across(attended_other[3].reshape(own_images, 3, width))
        d_time = absolute(attended_own[3].reshape(own_images, 3, width), d_time_got)
        gather_rows = ring.all_rows
        all_sum = ring.all_sum
    else:
        attend = [lax.all_gather(attend_weight, "mp", axis=2, tiled=True).transpose(0, 2, 1).reshape(-1, dim)]
        output = [lax.all_gather(output_weight, "mp", axis=0, tiled=True)]
        hidden_full = lax.all_gather(hidden_weight, "mp", axis=1, tiled=True)
        return_full = lax.all_gather(return_weight, "mp", axis=0, tiled=True)
        bias_full = lax.all_gather(hidden_bias, "mp", axis=0, tiled=True)
        strips = make_strips(lax.all_gather(bias_table, "mp", axis=0, tiled=True))
        full = lax.all_gather(time_proj, "mp", axis=2, tiled=True)
        times = times_of(lax.dynamic_slice_in_dim(full, first_own, own_images, 0))
        all_of = attend_forward(tokens2, *norm_first, attend[0], times, strips)
        middle, *forms = output_forward(
            live, tokens2, cotangent2, [all_of[3]], output, row(output_bias), *norm_second
        )
        fed = feed(False, core, forms, hidden_full, column(bias_full), return_full, 0, hidden_full.shape[1] // BLOCK)
        result, d_middle, second_sums, d_mixed = middle_backward(
            live, middle, cotangent2, row(second_gain), row(return_bias), [fed[0]], [fed[1]], output
        )
        attended = attend_backward(*all_of[:4], d_mixed, all_of[5], strips)
        (attend_full,) = attend_weights(
            False, core, [attended[1]], [all_of[6]], [0], [attended[1].shape[0] // STEP]
        )
        (output_full,) = attend_weights(False, core, [all_of[4]], [d_middle], [0], [dim // STEP])
        tokens_grad, first_sums = first_backward(
            tokens2, d_middle, row(first_gain), [attended[0]], attend, 0, own_images
        )

        def settle(value, axis):
            return lax.psum(lax.psum_scatter(value * inv_total, "mp", scatter_dimension=axis, tiled=True), "dp")

        hidden_grad = settle(fed[3], 1)
        return_grad = settle(fed[4], 0)
        attend_weight_grad = settle(attend_full.reshape(3, -1, dim), 1).transpose(0, 2, 1)
        output_weight_grad = settle(output_full, 0)
        table_full = table_gradient(attended[2])
        hidden_bias_full = fed[2][:, 0]
        d_time = lax.all_gather(attended[3].reshape(own_images, 3, -1), "mp", axis=0, tiled=True)
        d_time = lax.dynamic_slice_in_dim(d_time, rank * width, width, 2)

        def gather_rows(value):
            return lax.all_gather(value, "dp", axis=0, tiled=True)

        def all_sum(value):
            return lax.psum(value, ("dp", "mp"))

    packed = jnp.concatenate([d_time.reshape(images, -1), bucket.astype(jnp.float32)[:, None]], 1)
    packed = gather_rows(packed)
    d_time_all = packed[:, :-1].reshape(-1, 3, width)
    bucket_all = packed[:, -1].astype(jnp.int32)
    onehot_all = (bucket_all[:, None] == jnp.arange(buckets)[None, :]).astype(jnp.float32)
    time_all = jnp.dot(onehot_all, time_table, precision=HIGHEST)
    time_weight_grad = jnp.einsum("sce,sd->ced", d_time_all * inv_total, time_all, precision=HIGH).transpose(0, 2, 1)
    d_time_vec = jnp.einsum("sce,ced->sd", d_time, time_weight.transpose(0, 2, 1), precision=HIGH)
    time_table_part = jnp.dot(onehot.T, d_time_vec, precision=HIGHEST)

    small = [
        first_sums[0], first_sums[1], time_table_part, second_sums[2], second_sums[0], second_sums[1],
        second_sums[3], table_full, hidden_bias_full,
    ]
    flat = jnp.concatenate([s.reshape(-1) for s in small]) * inv_total
    size = flat.shape[0]
    flat = all_sum(jnp.pad(flat, (0, -size % 1024)).reshape(-1, 128)).reshape(-1)[:size]
    sums = []
    start = 0
    for s in small:
        sums.append(flat[start : start + s.size].reshape(s.shape))
        start += s.size
    bias_table_grad = lax.dynamic_slice_in_dim(sums[7], rank * heads_local, heads_local, 0)
    hidden_bias_grad = lax.dynamic_slice_in_dim(sums[8], rank * units, units, 0)
    return (
        result.reshape(tokens.shape),
        tokens_grad.reshape(tokens.shape),
        sums[0],
        sums[1],
        attend_weight_grad,
        time_weight_grad,
        sums[2],
        bias_table_grad,
        output_weight_grad,
        sums[3],
        sums[4],
        sums[5],
        hidden_grad,
        hidden_bias_grad,
        return_grad,
        sums[6],
    )


def solution(mesh):
    in_specs = (
        P(("dp", "mp"), None, None),
        P(("dp", "mp"), None, None),
        P("dp"),
        P(),
        P(),
        P(),
        P(None, None, "mp"),
        P(None, None, "mp"),
        P(),
        P("mp", None),
        P("mp", None),
        P(),
        P(),
        P(),
        P(None, "mp"),
        P("mp"),
        P("mp", None),
        P(),
    )
    out_specs = (
        P(("dp", "mp"), None, None),
        P(("dp", "mp"), None, None),
        P(),
        P(),
        P(None, None, "mp"),
        P(None, None, "mp"),
        P(),
        P("mp", None),
        P("mp", None),
        P(),
        P(),
        P(),
        P(None, "mp"),
        P("mp"),
        P("mp", None),
        P(),
    )
    split = mesh.shape["dp"] == 16 and mesh.shape["mp"] == 2
    return jax.shard_map(
        functools.partial(body, split), mesh=mesh, in_specs=in_specs, out_specs=out_specs, check_vma=False
    )
```

time: 2530 us -> 1320 us (0.52)
  matrix products: 953 us -> 19.4 us
  Pallas kernels: 0 us -> 603 us
  waiting for transfers between devices: 719 us -> 344 us
  other arithmetic: 423 us -> 165 us
  local copies, waits for them, and re-layouts: 300 us -> 107 us
  blocking collectives: 116 us -> 0 us
  starting transfers between devices: 0.41 us -> 63.4 us
    dot_general x23 -> x10, matrix products: 953 us -> 19.4 us  [the longest x1 6.61 us: body(): jnp.einsum('sd,ced->sce', time_vec, time_weight.transpose(0, 2, 1), preci...]
    pallas_call x0 -> x16, Pallas kernels: none -> 603 us  [the longest x4 311 us: feed(): pl.pallas_call(functools.partial(feed_kernel, split), grid=(blocks,), in_...]
    scatter-add x1 -> x0, other arithmetic: 347 us -> none  [body(): bias, bias_pull = jax.vjp(lambda table: table[:, offsets], bias_table)]
    ppermute x0 -> x76, waiting for transfers between devices: none -> 343 us  [the longest x19 184 us: across(): return lax.ppermute(value, 'mp', [(0, 1), (1, 0)])]
    all_gather x4 -> x6, waiting for transfers between devices: 257 us -> 0.06 us  [the longest x3 0.04 us: gather(): return lax.all_gather(value, 'dp', axis=self.axis, tiled=True)]
    reduce_scatter x4 -> x0, waiting for transfers between devices: 245 us -> none  [the longest x1 113 us: body(): lax.psum_scatter(attend_terms, 'mp', scatter_dimension=0, tiled=True)]
    gather x2 -> x0, local copies, waits for them, and re-layouts: 235 us -> none  [body(): bias, bias_pull = jax.vjp(lambda table: table[:, offsets], bias_table)]
    psum x2 -> x0, waiting for transfers between devices: 216 us -> none  [the longest x1 216 us: body(): lax.psum((attend_weight_grad * inv_total, time_weight_grad * inv_total, b...]
  transfers between devices with their start and end apart: 10 -> 82, of which waited for: 7 -> 22; matrix products, arithmetic and copies ran while one was open for 43% -> 20% of each run, Pallas kernels for 0% -> 46%
where the time goes in v1:
time: 1320 us
  Pallas kernels  603 us (46%)
  waiting for transfers between devices  344 us (26%)
  other arithmetic  165 us (12%)
  local copies, waits for them, and re-layouts  107 us (8%)
  starting transfers between devices  63.4 us (5%)
  matrix products  19.4 us (1%)
  between operations  16.7 us (1%)
    pallas_call x4, Pallas kernels, feed(): pl.pallas_call(functools.partial(feed_kernel, split), grid=(blocks,), in_...  311 us
    ppermute x19, waiting for transfers between devices, across(): return lax.ppermute(value, 'mp', [(0, 1), (1, 0)])  184 us
    ppermute x57, waiting for transfers between devices, along(): return lax.ppermute(value, 'dp', [(i, i ^ 1 << bit) for i in range(16)])  159 us
    pallas_call x2, Pallas kernels, attend_forward(): pl.pallas_call(functools.partial(attend_forward_kernel, heads), grid=(ima...  66.6 us
    pallas_call x4, Pallas kernels, attend_weights(): pl.pallas_call(functools.partial(attend_weights_kernel, split, steps), gr...  63 us
    pallas_call x2, Pallas kernels, attend_backward(): pl.pallas_call(functools.partial(attend_backward_kernel, heads), grid=(im...  61.7 us
    pallas_call x2, Pallas kernels, first_backward(): pl.pallas_call(functools.partial(first_kernel, parts), grid=(count // PAT...  50.3 us
    ppermute x57, starting transfers between devices, along(): return lax.ppermute(value, 'dp', [(i, i ^ 1 << bit) for i in range(16)])  44.3 us
  transfers between devices with their start and end apart: 82, of which 22 were waited for; matrix products, arithmetic and copies ran while one was open for 20% of the time, Pallas kernels for 46%

profile of v1, /device:TPU:0, one launch (start us, length us, event | category | flops | bytes accessed | tf_op | source)
XLA Modules:
  0.0 1317.5 jit_solution(10058060857045722707)
XLA Ops:
  11.3 7.8 collective-permute-done
  24.4 6.6 fusion.3
  37.5 33.3 %shard_map.297 = (f32[1024,576]{1,0:T(8,128)}, f32[1024,576]{1,0:T(8,128)}, f32[1024,576]{1,0:T(8,128)}, f32[1024,576]{1,0:T(8,128)}, f32[576,1024]{1,0:T(8,128)...) custom-call(f32[1024,1152]{1,0:T(8,128)} %bitcast.415, f32[1,1152]{1,0:T(1,128)} %reshape.1353.gain_ref.refs_2_, ...), custom_call_target="tpu_custom_call" | custom-call | flops 18673040 | bytes 22118 | tf_op jit(solution)/shard_map/pallas_call | solution.py:142
  72.2 8.9 collective-permute-done.7
  91.2 6.3 pad_maximum_fusion.weight_ref.refs_6_
  97.5 17.5 %collective-permute-done.3 = f32[288,1152]{1,0:T(8,128)} collective-permute-done((f32[288,1152]{1,0:T(8,128)}, f32[288,1152]{1,0:T(8,128)}, u32[]{:S(2)}, u32[]{:S(2)}) %collective-permute-start.3) | collective-permute-done | bytes 1327136 | tf_op jit(solution)/shard_map/ppermute | solution.py:611
  115.7 65.1 %collective-permute-done.9 = f32[640,1152]{1,0:T(8,128)S(1)} collective-permute-done((f32[640,1152]{1,0:T(8,128)}, f32[640,1152]{1,0:T(8,128)S(1)}, u32[]{:S(2)}, u32[]{:S(2)}) %collective-permute-start.9) | collective-permute-done | bytes 2949152 | tf_op jit(solution)/shard_map/ppermute | solution.py:611
  181.4 9.0 collective-permute-done.12
  205.0 49.1 %collective-permute-done.8 = f32[2304]{0:T(1024)S(1)} collective-permute-done((f32[2304]{0:T(1024)S(1)}, f32[2304]{0:T(1024)S(1)}, u32[]{:S(2)}, u32[]{:S(2)}) %collective-permute-start.8) | collective-permute-done | bytes 9248 | tf_op jit(solution)/shard_map/ppermute | solution.py:611
  260.0 33.3 %shard_map.298 = (f32[1024,576]{1,0:T(8,128)}, f32[1024,576]{1,0:T(8,128)}, f32[1024,576]{1,0:T(8,128)}, f32[1024,576]{1,0:T(8,128)}, f32[576,1024]{1,0:T(8,128)...) custom-call(f32[1024,1152]{1,0:T(8,128)} %bitcast.416, f32[1,1152]{1,0:T(1,128)} %reshape.1353.gain_ref.refs_2_, ...), custom_call_target="tpu_custom_call" | custom-call | flops 18673040 | bytes 22118 | tf_op jit(solution)/shard_map/pallas_call | solution.py:142
  298.6 21.6 %shard_map.299 = (f32[1024,1152]{1,0:T(8,128)}, bf16[1024,2304]{1,0:T(8,128)(2,1)}, bf16[2304,1024]{1,0:T(8,128)(2,1)}, bf16[1024,2304]{1,0:T(8,128)(2,1)}, bf16[2304,1024]{1,0:T(8,128)(2,1)}) custom-call(f32[4]{0:T(128)S(1)} %compare_convert_fusion.refs_0_, f32[1024,1152]{1,0:T(8,128)} %bitcast.417, f32[1024,1152]{1,0:T(8,128)} %bitcast.431, ...), custom_call_target="tpu_custom_call" | custom-call | flops 8153726 | bytes 28901 | tf_op jit(solution)/shard_map/pallas_call | solution.py:189
  320.2 85.2 %shard_map.300 = (f32[1152,1024]{1,0:T(8,128)}, f32[1152,1024]{1,0:T(8,128)}, f32[1280,1]{1,0:T(8,128)}, f32[8,72,1280]{2,1,0:T(8,128)}, f32[8,72,1280]{2,1,0:T(...) custom-call(s32[1]{0:T(128)} %bitcast.14.core_ref, bf16[1024,2304]{1,0:T(8,128)(2,1)} %get-tuple-element.302.pair_ref, ...), custom_call_target="tpu_custom_call" | custom-call | flops 54358180 | bytes 47185 | tf_op jit(solution)/shard_map/pallas_call | solution.py:321
  407.2 5.7 collective-permute-done.13
  417.3 70.5 %shard_map.301 = (f32[1152,1024]{1,0:T(8,128)}, f32[1152,1024]{1,0:T(8,128)}, f32[1024,1]{1,0:T(8,128)}, f32[8,72,1024]{2,1,0:T(8,128)}, f32[8,72,1024]{2,1,0:T(...) custom-call(s32[1]{0:T(128)} %bitcast.14.core_ref, bf16[1024,2304]{1,0:T(8,128)(2,1)} %get-tuple-element.302.pair_ref, ...), custom_call_target="tpu_custom_call" | custom-call | flops 43486544 | bytes 42467 | tf_op jit(solution)/shard_map/pallas_call | solution.py:321
  491.1 3.7 add.1235
  500.5 85.3 %shard_map.302 = (f32[1152,1024]{1,0:T(8,128)}, f32[1152,1024]{1,0:T(8,128)}, f32[1280,1]{1,0:T(8,128)}, f32[8,72,1280]{2,1,0:T(8,128)}, f32[8,72,1280]{2,1,0:T(...) custom-call(s32[1]{0:T(128)} %bitcast.14.core_ref, bf16[1024,2304]{1,0:T(8,128)(2,1)} %get-tuple-element.302.pair_ref, ...), custom_call_target="tpu_custom_call" | custom-call | flops 54358180 | bytes 47185 | tf_op jit(solution)/shard_map/pallas_call | solution.py:321
  597.5 70.5 %shard_map.303 = (f32[1152,1024]{1,0:T(8,128)}, f32[1152,1024]{1,0:T(8,128)}, f32[1024,1]{1,0:T(8,128)}, f32[8,72,1024]{2,1,0:T(8,128)}, f32[8,72,1024]{2,1,0:T(...) custom-call(s32[1]{0:T(128)} %bitcast.14.core_ref, bf16[1024,2304]{1,0:T(8,128)(2,1)} %get-tuple-element.302.pair_ref, ...), custom_call_target="tpu_custom_call" | custom-call | flops 43486544 | bytes 42467 | tf_op jit(solution)/shard_map/pallas_call | solution.py:321
  679.4 28.3 %shard_map.304 = (f32[1024,1152]{1,0:T(8,128)}, f32[1024,1152]{1,0:T(8,128)}, f32[8,1152]{1,0:T(8,128)}, f32[1024,576]{1,0:T(8,128)}, f32[1024,576]{1,0:T(8,128)}) custom-call(f32[4]{0:T(128)} %copy-done.4, f32[1024,1152]{1,0:T(8,128)} %get-tuple-element.319.refs_1_, f32[1024,1152]{1,0:T(8,128)} %bitcast.432, f32[1,1152]{1,0:T(1,128)} %copy-done.3, ...), custom_call_target="tpu_custom_call" | custom-call | flops 8153726 | bytes 47775 | tf_op jit(solution)/shard_map/pallas_call | solution.py:384
  710.0 5.6 constant_dynamic-slice_fusion.16
  721.3 30.9 %shard_map.305 = (f32[1024,1728]{1,0:T(8,128)}, f32[1728,1024]{1,0:T(8,128)}, f32[8,16,512]{2,1,0:T(8,128)}, f32[4,1,1728]{2,1,0:T(1,128)}) custom-call(f32[1024,576]{1,0:T(8,128)} %get-tuple-element.333.query_ref, f32[1024,576]{1,0:T(8,128)} %get-tuple-element.334.keys_ref, f32[1024,576]{1,0:T(8,128)} %get-tuple-element.335.values_ref, ...), custom_call_target="tpu_custom_call" | custom-call | flops 16106127 | bytes 21233 | tf_op jit(solution)/shard_map/pallas_call | solution.py:455
  759.8 14.6 %shard_map.306 = (f32[8,72,1152]{2,1,0:T(8,128)}, f32[8,72,1152]{2,1,0:T(8,128)}) custom-call(s32[1]{0:T(128)} %bitcast.14.core_ref, f32[1728,1024]{1,0:T(8,128)} %get-tuple-element.355.refs_0_, f32[1024,1152]{1,0:T(8,128)} %get-tuple-element.388.refs_1_.refs_2_), custom_call_target="tpu_custom_call" | custom-call | flops 8153726 | bytes 19464 | tf_op jit(solution)/shard_map/pallas_call | solution.py:521
  789.9 16.5 %shard_map.307 = (f32[8,72,1152]{2,1,0:T(8,128)}, f32[8,72,1152]{2,1,0:T(8,128)}) custom-call(s32[1]{0:T(128)} %bitcast.14.core_ref, f32[1728,1024]{1,0:T(8,128)} %get-tuple-element.355.refs_0_, f32[576,1024]{1,0:T(8,128)} %get-tuple-element.356.refs_1_, f32[1024,1152]{1,0:T(8,128)} %get-tuple-element.388.refs_1_.refs_2_, ...), custom_call_target="tpu_custom_call" | custom-call | flops 8153726 | bytes 19464 | tf_op jit(solution)/shard_map/pallas_call | solution.py:521
  808.6 4.3 collective-permute-done.31
  827.0 30.7 %shard_map.308 = (f32[1024,1728]{1,0:T(8,128)}, f32[1728,1024]{1,0:T(8,128)}, f32[8,16,512]{2,1,0:T(8,128)}, f32[4,1,1728]{2,1,0:T(1,128)}) custom-call(f32[1024,576]{1,0:T(8,128)} %get-tuple-element.330.query_ref, f32[1024,576]{1,0:T(8,128)} %get-tuple-element.331.keys_ref, f32[1024,576]{1,0:T(8,128)} %get-tuple-element.332.values_ref, ...), custom_call_target="tpu_custom_call" | custom-call | flops 16106127 | bytes 21233 | tf_op jit(solution)/shard_map/pallas_call | solution.py:455
  867.7 17.4 %shard_map.309 = (f32[8,72,1152]{2,1,0:T(8,128)}, f32[8,72,1152]{2,1,0:T(8,128)}) custom-call(s32[1]{0:T(128)} %bitcast.14.core_ref, f32[1728,1024]{1,0:T(8,128)} %get-tuple-element.384.refs_0_, f32[576,1024]{1,0:T(8,128)} %get-tuple-element.385.refs_1_, f32[1024,1152]{1,0:T(8,128)} %get-tuple-element.388.refs_1_.refs_2_, ...), custom_call_target="tpu_custom_call" | custom-call | flops 8153726 | bytes 19464 | tf_op jit(solution)/shard_map/pallas_call | solution.py:521
  905.7 14.5 %shard_map.310 = (f32[8,72,1152]{2,1,0:T(8,128)}, f32[8,72,1152]{2,1,0:T(8,128)}) custom-call(s32[1]{0:T(128)} %bitcast.14.core_ref, f32[1728,1024]{1,0:T(8,128)} %get-tuple-element.384.refs_0_, f32[1024,1152]{1,0:T(8,128)} %get-tuple-element.388.refs_1_.refs_2_), custom_call_target="tpu_custom_call" | custom-call | flops 8153726 | bytes 19464 | tf_op jit(solution)/shard_map/pallas_call | solution.py:521
  922.4 4.6 collective-permute-done.42
  935.6 16.5 %collective-permute-done.44 = f32[4,72,1152]{2,1,0:T(8,128)S(1)} collective-permute-done((f32[4,72,1152]{2,1,0:T(8,128)}, f32[4,72,1152]{2,1,0:T(8,128)S(1)}, u32[]{:S(2)}, u32[]{:S(2)}) %collective-permute-start.44) | collective-permute-done | bytes 1327136 | tf_op jit(solution)/shard_map/ppermute | solution.py:611
  960.0 25.1 %shard_map.311 = (f32[512,1152]{1,0:T(8,128)}, f32[8,1152]{1,0:T(8,128)}) custom-call(f32[1024,1152]{1,0:T(8,128)} %bitcast.418, f32[1024,1152]{1,0:T(8,128)} %get-tuple-element.329.refs_3_.refs_1_, f32[1,1152]{1,0:T(1,128)} %reshape.1353.gain_ref.refs_2_, f32[1024,1728]{1,0:T(8,128)} %get-tuple-element.411.refs_3_, ...), custom_call_target="tpu_custom_call" | custom-call | flops 12230590 | bytes 30081 | tf_op jit(solution)/shard_map/pallas_call | solution.py:561
  990.9 11.4 collective-permute-done.48
  1014.4 25.2 %shard_map.312 = (f32[512,1152]{1,0:T(8,128)}, f32[8,1152]{1,0:T(8,128)}) custom-call(f32[1024,1152]{1,0:T(8,128)} %bitcast.419, f32[1024,1152]{1,0:T(8,128)} %get-tuple-element.329.refs_3_.refs_1_, f32[1,1152]{1,0:T(1,128)} %reshape.1353.gain_ref.refs_2_, f32[1024,1728]{1,0:T(8,128)} %get-tuple-element.411.refs_3_, ...), custom_call_target="tpu_custom_call" | custom-call | flops 12230590 | bytes 30081 | tf_op jit(solution)/shard_map/pallas_call | solution.py:561
  1057.4 8.2 collective-permute-done.61
  1067.6 6.7 collective-permute-done.63
  1076.8 14.7 %collective-permute-done.60 = f32[2,72,1152]{2,1,0:T(8,128)} collective-permute-done((f32[2,72,1152]{2,1,0:T(8,128)}, f32[2,72,1152]{2,1,0:T(8,128)}, u32[]{:S(2)}, u32[]{:S(2)}) %collective-permute-start.60) | collective-permute-done | bytes 663584 | tf_op jit(solution)/shard_map/ppermute | solution.py:614
  1111.1 18.4 %collective-permute-done.64 = f32[1,72,1152]{2,1,0:T(8,128)} collective-permute-done((f32[1,72,1152]{2,1,0:T(8,128)S(1)}, f32[1,72,1152]{2,1,0:T(8,128)}, u32[]{:S(2)}, u32[]{:S(2)}) %collective-permute-start.64) | collective-permute-done | bytes 331808 | tf_op jit(solution)/shard_map/ppermute | solution.py:614
  1144.3 8.0 concatenate.106
  1152.3 5.8 copy.543
  1159.3 9.1 maximum_multiply_fusion
  1175.8 8.9 maximum_multiply_fusion.1
  1184.7 25.1 %collective-permute-done.69 = f32[2,72,1152]{2,1,0:T(8,128)S(1)} collective-permute-done((f32[2,72,1152]{2,1,0:T(8,128)S(1)}, f32[2,72,1152]{2,1,0:T(8,128)S(1)}, u32[]{:S(2)}, u32[]{:S(2)}) %collective-permute-start.69) | collective-permute-done | bytes 663584 | tf_op jit(solution)/shard_map/ppermute | solution.py:614
  1211.1 28.3 %collective-permute-done.70 = f32[4,72,1152]{2,1,0:T(8,128)S(1)} collective-permute-done((f32[4,72,1152]{2,1,0:T(8,128)S(1)}, f32[4,72,1152]{2,1,0:T(8,128)S(1)}, u32[]{:S(2)}, u32[]{:S(2)}) %collective-permute-start.70) | collective-permute-done | bytes 1327136 | tf_op jit(solution)/shard_map/ppermute | solution.py:614
  1241.9 10.2 collective-permute-done.56
  1253.7 9.5 collective-permute-done.57
  1263.3 5.4 convolution_bitcast_fusion
  1268.7 4.7 collective-permute-done.58
  1276.9 15.4 %collective-permute-done.59 = f32[792,128]{1,0:T(8,128)S(1)} collective-permute-done((f32[792,128]{1,0:T(8,128)S(1)}, f32[792,128]{1,0:T(8,128)S(1)}, u32[]{:S(2)}, u32[]{:S(2)}) %collective-permute-start.59) | collective-permute-done | bytes 405536 | tf_op jit(solution)/shard_map/ppermute | solution.py:614
  1302.1 4.5 slice_multiply_fusion
  1306.6 3.8 fusion
  (502 shorter events, 289.0 us)
Async XLA Ops:
  7.2 84.0 %all-gather.7.cloned.1.call-start = ((), (), s32[]{:S(2)}) async-start(), calls=%async_computation | async-start | bytes 5640192 | tf_op jit(solution)/shard_map/all_gather | solution.py:629
  19.8 300.4 %all-gather.9.cloned.1.call-start = ((), (), s32[]{:S(2)}) async-start(), calls=%async_computation.1 | async-start | bytes 6266880 | tf_op jit(solution)/shard_map/all_gather | solution.py:629
  22.4 49.5 %collective-permute-start.1 = (f32[288,1152]{1,0:T(8,128)}, f32[288,1152]{1,0:T(8,128)}, u32[]{:S(2)}, u32[]{:S(2)}) collective-permute-start(f32[288,1152]{1,0:T(8,128)} %constant_dynamic-slice_fusion.29), channel_id=1, source_target_pairs={{0,1},{1,0},{2,3},{3,2},{4,5},{5,4},{6,7},{7,6},{8,9},{9,8},{10,11... | collective-permute-start | bytes 3981320 | tf_op jit(solution)/shard_map/ppermute | solution.py:611
  81.9 335.4 %all-gather.11.cloned.1.call-start = ((), (), s32[]{:S(2)}) async-start(), calls=%async_computation.2 | async-start | bytes 5013504 | tf_op jit(solution)/shard_map/all_gather | solution.py:629
  115.0 65.7 %collective-permute-start.9 = (f32[640,1152]{1,0:T(8,128)}, f32[640,1152]{1,0:T(8,128)S(1)}, u32[]{:S(2)}, u32[]{:S(2)}) collective-permute-start(f32[640,1152]{1,0:T(8,128)} %constant_dynamic-slice_fusion.25), channel_id=1, source_target_pairs={{0,1},{1,0},{2,3},{3,2},{4,5},{5,4},{6,7},{7,6},{8,9},{9,8},{10,11... | collective-permute-start | bytes 8847368 | tf_op jit(solution)/shard_map/ppermute | solution.py:611
  191.1 961.2 %all-gather.15.cloned.1.call-start = ((), (), s32[]{:S(2)}) async-start(), calls=%async_computation.4 | async-start | bytes 6266880 | tf_op jit(solution)/shard_map/all_gather | solution.py:682
  194.4 98.8 %collective-permute-start.6 = (f32[288,1152]{1,0:T(8,128)}, f32[288,1152]{1,0:T(8,128)}, u32[]{:S(2)}, u32[]{:S(2)}) collective-permute-start(f32[288,1152]{1,0:T(8,128)} %collective-permute-done.3), channel_id=1, source_target_pairs={{0,2},{2,0},{4,6},{6,4},{8,10},{10,8},{12,14},{14,12},{16,18},{18,... | collective-permute-start | bytes 3981320 | tf_op jit(solution)/shard_map/ppermute | solution.py:614
  199.7 205.8 %collective-permute-start.11 = (f32[512,1152]{1,0:T(8,128)}, f32[512,1152]{1,0:T(8,128)}, u32[]{:S(2)}, u32[]{:S(2)}) collective-permute-start(f32[512,1152]{1,0:T(8,128)} %constant_dynamic-slice_fusion.24), channel_id=1, source_target_pairs={{0,1},{1,0},{2,3},{3,2},{4,5},{5,4},{6,7},{7,6},{8,9},{9,8},{10,11... | collective-permute-start | bytes 7077896 | tf_op jit(solution)/shard_map/ppermute | solution.py:611
  200.3 53.9 %collective-permute-start.8 = (f32[2304]{0:T(1024)S(1)}, f32[2304]{0:T(1024)S(1)}, u32[]{:S(2)}, u32[]{:S(2)}) collective-permute-start(f32[2304]{0:T(1024)S(1)} %copy-done.67), channel_id=1, source_target_pairs={{0,1},{1,0},{2,3},{3,2},{4,5},{5,4},{6,7},{7,6},{8,9},{9,8},{10,11... | collective-permute-start | bytes 27656 | tf_op jit(solution)/shard_map/ppermute | solution.py:611
  202.3 53.7 %collective-permute-start.5 = (f32[8,961]{1,0:T(8,128)S(1)}, f32[8,961]{1,0:T(8,128)S(1)}, u32[]{:S(2)}, u32[]{:S(2)}) collective-permute-start(f32[8,961]{1,0:T(8,128)S(1)} %copy-done.63), channel_id=1, source_target_pairs={{0,1},{1,0},{2,3},{3,2},{4,5},{5,4},{6,7},{7,6},{8,9},{9,8},{10,11... | collective-permute-start | bytes 92264 | tf_op jit(solution)/shard_map/ppermute | solution.py:611
  202.9 52.4 %collective-permute-start.4 = (f32[4,3,576]{2,0,1:T(4,128)S(1)}, f32[4,3,576]{2,0,1:T(4,128)S(1)}, u32[]{:S(2)}, u32[]{:S(2)}) collective-permute-start(f32[4,3,576]{2,0,1:T(4,128)S(1)} %copy-done.64), channel_id=1, source_target_pairs={{0,1},{1,0},{2,3},{3,2},{4,5},{5,4},{6,7},{7,6},{8,9},{9,8},{10,11... | collective-permute-start | bytes 82952 | tf_op jit(solution)/shard_map/ppermute | solution.py:611
  405.5 82.3 %collective-permute-start.15 = (f32[5,8,16,1152]{3,2,1,0:T(8,128)}, f32[5,8,16,1152]{3,2,1,0:T(8,128)}, u32[]{:S(2)}, u32[]{:S(2)}) collective-permute-start(f32[5,8,16,1152]{3,2,1,0:T(8,128)} %get-tuple-element.284), channel_id=1, source_target_pairs={{0,2},{2,0},{4,6},{6,4},{8,10},{10,8},{12,14},{14,12},{16,18},{18,... | collective-permute-start | bytes 8847368 | tf_op jit(solution)/shard_map/ppermute | solution.py:614
  406.0 85.1 %collective-permute-start.14 = (f32[8,72,1280]{2,1,0:T(8,128)}, f32[8,72,1280]{2,1,0:T(8,128)}, u32[]{:S(2)}, u32[]{:S(2)}) collective-permute-start(f32[8,72,1280]{2,1,0:T(8,128)} %get-tuple-element.282), channel_id=1, source_target_pairs={{0,2},{2,0},{4,6},{6,4},{8,10},{10,8},{12,14},{14,12},{16,18},{18,... | collective-permute-start | bytes 8847368 | tf_op jit(solution)/shard_map/ppermute | solution.py:614
  494.8 99.9 %collective-permute-start.18 = (f32[8,72,1280]{2,1,0:T(8,128)}, f32[8,72,1280]{2,1,0:T(8,128)}, u32[]{:S(2)}, u32[]{:S(2)}) collective-permute-start(f32[8,72,1280]{2,1,0:T(8,128)} %add.1235), channel_id=1, source_target_pairs={{0,1},{1,0},{2,3},{3,2},{4,5},{5,4},{6,7},{7,6},{8,9},{9,8},{10,11... | collective-permute-start | bytes 8847368 | tf_op jit(solution)/shard_map/ppermute | solution.py:611
  495.5 93.1 %collective-permute-start.16 = (f32[8,72,1024]{2,1,0:T(8,128)}, f32[8,72,1024]{2,1,0:T(8,128)}, u32[]{:S(2)}, u32[]{:S(2)}) collective-permute-start(f32[8,72,1024]{2,1,0:T(8,128)} %get-tuple-element.297), channel_id=1, source_target_pairs={{0,2},{2,0},{4,6},{6,4},{8,10},{10,8},{12,14},{14,12},{16,18},{18,... | collective-permute-start | bytes 7077896 | tf_op jit(solution)/shard_map/ppermute | solution.py:614
  495.5 96.7 %collective-permute-start.17 = (f32[4,8,16,1152]{3,2,1,0:T(8,128)}, f32[4,8,16,1152]{3,2,1,0:T(8,128)}, u32[]{:S(2)}, u32[]{:S(2)}) collective-permute-start(f32[4,8,16,1152]{3,2,1,0:T(8,128)} %get-tuple-element.299), channel_id=1, source_target_pairs={{0,2},{2,0},{4,6},{6,4},{8,10},{10,8},{12,14},{14,12},{16,18},{18,... | collective-permute-start | bytes 7077896 | tf_op jit(solution)/shard_map/ppermute | solution.py:614
  496.0 98.7 %collective-permute-start.19 = (f32[5,4,16,1152]{3,2,1,0:T(8,128)}, f32[5,4,16,1152]{3,2,1,0:T(8,128)}, u32[]{:S(2)}, u32[]{:S(2)}) collective-permute-start(f32[5,4,16,1152]{3,2,1,0:T(8,128)} %fusion.9), channel_id=1, source_target_pairs={{0,4},{2,6},{4,0},{6,2},{8,12},{10,14},{12,8},{14,10},{16,20},{18,... | collective-permute-start | bytes 4423688 | tf_op jit(solution)/shard_map/ppermute | solution.py:614
  594.7 76.6 %collective-permute-start.20 = (f32[5,8,16,1152]{3,2,1,0:T(8,128)}, f32[5,8,16,1152]{3,2,1,0:T(8,128)}, u32[]{:S(2)}, u32[]{:S(2)}) collective-permute-start(f32[5,8,16,1152]{3,2,1,0:T(8,128)} %get-tuple-element.314), channel_id=1, source_target_pairs={{0,2},{2,0},{4,6},{6,4},{8,10},{10,8},{12,14},{14,12},{16,18},{18,... | collective-permute-start | bytes 8847368 | tf_op jit(solution)/shard_map/ppermute | solution.py:614
  594.7 79.3 %collective-permute-start.21 = (f32[8,72,1024]{2,1,0:T(8,128)}, f32[8,72,1024]{2,1,0:T(8,128)}, u32[]{:S(2)}, u32[]{:S(2)}) collective-permute-start(f32[8,72,1024]{2,1,0:T(8,128)} %add.1239), channel_id=1, source_target_pairs={{0,1},{1,0},{2,3},{3,2},{4,5},{5,4},{6,7},{7,6},{8,9},{9,8},{10,11... | collective-permute-start | bytes 7077896 | tf_op jit(solution)/shard_map/ppermute | solution.py:611
  596.3 113.0 %collective-permute-start.22 = (f32[8,72,1280]{2,1,0:T(8,128)}, f32[8,72,1280]{2,1,0:T(8,128)}, u32[]{:S(2)}, u32[]{:S(2)}) collective-permute-start(f32[8,72,1280]{2,1,0:T(8,128)} %get-tuple-element.338), channel_id=1, source_target_pairs={{0,2},{2,0},{4,6},{6,4},{8,10},{10,8},{12,14},{14,12},{16,18},{18,... | collective-permute-start | bytes 8847368 | tf_op jit(solution)/shard_map/ppermute | solution.py:614
  597.1 79.3 %collective-permute-start.23 = (f32[4,4,16,1152]{3,2,1,0:T(8,128)}, f32[4,4,16,1152]{3,2,1,0:T(8,128)}, u32[]{:S(2)}, u32[]{:S(2)}) collective-permute-start(f32[4,4,16,1152]{3,2,1,0:T(8,128)} %fusion.16), channel_id=1, source_target_pairs={{0,4},{2,6},{4,0},{6,2},{8,12},{10,14},{12,8},{14,10},{16,20},{18,... | collective-permute-start | bytes 3538952 | tf_op jit(solution)/shard_map/ppermute | solution.py:614
  674.0 41.6 %collective-permute-start.24 = (f32[5,4,16,1152]{3,2,1,0:T(8,128)}, f32[5,4,16,1152]{3,2,1,0:T(8,128)}, u32[]{:S(2)}, u32[]{:S(2)}) collective-permute-start(f32[5,4,16,1152]{3,2,1,0:T(8,128)} %fusion.8), channel_id=1, source_target_pairs={{0,4},{2,6},{4,0},{6,2},{8,12},{10,14},{12,8},{14,10},{16,20},{18,... | collective-permute-start | bytes 4423688 | tf_op jit(solution)/shard_map/ppermute | solution.py:614
  675.7 39.9 %collective-permute-start.25 = (f32[5,4,16,1152]{3,2,1,0:T(8,128)}, f32[5,4,16,1152]{3,2,1,0:T(8,128)}, u32[]{:S(2)}, u32[]{:S(2)}) collective-permute-start(f32[5,4,16,1152]{3,2,1,0:T(8,128)} %add_add_fusion), channel_id=1, source_target_pairs={{0,1},{1,0},{2,3},{3,2},{4,5},{5,4},{6,7},{7,6},{8,9},{9,8},{10,11... | collective-permute-start | bytes 4423688 | tf_op jit(solution)/shard_map/ppermute | solution.py:611
  676.3 78.0 %collective-permute-start.28 = (f32[8,72,1024]{2,1,0:T(8,128)}, f32[8,72,1024]{2,1,0:T(8,128)}, u32[]{:S(2)}, u32[]{:S(2)}) collective-permute-start(f32[8,72,1024]{2,1,0:T(8,128)} %get-tuple-element.352), channel_id=1, source_target_pairs={{0,2},{2,0},{4,6},{6,4},{8,10},{10,8},{12,14},{14,12},{16,18},{18,... | collective-permute-start | bytes 7077896 | tf_op jit(solution)/shard_map/ppermute | solution.py:614
  718.1 39.5 %collective-permute-start.26 = (f32[4,72,1280]{2,1,0:T(8,128)}, f32[4,72,1280]{2,1,0:T(8,128)}, u32[]{:S(2)}, u32[]{:S(2)}) collective-permute-start(f32[4,72,1280]{2,1,0:T(8,128)} %get-tuple-element.349), channel_id=1, source_target_pairs={{0,4},{2,6},{4,0},{6,2},{8,12},{10,14},{12,8},{14,10},{16,20},{18,... | collective-permute-start | bytes 4423688 | tf_op jit(solution)/shard_map/ppermute | solution.py:614
  720.4 39.4 %collective-permute-start.29 = (f32[4,4,16,1152]{3,2,1,0:T(8,128)}, f32[4,4,16,1152]{3,2,1,0:T(8,128)}, u32[]{:S(2)}, u32[]{:S(2)}) collective-permute-start(f32[4,4,16,1152]{3,2,1,0:T(8,128)} %fusion.15), channel_id=1, source_target_pairs={{0,1},{1,0},{2,3},{3,2},{4,5},{5,4},{6,7},{7,6},{8,9},{9,8},{10,11... | collective-permute-start | bytes 3538952 | tf_op jit(solution)/shard_map/ppermute | solution.py:611
  721.3 66.1 %collective-permute-start.32 = (f32[4,8,16,1152]{3,2,1,0:T(8,128)}, f32[4,8,16,1152]{3,2,1,0:T(8,128)}, u32[]{:S(2)}, u32[]{:S(2)}) collective-permute-start(f32[4,8,16,1152]{3,2,1,0:T(8,128)} %get-tuple-element.368), channel_id=1, source_target_pairs={{0,2},{2,0},{4,6},{6,4},{8,10},{10,8},{12,14},{14,12},{16,18},{18,... | collective-permute-start | bytes 7077896 | tf_op jit(solution)/shard_map/ppermute | solution.py:614
  774.4 43.1 %collective-permute-start.30 = (f32[8,72,1152]{2,1,0:T(8,128)}, f32[8,72,1152]{2,1,0:T(8,128)}, u32[]{:S(2)}, u32[]{:S(2)}) collective-permute-start(f32[8,72,1152]{2,1,0:T(8,128)} %get-tuple-element.365), channel_id=1, source_target_pairs={{0,2},{2,0},{4,6},{6,4},{8,10},{10,8},{12,14},{14,12},{16,18},{18,... | collective-permute-start | bytes 7962632 | tf_op jit(solution)/shard_map/ppermute | solution.py:614
  777.5 37.6 %collective-permute-start.33 = (f32[4,72,1024]{2,1,0:T(8,128)}, f32[4,72,1024]{2,1,0:T(8,128)}, u32[]{:S(2)}, u32[]{:S(2)}) collective-permute-start(f32[4,72,1024]{2,1,0:T(8,128)} %fusion.13), channel_id=1, source_target_pairs={{0,4},{2,6},{4,0},{6,2},{8,12},{10,14},{12,8},{14,10},{16,20},{18,... | collective-permute-start | bytes 3538952 | tf_op jit(solution)/shard_map/ppermute | solution.py:614
  819.6 339.6 %all-gather.13.cloned.1.call-start = ((), (), s32[]{:S(2)}) async-start(), calls=%async_computation.3 | async-start | bytes 6266880 | tf_op jit(solution)/shard_map/all_gather | solution.py:682
  819.9 45.2 %collective-permute-start.35 = (f32[8,72,1152]{2,1,0:T(8,128)}, f32[8,72,1152]{2,1,0:T(8,128)}, u32[]{:S(2)}, u32[]{:S(2)}) collective-permute-start(f32[8,72,1152]{2,1,0:T(8,128)} %get-tuple-element.378), channel_id=1, source_target_pairs={{0,2},{2,0},{4,6},{6,4},{8,10},{10,8},{12,14},{14,12},{16,18},{18,... | collective-permute-start | bytes 7962632 | tf_op jit(solution)/shard_map/ppermute | solution.py:614
  822.4 38.1 %collective-permute-start.38 = (f32[2,72,1024]{2,1,0:T(8,128)}, f32[2,72,1024]{2,1,0:T(8,128)S(1)}, u32[]{:S(2)}, u32[]{:S(2)}) collective-permute-start(f32[2,72,1024]{2,1,0:T(8,128)} %fusion.21), channel_id=1, source_target_pairs={{0,8},{2,10},{4,12},{6,14},{8,0},{10,2},{12,4},{14,6},{16,24},{18,... | collective-permute-start | bytes 1769480 | tf_op jit(solution)/shard_map/ppermute | solution.py:614
  822.4 40.4 %collective-permute-start.37 = (f32[4,4,16,1152]{3,2,1,0:T(8,128)}, f32[4,4,16,1152]{3,2,1,0:T(8,128)}, u32[]{:S(2)}, u32[]{:S(2)}) collective-permute-start(f32[4,4,16,1152]{3,2,1,0:T(8,128)} %fusion.12), channel_id=1, source_target_pairs={{0,4},{2,6},{4,0},{6,2},{8,12},{10,14},{12,8},{14,10},{16,20},{18,... | collective-permute-start | bytes 3538952 | tf_op jit(solution)/shard_map/ppermute | solution.py:614
  824.6 43.1 %collective-permute-start.39 = (f32[4,72,1152]{2,1,0:T(8,128)}, f32[4,72,1152]{2,1,0:T(8,128)}, u32[]{:S(2)}, u32[]{:S(2)}) collective-permute-start(f32[4,72,1152]{2,1,0:T(8,128)} %get-tuple-element.475), channel_id=1, source_target_pairs={{0,1},{1,0},{2,3},{3,2},{4,5},{5,4},{6,7},{7,6},{8,9},{9,8},{10,11... | collective-permute-start | bytes 3981320 | tf_op jit(solution)/shard_map/ppermute | solution.py:611
  885.1 47.2 %collective-permute-start.40 = (f32[8,72,1152]{2,1,0:T(8,128)}, f32[8,72,1152]{2,1,0:T(8,128)}, u32[]{:S(2)}, u32[]{:S(2)}) collective-permute-start(f32[8,72,1152]{2,1,0:T(8,128)} %get-tuple-element.394), channel_id=1, source_target_pairs={{0,2},{2,0},{4,6},{6,4},{8,10},{10,8},{12,14},{14,12},{16,18},{18,... | collective-permute-start | bytes 7962632 | tf_op jit(solution)/shard_map/ppermute | solution.py:614
  890.7 38.4 %collective-permute-start.41 = (f32[4,72,1152]{2,1,0:T(8,128)}, f32[4,72,1152]{2,1,0:T(8,128)}, u32[]{:S(2)}, u32[]{:S(2)}) collective-permute-start(f32[4,72,1152]{2,1,0:T(8,128)} %fusion.11), channel_id=1, source_target_pairs={{0,4},{2,6},{4,0},{6,2},{8,12},{10,14},{12,8},{14,10},{16,20},{18,... | collective-permute-start | bytes 3981320 | tf_op jit(solution)/shard_map/ppermute | solution.py:614
  901.3 55.0 %collective-permute-start.72 = (f32[8,1729]{1,0:T(8,128)}, f32[8,1729]{1,0:T(8,128)}, u32[]{:S(2)}, u32[]{:S(2)}) collective-permute-start(f32[8,1729]{1,0:T(8,128)} %pad_maximum_fusion.20), channel_id=1, source_target_pairs={{0,2},{2,0},{4,6},{6,4},{8,10},{10,8},{12,14},{14,12},{16,18},{18,... | collective-permute-start | bytes 165992 | tf_op jit(solution)/shard_map/ppermute | solution.py:614
  905.6 396.4 %all-gather.17.cloned.1.call-start = ((), (), s32[]{:S(2)}) async-start(), calls=%async_computation.5 | async-start | bytes 5640192 | tf_op jit(solution)/shard_map/all_gather | solution.py:682
  952.0 54.0 %collective-permute-start.45 = (f32[8,72,1152]{2,1,0:T(8,128)}, f32[8,72,1152]{2,1,0:T(8,128)}, u32[]{:S(2)}, u32[]{:S(2)}) collective-permute-start(f32[8,72,1152]{2,1,0:T(8,128)} %get-tuple-element.403), channel_id=1, source_target_pairs={{0,2},{2,0},{4,6},{6,4},{8,10},{10,8},{12,14},{14,12},{16,18},{18,... | collective-permute-start | bytes 7962632 | tf_op jit(solution)/shard_map/ppermute | solution.py:614
  957.2 46.5 %collective-permute-start.46 = (f32[4,72,1152]{2,1,0:T(8,128)}, f32[4,72,1152]{2,1,0:T(8,128)}, u32[]{:S(2)}, u32[]{:S(2)}) collective-permute-start(f32[4,72,1152]{2,1,0:T(8,128)} %get-tuple-element.406), channel_id=1, source_target_pairs={{0,4},{2,6},{4,0},{6,2},{8,12},{10,14},{12,8},{14,10},{16,20},{18,... | collective-permute-start | bytes 3981320 | tf_op jit(solution)/shard_map/ppermute | solution.py:614
  957.6 46.1 %collective-permute-start.47 = (f32[4,72,1152]{2,1,0:T(8,128)}, f32[4,72,1152]{2,1,0:T(8,128)}, u32[]{:S(2)}, u32[]{:S(2)}) collective-permute-start(f32[4,72,1152]{2,1,0:T(8,128)} %bitcast_add_fusion.5), channel_id=1, source_target_pairs={{0,1},{1,0},{2,3},{3,2},{4,5},{5,4},{6,7},{7,6},{8,9},{9,8},{10,11... | collective-permute-start | bytes 3981320 | tf_op jit(solution)/shard_map/ppermute | solution.py:611
  958.4 91.6 %collective-permute-start.73 = (f32[16,1729]{1,0:T(8,128)S(1)}, f32[16,1729]{1,0:T(8,128)}, u32[]{:S(2)}, u32[]{:S(2)}) collective-permute-start(f32[16,1729]{1,0:T(8,128)S(1)} %pad_maximum_fusion.17), channel_id=1, source_target_pairs={{0,4},{2,6},{4,0},{6,2},{8,12},{10,14},{12,8},{14,10},{16,20},{18,... | collective-permute-start | bytes 331976 | tf_op jit(solution)/shard_map/ppermute | solution.py:614
  1054.2 44.6 %collective-permute-start.74 = (f32[32,1729]{1,0:T(8,128)}, f32[32,1729]{1,0:T(8,128)}, u32[]{:S(2)}, u32[]{:S(2)}) collective-permute-start(f32[32,1729]{1,0:T(8,128)} %pad_maximum_fusion.16), channel_id=1, source_target_pairs={{0,8},{2,10},{4,12},{6,14},{8,0},{10,2},{12,4},{14,6},{16,24},{18,... | collective-permute-start | bytes 663944 | tf_op jit(solution)/shard_map/ppermute | solution.py:614
  1054.2 38.5 %collective-permute-start.62 = (f32[4,72,1024]{2,1,0:T(8,128)}, f32[4,72,1024]{2,1,0:T(8,128)}, u32[]{:S(2)}, u32[]{:S(2)}) collective-permute-start(f32[4,72,1024]{2,1,0:T(8,128)} %bitcast.95), channel_id=1, source_target_pairs={{0,4},{2,6},{4,0},{6,2},{8,12},{10,14},{12,8},{14,10},{16,20},{18,... | collective-permute-start | bytes 3538952 | tf_op jit(solution)/shard_map/ppermute | solution.py:614
  1055.4 36.1 %collective-permute-start.60 = (f32[2,72,1152]{2,1,0:T(8,128)}, f32[2,72,1152]{2,1,0:T(8,128)}, u32[]{:S(2)}, u32[]{:S(2)}) collective-permute-start(f32[2,72,1152]{2,1,0:T(8,128)} %fusion.20), channel_id=1, source_target_pairs={{0,8},{2,10},{4,12},{6,14},{8,0},{10,2},{12,4},{14,6},{16,24},{18,... | collective-permute-start | bytes 1990664 | tf_op jit(solution)/shard_map/ppermute | solution.py:614
  1096.5 36.2 %collective-permute-start.65 = (f32[8,72,1024]{2,1,0:T(8,128)}, f32[8,72,1024]{2,1,0:T(8,128)}, u32[]{:S(2)}, u32[]{:S(2)}) collective-permute-start(f32[8,72,1024]{2,1,0:T(8,128)} %bitcast.113), channel_id=1, source_target_pairs={{0,2},{2,0},{4,6},{6,4},{8,10},{10,8},{12,14},{14,12},{16,18},{18,... | collective-permute-start | bytes 7077896 | tf_op jit(solution)/shard_map/ppermute | solution.py:614
  1173.6 36.2 %collective-permute-start.69 = (f32[2,72,1152]{2,1,0:T(8,128)S(1)}, f32[2,72,1152]{2,1,0:T(8,128)S(1)}, u32[]{:S(2)}, u32[]{:S(2)}) collective-permute-start(f32[2,72,1152]{2,1,0:T(8,128)S(1)} %maximum_bitcast_fusion), channel_id=1, source_target_pairs={{0,8},{2,10},{4,12},{6,14},{8,0},{10,2},{12,4},{14,6},{16,24},{18,... | collective-permute-start | bytes 1990664 | tf_op jit(solution)/shard_map/ppermute | solution.py:614
  1240.1 56.8 %collective-permute-start.71 = (f32[8,72,1152]{2,1,0:T(8,128)S(1)}, f32[8,72,1152]{2,1,0:T(8,128)}, u32[]{:S(2)}, u32[]{:S(2)}) collective-permute-start(f32[8,72,1152]{2,1,0:T(8,128)S(1)} %bitcast.434), channel_id=1, source_target_pairs={{0,2},{2,0},{4,6},{6,4},{8,10},{10,8},{12,14},{14,12},{16,18},{18,... | collective-permute-start | bytes 7962632 | tf_op jit(solution)/shard_map/ppermute | solution.py:614
  (115 other events, 1582.3 us)
Sparse Core Ops, SparseCore 0:
  20.0 57.8 all-gather.6
  82.0 60.0 all-gather.8
  191.2 53.7 all-gather.10
  819.7 71.3 all-gather.14
  905.7 68.0 all-gather.12
  1152.4 61.8 all-gather.16

commit v2 on v1

--- a/solution.py
+++ b/solution.py
@@ -168,7 +168,7 @@
     live_ref, tokens_ref, cotangent_ref = refs[:3]
     mixed_refs = refs[3 : 3 + parts]
     weight_refs = refs[3 + parts : 3 + 2 * parts]
-    bias_ref, gain_ref, shift_ref, middle_ref, pair_ref, flip_ref, grad_pair_ref, grad_flip_ref = refs[3 + 2 * parts :]
+    bias_ref, gain_ref, shift_ref, middle_ref, pair_ref, grad_ref = refs[3 + 2 * parts :]
     dim = tokens_ref.shape[1]
     middle = tokens_ref[...] + bias_ref[...]
     for mixed_ref, weight_ref in zip(mixed_refs, weight_refs):
@@ -176,10 +176,9 @@
     middle_ref[...] = middle
     scaled, _ = standardize(middle)
     normed = scaled * gain_ref[...] + shift_ref[...]
+    pair_ref[:, :dim], pair_ref[:, dim:] = halves(normed)
     grad = cotangent_ref[...] * live_ref[pl.program_id(0)]
-    for value, pair_out, flip_out in ((normed, pair_ref, flip_ref), (grad, grad_pair_ref, grad_flip_ref)):
-        pair_out[:, :dim], pair_out[:, dim:] = halves(value)
-        flip_out[:dim], flip_out[dim:] = halves(value.T)
+    grad_ref[:, :dim], grad_ref[:, dim:] = halves(grad)
 
 
 def output_forward(live, tokens, cotangent, mixed, weights, bias, gain, shift):
@@ -194,14 +193,16 @@
         + [rows(PATCHES, m.shape[1]) for m in mixed]
         + [fixed(w.shape) for w in weights]
         + [fixed((1, dim))] * 3,
-        out_specs=[rows(PATCHES, dim)]
-        + [rows(PATCHES, 2 * dim), pl.BlockSpec((2 * dim, PATCHES), lambda i: (0, i))] * 2,
-        out_shape=[jax.ShapeDtypeStruct((count, dim), jnp.float32)]
-        + [
-            jax.ShapeDtypeStruct((count, 2 * dim), jnp.bfloat16),
-            jax.ShapeDtypeStruct((2 * dim, count), jnp.bfloat16),
-        ]
-        * 2,
+        out_specs=[
+            rows(PATCHES, dim),
+            rows(PATCHES, 2 * dim),
+            rows(PATCHES, 2 * dim),
+        ],
+        out_shape=[
+            jax.ShapeDtypeStruct((count, dim), jnp.float32),
+            pair,
+            pair,
+        ],
         compiler_params=params(48),
         cost_estimate=cost(6 * count * dim * dim, 4 * (dim * dim + 5 * count * dim)),
     )(live, tokens, cotangent, *mixed, *weights, bias, gain, shift)
@@ -211,12 +212,10 @@
 PIECE = BLOCK // 16
 
 
-def feed_kernel(
-    split, core_ref, pair_ref, flip_ref, grad_pair_ref, grad_flip_ref, hidden_ref, bias_ref, return_ref, *refs
-):
+def feed_kernel(split, core_ref, pair_ref, grad_ref, hidden_ref, bias_ref, return_ref, *refs):
     result_ref, second_ref, d_bias_ref = refs[:3]
-    outs = refs[3:-7]
-    up_ref, down_ref, hidden3_ref, return3_ref, active3_ref, slope3_ref, block_ref = refs[-7:]
+    outs = refs[3:-5]
+    hidden3_ref, return3_ref, active3_ref, slope3_ref, block_ref = refs[-5:]
     count = pair_ref.shape[0]
     dim = pair_ref.shape[1] // 2
     chunk = min(512, count)
@@ -227,121 +226,105 @@
         second_ref[...] = jnp.zeros_like(second_ref)
 
     d_bias_ref[...] = jnp.zeros_like(d_bias_ref)
-
-    def triple_columns(ref, value, size):
-        high, low = halves(value)
-        ref[:, :size] = high
-        ref[:, size : 2 * size] = high
-        ref[:, 2 * size :] = low
-
-    def triple_rows(ref, part, value):
-        high, low = halves(value)
-        ref[:BLOCK, part] = high
-        ref[BLOCK : 2 * BLOCK, part] = low
-        ref[2 * BLOCK :, part] = high
-
-    triple_columns(down_ref, return_ref[...], dim)
-    triple_columns(up_ref, hidden_ref[...].T, dim)
-    triple_columns(hidden3_ref, hidden_ref[...], BLOCK)
-    triple_columns(return3_ref, return_ref[...].T, BLOCK)
-
-    def tokens_step(step, carry):
-        part = pl.ds(pl.multiple_of(step * chunk, chunk), chunk)
-        d_active = mul(down_ref[:, : 2 * dim], grad_flip_ref[:, part], 1, 0) + mul(
-            down_ref[:, 2 * dim :], grad_flip_ref[:dim, part], 1, 0
-        )
+    high, low = halves(hidden_ref[...])
+    hidden3_ref[:, :BLOCK] = high
+    hidden3_ref[:, BLOCK : 2 * BLOCK] = high
+    hidden3_ref[:, 2 * BLOCK :] = low
+    high, low = halves(return_ref[...])
+    return3_ref[:BLOCK] = high
+    return3_ref[BLOCK : 2 * BLOCK] = high
+    return3_ref[2 * BLOCK :] = low
+
+    for begin in range(0, count, chunk):
+        part = slice(begin, begin + chunk)
         hidden = (
-            mul(up_ref[:, : 2 * dim], flip_ref[:, part], 1, 0)
-            + mul(up_ref[:, 2 * dim :], flip_ref[:dim, part], 1, 0)
+            mul(pair_ref[part, :dim], hidden3_ref[:, :BLOCK], 1, 0)
+            + mul(pair_ref[part, dim:], hidden3_ref[:, :BLOCK], 1, 0)
+            + mul(pair_ref[part, :dim], hidden3_ref[:, 2 * BLOCK :], 1, 0)
             + bias_ref[...]
         )
+        d_active = (
+            mul(grad_ref[part, :dim], return3_ref[:BLOCK], 1, 1)
+            + mul(grad_ref[part, dim:], return3_ref[:BLOCK], 1, 1)
+            + mul(grad_ref[part, :dim], return3_ref[2 * BLOCK :], 1, 1)
+        )
         cumul = 0.5 * (1.0 + lax.erf(hidden * 2.0 ** (-0.5)))
-        triple_rows(active3_ref, part, hidden * cumul)
+        high, low = halves(hidden * cumul)
+        active3_ref[part, :BLOCK] = high
+        active3_ref[part, BLOCK : 2 * BLOCK] = low
+        active3_ref[part, 2 * BLOCK :] = high
         density = hidden * jnp.exp(-0.5 * hidden * hidden) * (1.0 / math.sqrt(2.0 * math.pi))
         d_hidden = d_active * (cumul + density)
-        triple_rows(slope3_ref, part, d_hidden)
-        d_bias_ref[...] += jnp.sum(d_hidden, 1, keepdims=True)
-        result_ref[:, part] += mul(return3_ref[...], active3_ref[:, part], 1, 0)
-        second_ref[:, part] += mul(hidden3_ref[...], slope3_ref[:, part], 1, 0)
-        return carry
-
-    lax.fori_loop(0, count // chunk, tokens_step, 0)
+        high, low = halves(d_hidden)
+        slope3_ref[part, :BLOCK] = high
+        slope3_ref[part, BLOCK : 2 * BLOCK] = low
+        slope3_ref[part, 2 * BLOCK :] = high
+        d_bias_ref[...] += jnp.sum(d_hidden, 0, keepdims=True)
+        result_ref[part, :] += mul(active3_ref[part, :], return3_ref[...], 1, 0)
+        second_ref[part, :] += mul(slope3_ref[part, :], hidden3_ref[...], 1, 1)
 
     def weight_grad(left_ref, right_ref):
-        wide = mul(left_ref[:BLOCK], right_ref[...], 1, 0)
-        return wide[:, :dim] + wide[:, dim:] + mul(left_ref[BLOCK : 2 * BLOCK], right_ref[:, :dim], 1, 0)
+        wide = mul(left_ref[:, :BLOCK], right_ref[...], 0, 0)
+        return wide[:, :dim] + wide[:, dim:] + mul(left_ref[:, BLOCK : 2 * BLOCK], right_ref[:, :dim], 0, 0)
 
     if split:
-        hidden_keep, hidden_send, return_keep, return_send = outs
-        block_ref[...] = weight_grad(active3_ref, grad_pair_ref)
-
-        def place_return(even_ref, odd_ref):
+        block_ref[0] = weight_grad(active3_ref, grad_ref)
+        block_ref[1] = weight_grad(slope3_ref, pair_ref)
+
+        def place(index, even_ref, odd_ref):
             for pair in range(8):
-                even_ref[0, pair] = block_ref[2 * pair * PIECE : (2 * pair + 1) * PIECE]
-                odd_ref[0, pair] = block_ref[(2 * pair + 1) * PIECE : (2 * pair + 2) * PIECE]
-
-        pl.when(core_ref[0] == 0)(lambda: place_return(return_keep, return_send))
-        pl.when(core_ref[0] == 1)(lambda: place_return(return_send, return_keep))
-        value = weight_grad(slope3_ref, pair_ref).T
-        piece = dim // 16
-
-        def place_hidden(even_ref, odd_ref):
-            for pair in range(8):
-                even_ref[pair] = value[2 * pair * piece : (2 * pair + 1) * piece]
-                odd_ref[pair] = value[(2 * pair + 1) * piece : (2 * pair + 2) * piece]
-
-        pl.when(core_ref[0] == 0)(lambda: place_hidden(hidden_keep, hidden_send))
-        pl.when(core_ref[0] == 1)(lambda: place_hidden(hidden_send, hidden_keep))
+                even_ref[0, pair] = block_ref[index, 2 * pair * PIECE : (2 * pair + 1) * PIECE]
+                odd_ref[0, pair] = block_ref[index, (2 * pair + 1) * PIECE : (2 * pair + 2) * PIECE]
+
+        @pl.when(core_ref[0] == 0)
+        def _():
+            place(0, outs[2], outs[3])
+            place(1, outs[0], outs[1])
+
+        @pl.when(core_ref[0] == 1)
+        def _():
+            place(0, outs[3], outs[2])
+            place(1, outs[1], outs[0])
     else:
-        outs[1][...] = weight_grad(active3_ref, grad_pair_ref)
-        outs[0][...] = weight_grad(slope3_ref, pair_ref).T
+        outs[1][...] = weight_grad(active3_ref, grad_ref)
+        outs[0][...] = weight_grad(slope3_ref, pair_ref)
 
 
 def feed(split, core, tokens_forms, hidden_weight, hidden_bias, return_weight, first, blocks):
-    pair, flip = tokens_forms[:2]
+    pair, grad = tokens_forms
     count = pair.shape[0]
     dim = pair.shape[1] // 2
     units = blocks * BLOCK
-    whole = jax.ShapeDtypeStruct((dim, count), jnp.float32)
+    whole = jax.ShapeDtypeStruct((count, dim), jnp.float32)
     if split:
-        hidden_out = jax.ShapeDtypeStruct((8, dim // 16, units), jnp.float32)
-        return_out = jax.ShapeDtypeStruct((blocks, 8, PIECE, dim), jnp.float32)
-        out_specs = [pl.BlockSpec((8, dim // 16, BLOCK), lambda i: (0, 0, i))] * 2 + [
-            pl.BlockSpec((1, 8, PIECE, dim), lambda i: (i, 0, 0, 0))
-        ] * 2
-        out_shape = [hidden_out] * 2 + [return_out] * 2
+        out_specs = [pl.BlockSpec((1, 8, PIECE, dim), lambda i: (i, 0, 0, 0))] * 4
+        out_shape = [jax.ShapeDtypeStruct((blocks, 8, PIECE, dim), jnp.float32)] * 4
     else:
-        out_specs = [pl.BlockSpec((dim, BLOCK), lambda i: (0, i)), rows(BLOCK, dim)]
-        out_shape = [
-            jax.ShapeDtypeStruct((dim, units), jnp.float32),
-            jax.ShapeDtypeStruct((units, dim), jnp.float32),
-        ]
-    wide = pltpu.VMEM((BLOCK, 3 * dim), jnp.bfloat16)
-    tall = pltpu.VMEM((dim, 3 * BLOCK), jnp.bfloat16)
+        out_specs = [rows(BLOCK, dim)] * 2
+        out_shape = [jax.ShapeDtypeStruct((units, dim), jnp.float32)] * 2
     return pl.pallas_call(
         functools.partial(feed_kernel, split),
         grid=(blocks,),
-        in_specs=[scalars()]
-        + [fixed(form.shape) for form in tokens_forms]
-        + [
+        in_specs=[
+            scalars(),
+            fixed(pair.shape),
+            fixed(grad.shape),
             pl.BlockSpec((dim, BLOCK), lambda i: (0, first + i)),
-            pl.BlockSpec((BLOCK, 1), lambda i: (first + i, 0)),
+            pl.BlockSpec((1, BLOCK), lambda i: (0, first + i)),
             pl.BlockSpec((BLOCK, dim), lambda i: (first + i, 0)),
         ],
-        out_specs=[fixed((dim, count)), fixed((dim, count)), rows(BLOCK, 1)] + out_specs,
-        out_shape=[whole, whole, jax.ShapeDtypeStruct((units, 1), jnp.float32)] + out_shape,
+        out_specs=[fixed((count, dim)), fixed((count, dim)), pl.BlockSpec((1, BLOCK), lambda i: (0, i))] + out_specs,
+        out_shape=[whole, whole, jax.ShapeDtypeStruct((1, units), jnp.float32)] + out_shape,
         scratch_shapes=[
-            wide,
-            wide,
-            tall,
-            tall,
-            pltpu.VMEM((3 * BLOCK, count), jnp.bfloat16),
-            pltpu.VMEM((3 * BLOCK, count), jnp.bfloat16),
-            pltpu.VMEM((BLOCK, dim), jnp.float32),
+            pltpu.VMEM((dim, 3 * BLOCK), jnp.bfloat16),
+            pltpu.VMEM((3 * BLOCK, dim), jnp.bfloat16),
+            pltpu.VMEM((count, 3 * BLOCK), jnp.bfloat16),
+            pltpu.VMEM((count, 3 * BLOCK), jnp.bfloat16),
+            pltpu.VMEM((2, BLOCK, dim), jnp.float32),
         ],
-        compiler_params=params(62),
+        compiler_params=params(60),
         cost_estimate=cost(36 * count * dim * units, 4 * (4 * dim * units + 5 * count * dim), 2 * count * units),
-    )(core, *tokens_forms, hidden_weight, hidden_bias, return_weight)
+    )(core, pair, grad, hidden_weight, hidden_bias, return_weight)
 
 
 def middle_kernel(parts, feeds, *refs):
@@ -353,14 +336,13 @@
     mix_refs = refs[8 + 2 * feeds + parts :]
     middle = middle_ref[...]
     grad = cotangent_ref[...] * live_ref[pl.program_id(0)]
-    result = result_parts[0][...]
+    result = middle + bias_ref[...]
     second = second_parts[0][...]
-    for part in result_parts[1:]:
+    for part in result_parts:
         result = result + part[...]
     for part in second_parts[1:]:
         second = second + part[...]
-    result_ref[...] = middle + bias_ref[...] + result.T
-    second = second.T
+    result_ref[...] = result
     scaled, inverse = standardize(middle)
     d_middle = grad + norm_back(second * gain_ref[...], scaled, inverse)
     d_middle_ref[...] = d_middle
@@ -387,7 +369,7 @@
         in_specs=[scalars()]
         + [rows(PATCHES, dim)] * 2
         + [fixed((1, dim))] * 2
-        + [pl.BlockSpec((dim, PATCHES), lambda i: (0, i))] * (2 * len(results))
+        + [rows(PATCHES, dim)] * (2 * len(results))
         + [fixed(w.shape) for w in weights],
         out_specs=[rows(PATCHES, dim)] * 2 + [fixed((8, dim))] + [rows(PATCHES, w.shape[0]) for w in weights],
         out_shape=[block, block, jax.ShapeDtypeStruct((8, dim), jnp.float32)]
@@ -635,10 +617,8 @@
             value = value + self.along(value, bit)
         return value
 
-    def all_rows(self, value):
-        for bit in range(4):
-            value = self.ordered(value, self.along(value, bit), bit)
-        return value
+    def rows_step(self, value, bit):
+        return self.ordered(value, self.along(value, bit), bit)
 
 
 class Reduction:
@@ -723,67 +703,78 @@
     norm_first = (row(first_gain), row(first_shift))
     norm_second = (row(second_gain), row(second_shift))
 
+    def time_gradient(packed):
+        d_time_all = packed[:, :-1].reshape(-1, 3, width)
+        onehot_all = packed[:, -1:].astype(jnp.int32) == jnp.arange(buckets)[None, :]
+        time_all = jnp.dot(onehot_all.astype(jnp.float32), time_table, precision=HIGHEST)
+        grad = jnp.einsum("sce,sd->ced", d_time_all * inv_total, time_all, precision=HIGH)
+        return grad.transpose(0, 2, 1)
+
+    def absolute(own, other):
+        flag = rank == 0
+        return jnp.concatenate([jnp.where(flag, own, other), jnp.where(flag, other, own)], 0)
+
     def times_of(value):
         return value.reshape(own_images, 1, -1)
 
     if split:
         ring = Ring()
-        more = (units // BLOCK + 1) // 2
-        cuts = [(0, more), (more, units // BLOCK - more)]
+        less = units // BLOCK // 2
+        cuts = [(0, less), (less, units // BLOCK - less)]
+        table_other = ring.across(bias_table)
+        bias_other = row(ring.across(hidden_bias))
+        hidden_shares = [ring.share(hidden_weight, dim, first * BLOCK, blocks * BLOCK) for first, blocks in cuts]
         qk = ring.across(ring.share(attend_own, 2 * width, 0, dim))
-        qk_full = ring.spread(qk)
+        hidden_share, hidden_share_2 = [ring.across(share) for share in hidden_shares]
         values_half = ring.core_half(attend_own, 2 * width, width)
-        values_half, qk = join(values_half, qk)
+        output_half = ring.core_half(output_weight, 0, width)
+        qk, table_other, bias_other, values_half, output_half, time_proj, strips_own = join(
+            qk, table_other, bias_other, values_half, output_half, time_proj, make_strips(bias_table)
+        )
+        attend_qk = ring.spread(qk)
         values_mine = ring.across(values_half)
+        output_mine = ring.across(output_half)
         time_mine = lax.dynamic_slice_in_dim(time_proj, first_own, own_images, 0)
         time_theirs = lax.dynamic_slice_in_dim(time_proj, (1 - rank) * own_images, own_images, 0)
-        strips_own = make_strips(bias_table)
-        tokens_a, qk, time_theirs = join(tokens2, qk, time_theirs)
-        own = attend_forward(tokens_a, *norm_first, attend_own, times_of(time_mine), strips_own)
-        own, values_mine, time_theirs, bias_table_b = join(own, values_mine, time_theirs, bias_table)
         time_other = ring.across(time_theirs)
-        table_other = ring.across(bias_table_b)
-        bias_other = column(ring.across(hidden_bias))
-        output_mine = ring.across(ring.core_half(output_weight, 0, width))
-        values_theirs = ring.along(values_mine, 0)
-        hidden_other = []
-        for first, blocks in cuts:
-            part = ring.share(hidden_weight, dim, first * BLOCK, blocks * BLOCK)
-            part, values_mine = join(part, values_mine)
-            hidden_other.append(ring.spread(ring.across(part)))
-        attend_other = jnp.concatenate([qk_full, ring.ordered(values_mine, values_theirs, 0)], 0)
-        attend_other, output_mine = join(attend_other, output_mine)
-        first_half = ring.core_half(return_weight, 0, cuts[0][1] * BLOCK)
-        first_half, output_mine = join(first_half, output_mine)
-        return_mine = ring.across(first_half)
+        own = attend_forward(tokens2, *norm_first, attend_own, times_of(time_mine), strips_own)
+        return_halves = [ring.core_half(return_weight, first * BLOCK, blocks * BLOCK) for first, blocks in cuts]
+        own, values_mine, output_mine, time_other, return_half, hidden_share, hidden_share_2 = join(
+            own, values_mine, output_mine, time_other, return_halves[0], hidden_share, hidden_share_2
+        )
+        hidden_other = [ring.spread(hidden_share), ring.spread(hidden_share_2)]
+        strips_other = make_strips(table_other)
+        values_full = ring.ordered(values_mine, ring.along(values_mine, 0), 0)
         output_other = ring.ordered(output_mine, ring.along(output_mine, 0), 0)
-        other = attend_forward(
-            tokens2, *norm_first, attend_other, times_of(time_other), make_strips(table_other)
-        )
-        strips_other = make_strips(table_other)
+        attend_other = jnp.concatenate([attend_qk, values_full], 0)
+        return_mine = ring.across(return_half)
+        other = attend_forward(tokens2, *norm_first, attend_other, times_of(time_other), strips_other)
         attend = [attend_own, attend_other]
         output = [output_weight, output_other]
+        other, return_mine = join(other, return_mine)
+        return_theirs = ring.along(return_mine, 0)
         middle, *forms = output_forward(
             live, tokens2, cotangent2, [own[3], other[3]], output, row(output_bias), *norm_second
         )
-        second_half = ring.core_half(return_weight, cuts[1][0] * BLOCK, cuts[1][1] * BLOCK)
-        return_1, second_half = join(ring.ordered(return_mine, ring.along(return_mine, 0), 0), second_half)
-        return_mine = ring.across(second_half)
+        forms, return_theirs, return_half = join(forms, return_theirs, return_halves[1])
+        return_1 = ring.ordered(return_mine, return_theirs, 0)
+        return_mine = ring.across(return_half)
 
         def feed_other(forms, index, hidden, back):
             first, blocks = cuts[index]
-            bias = bias_other[first * BLOCK : (first + blocks) * BLOCK]
+            bias = bias_other[:, first * BLOCK : (first + blocks) * BLOCK]
             return feed(True, core, forms, hidden, bias, back, 0, blocks)
 
         def feed_own(forms, index):
-            return feed(True, core, forms, hidden_weight, column(hidden_bias), return_weight, *cuts[index])
-
-        h1, h2, r1, r2, qa, qb = (Reduction(ring, axis) for axis in (0, 0, 1, 1, 0, 0))
+            return feed(True, core, forms, hidden_weight, row(hidden_bias), return_weight, *cuts[index])
+
+        h1, h2, r1, r2, qa, qb = (Reduction(ring, axis) for axis in (1, 1, 1, 1, 0, 0))
         other_1 = feed_other(forms, 0, hidden_other[0], return_1)
         forms, other_1, return_mine = join(forms, other_1, return_mine)
-        h1.begin("other", *other_1[3:5])
-        r1.begin("other", *other_1[5:7])
         return_2 = ring.ordered(return_mine, ring.along(return_mine, 0), 0)
+        forms, return_2, sent = join(forms, return_2, other_1[3:7])
+        h1.begin("other", *sent[:2])
+        r1.begin("other", *sent[2:])
         other_2 = feed_other(forms, 1, hidden_other[1], return_2)
         forms, other_2, a, b = join(forms, other_2, h1.value("other"), r1.send("other"))
         h1_cross, r1_y = a, b
@@ -823,6 +814,9 @@
         r1.pass_on("own", b)
         h2.pass_on("own", c)
 
+        def pair_up(first, second):
+            return jnp.stack([first, second]).reshape(1, -1, dim)
+
         def weights_a(attended, normed):
             return attend_weights(True, core, [attended[1]], [normed], [0], [2])
 
@@ -843,79 +837,86 @@
         r2.pass_on("own", c)
         r2.terms["own"].append(r2_crossed)
         h2.pass_on("own", d)
-        return_1 = r1.gather(e)
+        return_1 = e
         attended_own = attend_backward(*own[:4], d_mixed_own, own[5], strips_own)
         attended_own, a, b, c, d, e, qa_first = join(
-            attended_own, qb.send("other"), h1.value("own"), r2.send("own"), h2.send("own"), a[4:], qa_first
+            attended_own, qb.send("other"), pair_up(h1.value("own"), return_1), r2.send("own"), h2.send("own"), a[4:],
+            qa_first,
         )
         qb.pass_on("other", a)
-        hidden_1 = h1.gather(b)
+        units_1 = ring.spread(b)
         r2.pass_on("own", c)
         h2.pass_on("own", d)
         qa_second = ring.across(e)
+        d_time_got = ring.across(attended_other[3].reshape(own_images, 3, width))
         part = weights_b(attended_own, normed_first, own[4])
-        part, normed_first = join(part, normed_first)
+        part, normed_first, d_time_got = join(part, normed_first, d_time_got)
+        d_time = absolute(attended_own[3].reshape(own_images, 3, width), d_time_got)
+        packed = jnp.concatenate([d_time.reshape(images, -1), bucket.astype(jnp.float32)[:, None]], 1)
+        packed = ring.rows_step(packed, 0)
         qb.begin("own", *part)
         part = weights_a(attended_own, normed_first)
-        part, d_projs, a, b, c, d, qa_second = join(
+        part, d_projs, a, b, c, qa_second, packed = join(
             part, [attended_own[0], attended_other[0]], qb.send("own"), qb.value("other"), r2.send("own"),
-            h2.value("own"), qa_second,
+            qa_second, packed,
         )
         qa.begin("own", *part)
         qa.terms["own"].append(jnp.concatenate([qa_first, qa_second], 0))
         qb.pass_on("own", a)
         qb.cross(b)
         r2.pass_on("own", c)
-        hidden_2 = h2.back(d, 3)
+        packed = ring.rows_step(packed, 1)
         half = own_images // 2
         tokens_a, sums_a = first_backward(tokens2, d_middle, row(first_gain), d_projs, attend, 0, half)
-        tokens_a, d_projs, a, b, c, hidden_2 = join(
-            tokens_a, d_projs, qa.send("own"), qb.send("own"), r2.value("own"), hidden_2
+        tokens_a, d_projs, a, b, c, packed = join(
+            tokens_a, d_projs, qa.send("own"), qb.send("own"), pair_up(h2.value("own"), r2.value("own")), packed
         )
         qa.pass_on("own", a)
         qb.pass_on("own", b)
-        return_2 = r2.back(c, 3)
-        hidden_2 = h2.back(hidden_2, 2)
+        units_2 = ring.spread(c)
+        packed = ring.rows_step(packed, 2)
         tokens_b, sums_b = first_backward(
             tokens2, d_middle, row(first_gain), d_projs, attend, half, own_images - half
         )
-        tokens_b, a, b, hidden_2, return_2 = join(tokens_b, qa.send("own"), qb.send("own"), hidden_2, return_2)
+        tokens_b, sums_b, a, b, packed = join(tokens_b, sums_b, qa.send("own"), qb.send("own"), packed)
         qa.pass_on("own", a)
         qb.pass_on("own", b)
-        hidden_2 = h2.back(hidden_2, 1)
-        return_2 = r2.back(return_2, 2)
-        a, b, hidden_2, return_2 = join(qa.send("own"), qb.value("own"), hidden_2, return_2)
+        packed = ring.rows_step(packed, 3)
+        a, packed, strips_a, strips_b, d_time, tokens_a, units_1 = join(
+            qa.send("own"), packed, attended_own[2], attended_other[2], d_time, tokens_a, units_1
+        )
         qa.pass_on("own", a)
-        attend_b = qb.gather(b)
-        hidden_2 = h2.back(hidden_2, 0)
-        return_2 = r2.back(return_2, 1)
-        a, hidden_2, return_2 = join(qa.value("own"), hidden_2, return_2)
-        attend_a = qa.back(a, 3)
-        return_2 = r2.back(return_2, 0)
-        hidden_grad = jnp.concatenate([g.reshape(dim, -1) for g in (hidden_1, hidden_2)], 1) * inv_total
-        attend_a, hidden_grad, return_2 = join(attend_a, hidden_grad, return_2)
-        attend_a = qa.back(attend_a, 2)
-        return_grad = jnp.concatenate([g.reshape(-1, dim) for g in (return_1, return_2)], 0) * inv_total
-        attend_a, return_grad = join(attend_a, return_grad)
-        attend_a = qa.back(qa.back(attend_a, 1), 0)
+        d_time_vec = jnp.einsum("sce,ced->sd", d_time, time_weight.transpose(0, 2, 1), precision=HIGH)
+        time_table_part = jnp.dot(onehot.T, d_time_vec, precision=HIGHEST)
+        table_full = absolute(table_gradient(strips_a), table_gradient(strips_b))
+        bias_own = jnp.concatenate([own_1[2][0], own_2[2][0]])
+        hidden_bias_full = absolute(bias_own, jnp.concatenate([other_1[2][0], other_2[2][0]]))
+        first_sums = sums_a + sums_b
+        small = [
+            first_sums[0], first_sums[1], time_table_part, second_sums[2], second_sums[0], second_sums[1],
+            second_sums[3], table_full, hidden_bias_full,
+        ]
+        flat = jnp.concatenate([v.reshape(-1) for v in small]) * inv_total
+        flat = jnp.pad(flat, (0, -flat.shape[0] % 1024)).reshape(-1, 128)
+        last = jnp.stack([qa.value("own"), qb.value("own")]).reshape(1, -1, dim)
+        last, flat, packed, units_1, units_2, tokens_a = join(last, flat, packed, units_1, units_2, tokens_a)
+        attend_all = ring.spread(last).reshape(16, 2, -1, dim)
+        flat = ring.all_sum(flat)
+        time_weight_grad = time_gradient(packed)
         tokens_grad = jnp.concatenate([tokens_a, tokens_b], 0)
-        first_sums = sums_a + sums_b
-        attend_a = attend_a.reshape(2, width, dim)
-        attend_b = attend_b.reshape(2, width, dim)
-        attend_weight_grad = (jnp.concatenate([attend_a, attend_b[:1]], 0) * inv_total).transpose(0, 2, 1)
-        output_weight_grad = attend_b[1] * inv_total
-
-        def absolute(own, other):
-            flag = rank == 0
-            return jnp.concatenate([jnp.where(flag, own, other), jnp.where(flag, other, own)], 0)
-
-        table_full = absolute(table_gradient(attended_own[2]), table_gradient(attended_other[2]))
-        bias_own = jnp.concatenate([own_1[2][:, 0], own_2[2][:, 0]])
-        hidden_bias_full = absolute(bias_own, jnp.concatenate([other_1[2][:, 0], other_2[2][:, 0]]))
-        d_time_got = ring.across(attended_other[3].reshape(own_images, 3, width))
-        d_time = absolute(attended_own[3].reshape(own_images, 3, width), d_time_got)
-        gather_rows = ring.all_rows
-        all_sum = ring.all_sum
+
+        def units_of(index):
+            found = [
+                g.reshape(16, 2, -1, PIECE, dim)[:, index].transpose(1, 0, 2, 3).reshape(-1, dim)
+                for g in (units_1, units_2)
+            ]
+            return jnp.concatenate(found, 0) * inv_total
+
+        hidden_grad = units_of(0).T
+        return_grad = units_of(1)
+        attend_all = attend_all.transpose(1, 0, 2, 3).reshape(4, width, dim) * inv_total
+        attend_weight_grad = attend_all[:3].transpose(0, 2, 1)
+        output_weight_grad = attend_all[3]
     else:
         attend = [lax.all_gather(attend_weight, "mp", axis=2, tiled=True).transpose(0, 2, 1).reshape(-1, dim)]
         output = [lax.all_gather(output_weight, "mp", axis=0, tiled=True)]
@@ -929,7 +930,7 @@
         middle, *forms = output_forward(
             live, tokens2, cotangent2, [all_of[3]], output, row(output_bias), *norm_second
         )
-        fed = feed(False, core, forms, hidden_full, column(bias_full), return_full, 0, hidden_full.shape[1] // BLOCK)
+        fed = feed(False, core, forms, hidden_full, row(bias_full), return_full, 0, hidden_full.shape[1] // BLOCK)
         result, d_middle, second_sums, d_mixed = middle_backward(
             live, middle, cotangent2, row(second_gain), row(return_bias), [fed[0]], [fed[1]], output
         )
@@ -945,38 +946,26 @@
         def settle(value, axis):
             return lax.psum(lax.psum_scatter(value * inv_total, "mp", scatter_dimension=axis, tiled=True), "dp")
 
-        hidden_grad = settle(fed[3], 1)
+        hidden_grad = settle(fed[3], 0).T
         return_grad = settle(fed[4], 0)
         attend_weight_grad = settle(attend_full.reshape(3, -1, dim), 1).transpose(0, 2, 1)
         output_weight_grad = settle(output_full, 0)
         table_full = table_gradient(attended[2])
-        hidden_bias_full = fed[2][:, 0]
+        hidden_bias_full = fed[2][0]
         d_time = lax.all_gather(attended[3].reshape(own_images, 3, -1), "mp", axis=0, tiled=True)
         d_time = lax.dynamic_slice_in_dim(d_time, rank * width, width, 2)
 
-        def gather_rows(value):
-            return lax.all_gather(value, "dp", axis=0, tiled=True)
-
-        def all_sum(value):
-            return lax.psum(value, ("dp", "mp"))
-
-    packed = jnp.concatenate([d_time.reshape(images, -1), bucket.astype(jnp.float32)[:, None]], 1)
-    packed = gather_rows(packed)
-    d_time_all = packed[:, :-1].reshape(-1, 3, width)
-    bucket_all = packed[:, -1].astype(jnp.int32)
-    onehot_all = (bucket_all[:, None] == jnp.arange(buckets)[None, :]).astype(jnp.float32)
-    time_all = jnp.dot(onehot_all, time_table, precision=HIGHEST)
-    time_weight_grad = jnp.einsum("sce,sd->ced", d_time_all * inv_total, time_all, precision=HIGH).transpose(0, 2, 1)
-    d_time_vec = jnp.einsum("sce,ced->sd", d_time, time_weight.transpose(0, 2, 1), precision=HIGH)
-    time_table_part = jnp.dot(onehot.T, d_time_vec, precision=HIGHEST)
-
-    small = [
-        first_sums[0], first_sums[1], time_table_part, second_sums[2], second_sums[0], second_sums[1],
-        second_sums[3], table_full, hidden_bias_full,
-    ]
-    flat = jnp.concatenate([s.reshape(-1) for s in small]) * inv_total
-    size = flat.shape[0]
-    flat = all_sum(jnp.pad(flat, (0, -size % 1024)).reshape(-1, 128)).reshape(-1)[:size]
+        packed = jnp.concatenate([d_time.reshape(images, -1), bucket.astype(jnp.float32)[:, None]], 1)
+        time_weight_grad = time_gradient(lax.all_gather(packed, "dp", axis=0, tiled=True))
+        d_time_vec = jnp.einsum("sce,ced->sd", d_time, time_weight.transpose(0, 2, 1), precision=HIGH)
+        time_table_part = jnp.dot(onehot.T, d_time_vec, precision=HIGHEST)
+        small = [
+            first_sums[0], first_sums[1], time_table_part, second_sums[2], second_sums[0], second_sums[1],
+            second_sums[3], table_full, hidden_bias_full,
+        ]
+        flat = lax.psum(jnp.concatenate([v.reshape(-1) for v in small]) * inv_total, ("dp", "mp"))
+
+    flat = flat.reshape(-1)
     sums = []
     start = 0
     for s in small:

time: 1320 us -> 1130 us (0.86)
  waiting for transfers between devices: 344 us -> 202 us
  Pallas kernels: 603 us -> 559 us
  other arithmetic: 165 us -> 137 us
  local copies, waits for them, and re-layouts: 107 us -> 127 us
    ppermute x19, waiting for transfers between devices: 184 us -> 37.1 us  [across(): return lax.ppermute(value, 'mp', [(0, 1), (1, 0)])]
    pallas_call x4, Pallas kernels: 311 us -> 269 us  [feed(): pl.pallas_call(functools.partial(feed_kernel, split), grid=(blocks,), in_...]
    transpose x0 -> x7, local copies, waits for them, and re-layouts: none -> 33.5 us  [the longest x6 26.5 us: units_of(): g.reshape(16, 2, -1, PIECE, dim)[:, index].transpose(1, 0, 2, 3)]
    concatenate x13 -> x1, local copies, waits for them, and re-layouts: 25.1 us -> 1.72 us  [body(): flat = jnp.concatenate([v.reshape(-1) for v in small]) * inv_total]
    select_n x19 -> x8, other arithmetic: 26.6 us -> 9.24 us  [ordered(): jnp.where(flag, mine, theirs)]
    add x12 -> x7, other arithmetic: 30.2 us -> 19.4 us  [value(): out = out + term]
    ppermute x57 -> x45, starting transfers between devices: 44.3 us -> 35.4 us  [along(): return lax.ppermute(value, 'dp', [(i, i ^ 1 << bit) for i in range(16)])]
    ppermute x57 -> x45, waiting for transfers between devices: 159 us -> 165 us  [along(): return lax.ppermute(value, 'dp', [(i, i ^ 1 << bit) for i in range(16)])]
  transfers between devices with their start and end apart: 82 -> 70, of which waited for: 22 -> 16; matrix products, arithmetic and copies ran while one was open for 20% -> 23% of each run, Pallas kernels for 46% -> 50%
where the time goes in v2:
time: 1130 us; the launch traced here: 1120 us
  Pallas kernels  559 us (49%)
  waiting for transfers between devices  202 us (18%)
  other arithmetic  137 us (12%)
  local copies, waits for them, and re-layouts  127 us (11%)
  starting transfers between devices  57.6 us (5%)
  matrix products  22.2 us (2%)
  between operations  16.3 us (1%)
    pallas_call x4, Pallas kernels, feed(): pl.pallas_call(functools.partial(feed_kernel, split), grid=(blocks,), in_...  269 us
    ppermute x45, waiting for transfers between devices, along(): return lax.ppermute(value, 'dp', [(i, i ^ 1 << bit) for i in range(16)])  165 us
    pallas_call x2, Pallas kernels, attend_forward(): pl.pallas_call(functools.partial(attend_forward_kernel, heads), grid=(ima...  66.1 us
    pallas_call x4, Pallas kernels, attend_weights(): pl.pallas_call(functools.partial(attend_weights_kernel, split, steps), gr...  63.3 us
    pallas_call x2, Pallas kernels, attend_backward(): pl.pallas_call(functools.partial(attend_backward_kernel, heads), grid=(im...  61.1 us
    pallas_call x2, Pallas kernels, first_backward(): pl.pallas_call(functools.partial(first_kernel, parts), grid=(count // PAT...  50.5 us
    add x18, other arithmetic, send(): out = out + pick(cut, 1 - bit, axis + 1)  39.3 us
    ppermute x19, waiting for transfers between devices, across(): return lax.ppermute(value, 'mp', [(0, 1), (1, 0)])  37.1 us
  transfers between devices with their start and end apart: 70, of which 16 were waited for; matrix products, arithmetic and copies ran while one was open for 23% of the time, Pallas kernels for 50%

profile of v2, /device:TPU:0, one launch (start us, length us, event | category | flops | bytes accessed | tf_op | source)
XLA Modules:
  0.0 1121.5 jit_solution(2762532350331775316)
XLA Ops:
  15.9 6.8 fusion.3
  37.3 3.3 constant_dynamic-slice_fusion.31
  42.5 33.1 %shard_map.297 = (f32[1024,576]{1,0:T(8,128)}, f32[1024,576]{1,0:T(8,128)}, f32[1024,576]{1,0:T(8,128)}, f32[1024,576]{1,0:T(8,128)}, f32[576,1024]{1,0:T(8,128)...) custom-call(f32[1024,1152]{1,0:T(8,128)} %bitcast.439, f32[1,1152]{1,0:T(1,128)} %reshape.1162.gain_ref.refs_2_, ...), custom_call_target="tpu_custom_call" | custom-call | flops 18673040 | bytes 22118 | tf_op jit(solution)/shard_map/pallas_call | solution.py:142
  75.6 22.3 %collective-permute-done.6 = f32[72,1024]{1,0:T(8,128)S(1)} collective-permute-done((f32[72,1024]{1,0:T(8,128)S(1)}, f32[72,1024]{1,0:T(8,128)S(1)}, u32[]{:S(2)}, u32[]{:S(2)}) %collective-permute-start.6) | collective-permute-done | bytes 294944 | tf_op jit(solution)/shard_map/ppermute | solution.py:593
  98.0 6.5 collective-permute-done.5
  111.9 6.5 pad_maximum_fusion.weight_ref.refs_6_
  118.4 33.1 %shard_map.298 = (f32[1024,576]{1,0:T(8,128)}, f32[1024,576]{1,0:T(8,128)}, f32[1024,576]{1,0:T(8,128)}, f32[1024,576]{1,0:T(8,128)}, f32[576,1024]{1,0:T(8,128)...) custom-call(f32[1024,1152]{1,0:T(8,128)} %bitcast.440, f32[1,1152]{1,0:T(1,128)} %reshape.1162.gain_ref.refs_2_, ...), custom_call_target="tpu_custom_call" | custom-call | flops 18673040 | bytes 22118 | tf_op jit(solution)/shard_map/pallas_call | solution.py:142
  151.5 7.3 collective-permute-done.9
  171.1 21.0 %shard_map.299 = (f32[1024,1152]{1,0:T(8,128)}, bf16[1024,2304]{1,0:T(8,128)(2,1)}, bf16[1024,2304]{1,0:T(8,128)(2,1)}) custom-call(f32[4]{0:T(128)S(1)} %compare_convert_fusion.refs_0_, f32[1024,1152]{1,0:T(8,128)} %bitcast.441, f32[1024,1152]{1,0:T(8,128)} %bitcast.456, f32[1024,576]{1,0:T(8,128)S(1)} %copy-done.1, f32[1024,576]{1,0:T(8,128)S(1)} %copy-done.2, ...), custom_call_target="tpu_custom_call" | custom-call | flops 8153726 | bytes 28901 | tf_op jit(solution)/shard_map/pallas_call | solution.py:188
  198.4 60.6 %shard_map.300 = (f32[1024,1152]{1,0:T(8,128)}, f32[1024,1152]{1,0:T(8,128)}, f32[1,1024]{1,0:T(1,128)}, f32[4,8,16,1152]{3,2,1,0:T(8,128)}, f32[4,8,16,1152]{3,...) custom-call(s32[1]{0:T(128)} %bitcast.14.core_ref, ...), custom_call_target="tpu_custom_call" | custom-call | flops 43486544 | bytes 42467 | tf_op jit(solution)/shard_map/pallas_call | solution.py:305
  259.1 5.6 collective-permute-done.13
  270.9 73.5 %shard_map.301 = (f32[1024,1152]{1,0:T(8,128)}, f32[1024,1152]{1,0:T(8,128)}, f32[1,1280]{1,0:T(1,128)}, f32[5,8,16,1152]{3,2,1,0:T(8,128)}, f32[5,8,16,1152]{3,...) custom-call(s32[1]{0:T(128)} %bitcast.14.core_ref, ...), custom_call_target="tpu_custom_call" | custom-call | flops 54358180 | bytes 47185 | tf_op jit(solution)/shard_map/pallas_call | solution.py:305
  354.7 61.0 %shard_map.302 = (f32[1024,1152]{1,0:T(8,128)}, f32[1024,1152]{1,0:T(8,128)}, f32[1,1024]{1,0:T(1,128)}, f32[4,8,16,1152]{3,2,1,0:T(8,128)}, f32[4,8,16,1152]{3,...) custom-call(s32[1]{0:T(128)} %bitcast.14.core_ref, ...), custom_call_target="tpu_custom_call" | custom-call | flops 43486544 | bytes 42467 | tf_op jit(solution)/shard_map/pallas_call | solution.py:305
  417.1 4.9 add.1246
  426.6 73.6 %shard_map.303 = (f32[1024,1152]{1,0:T(8,128)}, f32[1024,1152]{1,0:T(8,128)}, f32[1,1280]{1,0:T(1,128)}, f32[5,8,16,1152]{3,2,1,0:T(8,128)}, f32[5,8,16,1152]{3,...) custom-call(s32[1]{0:T(128)} %bitcast.14.core_ref, ...), custom_call_target="tpu_custom_call" | custom-call | flops 54358180 | bytes 47185 | tf_op jit(solution)/shard_map/pallas_call | solution.py:305
  509.9 3.4 bitcast_add_fusion.3
  515.9 4.3 constant_dynamic-slice_fusion.19
  520.2 28.3 %shard_map.304 = (f32[1024,1152]{1,0:T(8,128)}, f32[1024,1152]{1,0:T(8,128)}, f32[8,1152]{1,0:T(8,128)}, f32[1024,576]{1,0:T(8,128)}, f32[1024,576]{1,0:T(8,128)}) custom-call(f32[4]{0:T(128)} %copy-done.4, f32[1024,1152]{1,0:T(8,128)} %get-tuple-element.335.refs_1_, f32[1024,1152]{1,0:T(8,128)} %bitcast.457, f32[1,1152]{1,0:T(1,128)} %copy-done.3, ...), custom_call_target="tpu_custom_call" | custom-call | flops 8153726 | bytes 47775 | tf_op jit(solution)/shard_map/pallas_call | solution.py:366
  552.8 30.7 %shard_map.305 = (f32[1024,1728]{1,0:T(8,128)}, f32[1728,1024]{1,0:T(8,128)}, f32[8,16,512]{2,1,0:T(8,128)}, f32[4,1,1728]{2,1,0:T(1,128)}) custom-call(f32[1024,576]{1,0:T(8,128)} %get-tuple-element.348.query_ref, f32[1024,576]{1,0:T(8,128)} %get-tuple-element.349.keys_ref, f32[1024,576]{1,0:T(8,128)} %get-tuple-element.350.values_ref, ...), custom_call_target="tpu_custom_call" | custom-call | flops 16106127 | bytes 21233 | tf_op jit(solution)/shard_map/pallas_call | solution.py:437
  591.0 14.6 %shard_map.306 = (f32[8,72,1152]{2,1,0:T(8,128)}, f32[8,72,1152]{2,1,0:T(8,128)}) custom-call(s32[1]{0:T(128)} %bitcast.14.core_ref, f32[1728,1024]{1,0:T(8,128)} %get-tuple-element.370.refs_0_, f32[1024,1152]{1,0:T(8,128)} %get-tuple-element.406.refs_1_.refs_2_), custom_call_target="tpu_custom_call" | custom-call | flops 8153726 | bytes 19464 | tf_op jit(solution)/shard_map/pallas_call | solution.py:503
  613.9 4.1 constant_dynamic-slice_fusion.3
  620.7 16.7 %shard_map.307 = (f32[8,72,1152]{2,1,0:T(8,128)}, f32[8,72,1152]{2,1,0:T(8,128)}) custom-call(s32[1]{0:T(128)} %bitcast.14.core_ref, f32[1728,1024]{1,0:T(8,128)} %get-tuple-element.370.refs_0_, f32[576,1024]{1,0:T(8,128)} %get-tuple-element.371.refs_1_, f32[1024,1152]{1,0:T(8,128)} %get-tuple-element.406.refs_1_.refs_2_, ...), custom_call_target="tpu_custom_call" | custom-call | flops 8153726 | bytes 19464 | tf_op jit(solution)/shard_map/pallas_call | solution.py:503
  657.4 30.3 %shard_map.308 = (f32[1024,1728]{1,0:T(8,128)}, f32[1728,1024]{1,0:T(8,128)}, f32[8,16,512]{2,1,0:T(8,128)}, f32[4,1,1728]{2,1,0:T(1,128)}) custom-call(f32[1024,576]{1,0:T(8,128)} %get-tuple-element.345.query_ref, f32[1024,576]{1,0:T(8,128)} %get-tuple-element.346.keys_ref, f32[1024,576]{1,0:T(8,128)} %get-tuple-element.347.values_ref, ...), custom_call_target="tpu_custom_call" | custom-call | flops 16106127 | bytes 21233 | tf_op jit(solution)/shard_map/pallas_call | solution.py:437
  699.7 17.3 %shard_map.309 = (f32[8,72,1152]{2,1,0:T(8,128)}, f32[8,72,1152]{2,1,0:T(8,128)}) custom-call(s32[1]{0:T(128)} %bitcast.14.core_ref, f32[1728,1024]{1,0:T(8,128)} %get-tuple-element.401.refs_0_, f32[576,1024]{1,0:T(8,128)} %get-tuple-element.402.refs_1_, f32[1024,1152]{1,0:T(8,128)} %get-tuple-element.406.refs_1_.refs_2_, ...), custom_call_target="tpu_custom_call" | custom-call | flops 8153726 | bytes 19464 | tf_op jit(solution)/shard_map/pallas_call | solution.py:503
  719.6 14.6 %shard_map.310 = (f32[8,72,1152]{2,1,0:T(8,128)}, f32[8,72,1152]{2,1,0:T(8,128)}) custom-call(s32[1]{0:T(128)} %bitcast.14.core_ref, f32[1728,1024]{1,0:T(8,128)} %get-tuple-element.401.refs_0_, f32[1024,1152]{1,0:T(8,128)} %get-tuple-element.406.refs_1_.refs_2_), custom_call_target="tpu_custom_call" | custom-call | flops 8153726 | bytes 19464 | tf_op jit(solution)/shard_map/pallas_call | solution.py:503
  735.9 19.7 %collective-permute-done.43 = f32[5,2,16,1152]{3,2,0,1:T(8,128)} collective-permute-done((f32[5,2,16,1152]{3,2,0,1:T(8,128)}, f32[5,2,16,1152]{3,2,0,1:T(8,128)}, u32[]{:S(2)}, u32[]{:S(2)}) %collective-permute-start.43) | collective-permute-done | bytes 737312 | tf_op jit(solution)/shard_map/ppermute | solution.py:596
  761.1 3.8 constant_dynamic-slice_fusion.28
  775.5 25.2 %shard_map.311 = (f32[512,1152]{1,0:T(8,128)}, f32[8,1152]{1,0:T(8,128)}) custom-call(f32[1024,1152]{1,0:T(8,128)} %bitcast.442, f32[1024,1152]{1,0:T(8,128)} %get-tuple-element.376.refs_3_.refs_1_, f32[1,1152]{1,0:T(1,128)} %reshape.1162.gain_ref.refs_2_, f32[1024,1728]{1,0:T(8,128)} %get-tuple-element.431.refs_3_, ...), custom_call_target="tpu_custom_call" | custom-call | flops 12230590 | bytes 30081 | tf_op jit(solution)/shard_map/pallas_call | solution.py:543
  800.8 4.6 collective-permute-done.50
  821.4 25.3 %shard_map.312 = (f32[512,1152]{1,0:T(8,128)}, f32[8,1152]{1,0:T(8,128)}) custom-call(f32[1024,1152]{1,0:T(8,128)} %bitcast.443, f32[1024,1152]{1,0:T(8,128)} %get-tuple-element.376.refs_3_.refs_1_, f32[1,1152]{1,0:T(1,128)} %reshape.1162.gain_ref.refs_2_, f32[1024,1728]{1,0:T(8,128)} %get-tuple-element.431.refs_3_, ...), custom_call_target="tpu_custom_call" | custom-call | flops 12230590 | bytes 30081 | tf_op jit(solution)/shard_map/pallas_call | solution.py:543
  850.2 13.2 %collective-permute-done.53 = f32[2,72,1152]{2,1,0:T(8,128)} collective-permute-done((f32[2,72,1152]{2,1,0:T(8,128)}, f32[2,72,1152]{2,1,0:T(8,128)}, u32[]{:S(2)}, u32[]{:S(2)}) %collective-permute-start.53) | collective-permute-done | bytes 663584 | tf_op jit(solution)/shard_map/ppermute | solution.py:596
  871.7 38.8 %collective-permute-done.58 = f32[1,72,1152]{2,1,0:T(8,128)} collective-permute-done((f32[1,72,1152]{2,1,0:T(8,128)}, f32[1,72,1152]{2,1,0:T(8,128)}, u32[]{:S(2)}, u32[]{:S(2)}) %collective-permute-start.58) | collective-permute-done | bytes 331808 | tf_op jit(solution)/shard_map/ppermute | solution.py:596
  912.8 27.4 %collective-permute-done.56 = f32[64,1729]{1,0:T(8,128)} collective-permute-done((f32[64,1729]{1,0:T(8,128)}, f32[64,1729]{1,0:T(8,128)}, u32[]{:S(2)}, u32[]{:S(2)}) %collective-permute-start.56) | collective-permute-done | bytes 442656 | tf_op jit(solution)/shard_map/ppermute | solution.py:596
  945.4 5.5 fusion.5
  963.9 5.6 collective-permute-done.57
  972.0 7.0 slice_bitcast_fusion.3
  981.7 7.7 slice_bitcast_fusion.1
  992.5 8.9 maximum_multiply_fusion.1
  1012.1 7.3 fusion
  1019.3 12.8 %copy.568 = f32[1152,2304]{1,0:T(8,128)} copy(f32[1152,2304]{0,1:T(8,128)} %fusion) | data formatting | bytes 21233664
  1035.7 13.9 %collective-permute-done.61 = f32[792,128]{1,0:T(8,128)S(1)} collective-permute-done((f32[792,128]{1,0:T(8,128)S(1)}, f32[792,128]{1,0:T(8,128)S(1)}, u32[]{:S(2)}, u32[]{:S(2)}) %collective-permute-start.61) | collective-permute-done | bytes 405536 | tf_op jit(solution)/shard_map/ppermute | solution.py:596
  1051.2 5.4 convolution_bitcast_fusion
  1056.6 14.5 %collective-permute-done.62 = f32[792,128]{1,0:T(8,128)S(1)} collective-permute-done((f32[792,128]{1,0:T(8,128)S(1)}, f32[792,128]{1,0:T(8,128)S(1)}, u32[]{:S(2)}, u32[]{:S(2)}) %collective-permute-start.62) | collective-permute-done | bytes 405536 | tf_op jit(solution)/shard_map/ppermute | solution.py:596
  1075.1 16.7 %collective-permute-done.63 = f32[792,128]{1,0:T(8,128)S(1)} collective-permute-done((f32[792,128]{1,0:T(8,128)S(1)}, f32[792,128]{1,0:T(8,128)S(1)}, u32[]{:S(2)}, u32[]{:S(2)}) %collective-permute-start.63) | collective-permute-done | bytes 405536 | tf_op jit(solution)/shard_map/ppermute | solution.py:596
  1094.7 4.7 broadcast_multiply_fusion
  1099.4 4.6 copy.563
  1104.0 3.4 slice_bitcast_fusion.5
  1107.5 7.0 slice_bitcast_fusion
  (425 shorter events, 238.5 us)
Async XLA Ops:
  7.2 104.7 %all-gather.7.cloned.1.call-start = ((), (), s32[]{:S(2)}) async-start(), calls=%async_computation | async-start | bytes 5640192 | tf_op jit(solution)/shard_map/all_gather | solution.py:611
  30.3 168.1 %all-gather.9.cloned.1.call-start = ((), (), s32[]{:S(2)}) async-start(), calls=%async_computation.1 | async-start | bytes 5013504 | tf_op jit(solution)/shard_map/all_gather | solution.py:611
  30.8 73.6 %collective-permute-start.3 = (f32[288,1152]{1,0:T(8,128)}, f32[288,1152]{1,0:T(8,128)}, u32[]{:S(2)}, u32[]{:S(2)}) collective-permute-start(f32[288,1152]{1,0:T(8,128)} %get-tuple-element.250), channel_id=1, source_target_pairs={{0,1},{1,0},{2,3},{3,2},{4,5},{5,4},{6,7},{7,6},{8,9},{9,8},{10,11... | collective-permute-start | bytes 3981320 | tf_op jit(solution)/shard_map/ppermute | solution.py:593
  31.0 73.5 %collective-permute-start.4 = (f32[288,1152]{1,0:T(8,128)}, f32[288,1152]{1,0:T(8,128)}, u32[]{:S(2)}, u32[]{:S(2)}) collective-permute-start(f32[288,1152]{1,0:T(8,128)} %get-tuple-element.251), channel_id=1, source_target_pairs={{0,1},{1,0},{2,3},{3,2},{4,5},{5,4},{6,7},{7,6},{8,9},{9,8},{10,11... | collective-permute-start | bytes 3981320 | tf_op jit(solution)/shard_map/ppermute | solution.py:593
  33.9 64.0 %collective-permute-start.6 = (f32[72,1024]{1,0:T(8,128)S(1)}, f32[72,1024]{1,0:T(8,128)S(1)}, u32[]{:S(2)}, u32[]{:S(2)}) collective-permute-start(f32[72,1024]{1,0:T(8,128)S(1)} %constant_dynamic-slice_fusion.30), channel_id=1, source_target_pairs={{0,1},{1,0},{2,3},{3,2},{4,5},{5,4},{6,7},{7,6},{8,9},{9,8},{10,11... | collective-permute-start | bytes 884744 | tf_op jit(solution)/shard_map/ppermute | solution.py:593
  35.1 69.4 %collective-permute-start.7 = (f32[72,1280]{1,0:T(8,128)S(1)}, f32[72,1280]{1,0:T(8,128)S(1)}, u32[]{:S(2)}, u32[]{:S(2)}) collective-permute-start(f32[72,1280]{1,0:T(8,128)S(1)} %constant_dynamic-slice_fusion.37), channel_id=1, source_target_pairs={{0,1},{1,0},{2,3},{3,2},{4,5},{5,4},{6,7},{7,6},{8,9},{9,8},{10,11... | collective-permute-start | bytes 1105928 | tf_op jit(solution)/shard_map/ppermute | solution.py:593
  37.1 67.3 %collective-permute-start.5 = (f32[4,3,576]{2,0,1:T(4,128)S(1)}, f32[4,3,576]{2,0,1:T(4,128)S(1)}, u32[]{:S(2)}, u32[]{:S(2)}) collective-permute-start(f32[4,3,576]{2,0,1:T(4,128)S(1)} %get-tuple-element.626), channel_id=1, source_target_pairs={{0,1},{1,0},{2,3},{3,2},{4,5},{5,4},{6,7},{7,6},{8,9},{9,8},{10,11... | collective-permute-start | bytes 82952 | tf_op jit(solution)/shard_map/ppermute | solution.py:593
  104.5 166.4 %all-gather.11.cloned.1.call-start = ((), (), s32[]{:S(2)}) async-start(), calls=%async_computation.2 | async-start | bytes 6266880 | tf_op jit(solution)/shard_map/all_gather | solution.py:611
  104.8 54.0 %collective-permute-start.9 = (f32[512,1152]{1,0:T(8,128)}, f32[512,1152]{1,0:T(8,128)}, u32[]{:S(2)}, u32[]{:S(2)}) collective-permute-start(f32[512,1152]{1,0:T(8,128)} %constant_dynamic-slice_fusion.31), channel_id=1, source_target_pairs={{0,1},{1,0},{2,3},{3,2},{4,5},{5,4},{6,7},{7,6},{8,9},{9,8},{10,11... | collective-permute-start | bytes 7077896 | tf_op jit(solution)/shard_map/ppermute | solution.py:593
  162.7 782.7 %all-gather.13.cloned.1.call-start = ((), (), s32[]{:S(2)}) async-start(), calls=%async_computation.3 | async-start | bytes 10027008 | tf_op jit(solution)/shard_map/all_gather | solution.py:611
  192.1 66.9 %collective-permute-start.12 = (f32[640,1152]{1,0:T(8,128)S(1)}, f32[640,1152]{1,0:T(8,128)}, u32[]{:S(2)}, u32[]{:S(2)}) collective-permute-start(f32[640,1152]{1,0:T(8,128)S(1)} %constant_dynamic-slice_fusion.29), channel_id=1, source_target_pairs={{0,1},{1,0},{2,3},{3,2},{4,5},{5,4},{6,7},{7,6},{8,9},{9,8},{10,11... | collective-permute-start | bytes 8847368 | tf_op jit(solution)/shard_map/ppermute | solution.py:593
  269.8 74.6 %collective-permute-start.15 = (f32[4,8,16,1152]{3,2,1,0:T(8,128)}, f32[4,8,16,1152]{3,2,1,0:T(8,128)}, u32[]{:S(2)}, u32[]{:S(2)}) collective-permute-start(f32[4,8,16,1152]{3,2,1,0:T(8,128)} %get-tuple-element.304), channel_id=1, source_target_pairs={{0,2},{2,0},{4,6},{6,4},{8,10},{10,8},{12,14},{14,12},{16,18},{18,... | collective-permute-start | bytes 7077896 | tf_op jit(solution)/shard_map/ppermute | solution.py:596
  270.0 77.4 %collective-permute-start.14 = (f32[4,8,16,1152]{3,2,1,0:T(8,128)}, f32[4,8,16,1152]{3,2,1,0:T(8,128)S(1)}, u32[]{:S(2)}, u32[]{:S(2)}) collective-permute-start(f32[4,8,16,1152]{3,2,1,0:T(8,128)} %get-tuple-element.302), channel_id=1, source_target_pairs={{0,2},{2,0},{4,6},{6,4},{8,10},{10,8},{12,14},{14,12},{16,18},{18,... | collective-permute-start | bytes 7077896 | tf_op jit(solution)/shard_map/ppermute | solution.py:596
  349.1 68.0 %collective-permute-start.16 = (f32[5,8,16,1152]{3,2,1,0:T(8,128)}, f32[5,8,16,1152]{3,2,1,0:T(8,128)}, u32[]{:S(2)}, u32[]{:S(2)}) collective-permute-start(f32[5,8,16,1152]{3,2,1,0:T(8,128)} %get-tuple-element.315), channel_id=1, source_target_pairs={{0,2},{2,0},{4,6},{6,4},{8,10},{10,8},{12,14},{14,12},{16,18},{18,... | collective-permute-start | bytes 8847368 | tf_op jit(solution)/shard_map/ppermute | solution.py:596
  349.3 72.7 %collective-permute-start.17 = (f32[5,8,16,1152]{3,2,1,0:T(8,128)}, f32[5,8,16,1152]{3,2,1,0:T(8,128)}, u32[]{:S(2)}, u32[]{:S(2)}) collective-permute-start(f32[5,8,16,1152]{3,2,1,0:T(8,128)} %get-tuple-element.317), channel_id=1, source_target_pairs={{0,2},{2,0},{4,6},{6,4},{8,10},{10,8},{12,14},{14,12},{16,18},{18,... | collective-permute-start | bytes 8847368 | tf_op jit(solution)/shard_map/ppermute | solution.py:596
  349.6 75.1 %collective-permute-start.18 = (f32[4,8,16,1152]{3,2,1,0:T(8,128)}, f32[4,8,16,1152]{3,2,1,0:T(8,128)}, u32[]{:S(2)}, u32[]{:S(2)}) collective-permute-start(f32[4,8,16,1152]{3,2,1,0:T(8,128)} %add.1242), channel_id=1, source_target_pairs={{0,1},{1,0},{2,3},{3,2},{4,5},{5,4},{6,7},{7,6},{8,9},{9,8},{10,11... | collective-permute-start | bytes 7077896 | tf_op jit(solution)/shard_map/ppermute | solution.py:593
  351.2 73.5 %collective-permute-start.19 = (f32[4,4,16,1152]{3,2,1,0:T(8,128)}, f32[4,4,16,1152]{3,2,1,0:T(8,128)}, u32[]{:S(2)}, u32[]{:S(2)}) collective-permute-start(f32[4,4,16,1152]{3,2,1,0:T(8,128)} %fusion.13), channel_id=1, source_target_pairs={{0,4},{2,6},{4,0},{6,2},{8,12},{10,14},{12,8},{14,10},{16,20},{18,... | collective-permute-start | bytes 3538952 | tf_op jit(solution)/shard_map/ppermute | solution.py:596
  424.7 80.8 %collective-permute-start.21 = (f32[5,8,16,1152]{3,2,1,0:T(8,128)}, f32[5,8,16,1152]{3,2,1,0:T(8,128)}, u32[]{:S(2)}, u32[]{:S(2)}) collective-permute-start(f32[5,8,16,1152]{3,2,1,0:T(8,128)} %add.1246), channel_id=1, source_target_pairs={{0,1},{1,0},{2,3},{3,2},{4,5},{5,4},{6,7},{7,6},{8,9},{9,8},{10,11... | collective-permute-start | bytes 8847368 | tf_op jit(solution)/shard_map/ppermute | solution.py:593
  425.3 77.6 %collective-permute-start.20 = (f32[4,8,16,1152]{3,2,1,0:T(8,128)}, f32[4,8,16,1152]{3,2,1,0:T(8,128)}, u32[]{:S(2)}, u32[]{:S(2)}) collective-permute-start(f32[4,8,16,1152]{3,2,1,0:T(8,128)} %get-tuple-element.330), channel_id=1, source_target_pairs={{0,2},{2,0},{4,6},{6,4},{8,10},{10,8},{12,14},{14,12},{16,18},{18,... | collective-permute-start | bytes 7077896 | tf_op jit(solution)/shard_map/ppermute | solution.py:596
  425.3 90.6 %collective-permute-start.22 = (f32[4,8,16,1152]{3,2,1,0:T(8,128)}, f32[4,8,16,1152]{3,2,1,0:T(8,128)}, u32[]{:S(2)}, u32[]{:S(2)}) collective-permute-start(f32[4,8,16,1152]{3,2,1,0:T(8,128)} %get-tuple-element.353), channel_id=1, source_target_pairs={{0,2},{2,0},{4,6},{6,4},{8,10},{10,8},{12,14},{14,12},{16,18},{18,... | collective-permute-start | bytes 7077896 | tf_op jit(solution)/shard_map/ppermute | solution.py:596
  425.8 84.1 %collective-permute-start.23 = (f32[5,4,16,1152]{3,2,1,0:T(8,128)}, f32[5,4,16,1152]{3,2,1,0:T(8,128)}, u32[]{:S(2)}, u32[]{:S(2)}) collective-permute-start(f32[5,4,16,1152]{3,2,1,0:T(8,128)} %fusion.9), channel_id=1, source_target_pairs={{0,4},{2,6},{4,0},{6,2},{8,12},{10,14},{12,8},{14,10},{16,20},{18,... | collective-permute-start | bytes 4423688 | tf_op jit(solution)/shard_map/ppermute | solution.py:596
  505.5 82.3 %collective-permute-start.28 = (f32[5,8,16,1152]{3,2,1,0:T(8,128)}, f32[5,8,16,1152]{3,2,1,0:T(8,128)}, u32[]{:S(2)}, u32[]{:S(2)}) collective-permute-start(f32[5,8,16,1152]{3,2,1,0:T(8,128)} %get-tuple-element.367), channel_id=1, source_target_pairs={{0,2},{2,0},{4,6},{6,4},{8,10},{10,8},{12,14},{14,12},{16,18},{18,... | collective-permute-start | bytes 8847368 | tf_op jit(solution)/shard_map/ppermute | solution.py:596
  506.6 41.9 %collective-permute-start.24 = (f32[4,4,16,1152]{3,2,1,0:T(8,128)}, f32[4,4,16,1152]{3,2,1,0:T(8,128)}, u32[]{:S(2)}, u32[]{:S(2)}) collective-permute-start(f32[4,4,16,1152]{3,2,1,0:T(8,128)} %fusion.12), channel_id=1, source_target_pairs={{0,4},{2,6},{4,0},{6,2},{8,12},{10,14},{12,8},{14,10},{16,20},{18,... | collective-permute-start | bytes 3538952 | tf_op jit(solution)/shard_map/ppermute | solution.py:596
  508.5 40.1 %collective-permute-start.25 = (f32[4,4,16,1152]{3,2,1,0:T(8,128)}, f32[4,4,16,1152]{3,2,1,0:T(8,128)}, u32[]{:S(2)}, u32[]{:S(2)}) collective-permute-start(f32[4,4,16,1152]{3,2,1,0:T(8,128)} %add_add_fusion), channel_id=1, source_target_pairs={{0,1},{1,0},{2,3},{3,2},{4,5},{5,4},{6,7},{7,6},{8,9},{9,8},{10,11... | collective-permute-start | bytes 3538952 | tf_op jit(solution)/shard_map/ppermute | solution.py:593
  520.2 93.7 %collective-permute-start.32 = (f32[5,8,16,1152]{3,2,1,0:T(8,128)}, f32[5,8,16,1152]{3,2,1,0:T(8,128)}, u32[]{:S(2)}, u32[]{:S(2)}) collective-permute-start(f32[5,8,16,1152]{3,2,1,0:T(8,128)} %get-tuple-element.384), channel_id=1, source_target_pairs={{0,2},{2,0},{4,6},{6,4},{8,10},{10,8},{12,14},{14,12},{16,18},{18,... | collective-permute-start | bytes 8847368 | tf_op jit(solution)/shard_map/ppermute | solution.py:596
  550.6 40.4 %collective-permute-start.29 = (f32[5,4,16,1152]{3,2,1,0:T(8,128)}, f32[5,4,16,1152]{3,2,1,0:T(8,128)}, u32[]{:S(2)}, u32[]{:S(2)}) collective-permute-start(f32[5,4,16,1152]{3,2,1,0:T(8,128)} %bitcast_add_fusion.3), channel_id=1, source_target_pairs={{0,1},{1,0},{2,3},{3,2},{4,5},{5,4},{6,7},{7,6},{8,9},{9,8},{10,11... | collective-permute-start | bytes 4423688 | tf_op jit(solution)/shard_map/ppermute | solution.py:593
  605.7 39.2 %collective-permute-start.30 = (f32[8,72,1152]{2,1,0:T(8,128)}, f32[8,72,1152]{2,1,0:T(8,128)}, u32[]{:S(2)}, u32[]{:S(2)}) collective-permute-start(f32[8,72,1152]{2,1,0:T(8,128)} %get-tuple-element.381), channel_id=1, source_target_pairs={{0,2},{2,0},{4,6},{6,4},{8,10},{10,8},{12,14},{14,12},{16,18},{18,... | collective-permute-start | bytes 7962632 | tf_op jit(solution)/shard_map/ppermute | solution.py:596
  646.9 48.1 %collective-permute-start.35 = (f32[8,72,1152]{2,1,0:T(8,128)}, f32[8,72,1152]{2,1,0:T(8,128)}, u32[]{:S(2)}, u32[]{:S(2)}) collective-permute-start(f32[8,72,1152]{2,1,0:T(8,128)} %get-tuple-element.394), channel_id=1, source_target_pairs={{0,2},{2,0},{4,6},{6,4},{8,10},{10,8},{12,14},{14,12},{16,18},{18,... | collective-permute-start | bytes 7962632 | tf_op jit(solution)/shard_map/ppermute | solution.py:596
  649.5 38.2 %collective-permute-start.36 = (f32[4,1,16,1152]{3,2,0,1:T(8,128)S(1)}, f32[4,1,16,1152]{3,2,0,1:T(8,128)S(1)}, u32[]{:S(2)}, u32[]{:S(2)}) collective-permute-start(f32[4,1,16,1152]{3,2,0,1:T(8,128)S(1)} %fusion.47), channel_id=1, source_target_pairs={{0,16},{2,18},{4,20},{6,22},{8,24},{10,26},{12,28},{14,30},{16,0},... | collective-permute-start | bytes 884744 | tf_op jit(solution)/shard_map/ppermute | solution.py:596
  652.0 38.0 %collective-permute-start.38 = (f32[5,2,16,1152]{3,2,0,1:T(8,128)}, f32[5,2,16,1152]{3,2,0,1:T(8,128)}, u32[]{:S(2)}, u32[]{:S(2)}) collective-permute-start(f32[5,2,16,1152]{3,2,0,1:T(8,128)} %fusion.17), channel_id=1, source_target_pairs={{0,8},{2,10},{4,12},{6,14},{8,0},{10,2},{12,4},{14,6},{16,24},{18,... | collective-permute-start | bytes 2211848 | tf_op jit(solution)/shard_map/ppermute | solution.py:596
  652.5 39.7 %collective-permute-start.37 = (f32[5,4,16,1152]{3,2,1,0:T(8,128)}, f32[5,4,16,1152]{3,2,1,0:T(8,128)}, u32[]{:S(2)}, u32[]{:S(2)}) collective-permute-start(f32[5,4,16,1152]{3,2,1,0:T(8,128)} %get-tuple-element.397), channel_id=1, source_target_pairs={{0,4},{2,6},{4,0},{6,2},{8,12},{10,14},{12,8},{14,10},{16,20},{18,... | collective-permute-start | bytes 4423688 | tf_op jit(solution)/shard_map/ppermute | solution.py:596
  655.9 42.8 %collective-permute-start.39 = (f32[4,72,1152]{2,1,0:T(8,128)}, f32[4,72,1152]{2,1,0:T(8,128)}, u32[]{:S(2)}, u32[]{:S(2)}) collective-permute-start(f32[4,72,1152]{2,1,0:T(8,128)} %get-tuple-element.598), channel_id=1, source_target_pairs={{0,1},{1,0},{2,3},{3,2},{4,5},{5,4},{6,7},{7,6},{8,9},{9,8},{10,11... | collective-permute-start | bytes 3981320 | tf_op jit(solution)/shard_map/ppermute | solution.py:593
  698.8 273.1 %all-gather.15.cloned.1.call-start = ((), (), s32[]{:S(2)}) async-start(), calls=%async_computation.4 | async-start | bytes 12533760 | tf_op jit(solution)/shard_map/all_gather | solution.py:611
  717.0 44.2 %collective-permute-start.41 = (f32[8,72,1152]{2,1,0:T(8,128)}, f32[8,72,1152]{2,1,0:T(8,128)}, u32[]{:S(2)}, u32[]{:S(2)}) collective-permute-start(f32[8,72,1152]{2,1,0:T(8,128)} %get-tuple-element.412), channel_id=1, source_target_pairs={{0,2},{2,0},{4,6},{6,4},{8,10},{10,8},{12,14},{14,12},{16,18},{18,... | collective-permute-start | bytes 7962632 | tf_op jit(solution)/shard_map/ppermute | solution.py:596
  717.3 38.3 %collective-permute-start.43 = (f32[5,2,16,1152]{3,2,0,1:T(8,128)}, f32[5,2,16,1152]{3,2,0,1:T(8,128)}, u32[]{:S(2)}, u32[]{:S(2)}) collective-permute-start(f32[5,2,16,1152]{3,2,0,1:T(8,128)} %fusion.16), channel_id=1, source_target_pairs={{0,8},{2,10},{4,12},{6,14},{8,0},{10,2},{12,4},{14,6},{16,24},{18,... | collective-permute-start | bytes 2211848 | tf_op jit(solution)/shard_map/ppermute | solution.py:596
  719.0 38.9 %collective-permute-start.42 = (f32[4,72,1152]{2,1,0:T(8,128)}, f32[4,72,1152]{2,1,0:T(8,128)}, u32[]{:S(2)}, u32[]{:S(2)}) collective-permute-start(f32[4,72,1152]{2,1,0:T(8,128)} %fusion.11), channel_id=1, source_target_pairs={{0,4},{2,6},{4,0},{6,2},{8,12},{10,14},{12,8},{14,10},{16,20},{18,... | collective-permute-start | bytes 3981320 | tf_op jit(solution)/shard_map/ppermute | solution.py:596
  719.4 46.4 %collective-permute-start.49 = (f32[5,1,16,1152]{3,2,0,1:T(8,128)}, f32[5,1,16,1152]{3,2,0,1:T(8,128)}, u32[]{:S(2)}, u32[]{:S(2)}) collective-permute-start(f32[5,1,16,1152]{3,2,0,1:T(8,128)} %fusion.33), channel_id=1, source_target_pairs={{0,16},{2,18},{4,20},{6,22},{8,24},{10,26},{12,28},{14,30},{16,0},... | collective-permute-start | bytes 1105928 | tf_op jit(solution)/shard_map/ppermute | solution.py:596
  765.9 44.5 %collective-permute-start.46 = (f32[8,72,1152]{2,1,0:T(8,128)}, f32[8,72,1152]{2,1,0:T(8,128)}, u32[]{:S(2)}, u32[]{:S(2)}) collective-permute-start(f32[8,72,1152]{2,1,0:T(8,128)} %get-tuple-element.419), channel_id=1, source_target_pairs={{0,2},{2,0},{4,6},{6,4},{8,10},{10,8},{12,14},{14,12},{16,18},{18,... | collective-permute-start | bytes 7962632 | tf_op jit(solution)/shard_map/ppermute | solution.py:596
  769.4 36.0 %collective-permute-start.50 = (f32[5,1,16,1152]{3,2,0,1:T(8,128)}, f32[5,1,16,1152]{3,2,0,1:T(8,128)}, u32[]{:S(2)}, u32[]{:S(2)}) collective-permute-start(f32[5,1,16,1152]{3,2,0,1:T(8,128)} %fusion.31), channel_id=1, source_target_pairs={{0,16},{2,18},{4,20},{6,22},{8,24},{10,26},{12,28},{14,30},{16,0},... | collective-permute-start | bytes 1105928 | tf_op jit(solution)/shard_map/ppermute | solution.py:596
  772.0 35.9 %collective-permute-start.47 = (f32[4,72,1152]{2,1,0:T(8,128)}, f32[4,72,1152]{2,1,0:T(8,128)}, u32[]{:S(2)}, u32[]{:S(2)}) collective-permute-start(f32[4,72,1152]{2,1,0:T(8,128)} %get-tuple-element.425), channel_id=1, source_target_pairs={{0,4},{2,6},{4,0},{6,2},{8,12},{10,14},{12,8},{14,10},{16,20},{18,... | collective-permute-start | bytes 3981320 | tf_op jit(solution)/shard_map/ppermute | solution.py:596
  772.1 35.8 %collective-permute-start.48 = (f32[4,72,1152]{2,1,0:T(8,128)}, f32[4,72,1152]{2,1,0:T(8,128)}, u32[]{:S(2)}, u32[]{:S(2)}) collective-permute-start(f32[4,72,1152]{2,1,0:T(8,128)} %bitcast_add_fusion.7), channel_id=1, source_target_pairs={{0,1},{1,0},{2,3},{3,2},{4,5},{5,4},{6,7},{7,6},{8,9},{9,8},{10,11... | collective-permute-start | bytes 3981320 | tf_op jit(solution)/shard_map/ppermute | solution.py:593
  813.1 281.7 %all-gather.17.cloned.1.call-start = ((), (), s32[]{:S(2)}) async-start(), calls=%async_computation.5 | async-start | bytes 11280384 | tf_op jit(solution)/shard_map/all_gather | solution.py:611
  818.5 44.9 %collective-permute-start.53 = (f32[2,72,1152]{2,1,0:T(8,128)}, f32[2,72,1152]{2,1,0:T(8,128)}, u32[]{:S(2)}, u32[]{:S(2)}) collective-permute-start(f32[2,72,1152]{2,1,0:T(8,128)} %add_bitcast_fusion.3), channel_id=1, source_target_pairs={{0,8},{2,10},{4,12},{6,14},{8,0},{10,2},{12,4},{14,6},{16,24},{18,... | collective-permute-start | bytes 1990664 | tf_op jit(solution)/shard_map/ppermute | solution.py:596
  820.6 44.9 %collective-permute-start.52 = (f32[4,72,1152]{2,1,0:T(8,128)}, f32[4,72,1152]{2,1,0:T(8,128)}, u32[]{:S(2)}, u32[]{:S(2)}) collective-permute-start(f32[4,72,1152]{2,1,0:T(8,128)} %fusion.10), channel_id=1, source_target_pairs={{0,4},{2,6},{4,0},{6,2},{8,12},{10,14},{12,8},{14,10},{16,20},{18,... | collective-permute-start | bytes 3981320 | tf_op jit(solution)/shard_map/ppermute | solution.py:596
  867.6 42.9 %collective-permute-start.58 = (f32[1,72,1152]{2,1,0:T(8,128)}, f32[1,72,1152]{2,1,0:T(8,128)}, u32[]{:S(2)}, u32[]{:S(2)}) collective-permute-start(f32[1,72,1152]{2,1,0:T(8,128)} %bitcast_add_fusion.21), channel_id=1, source_target_pairs={{0,16},{2,18},{4,20},{6,22},{8,24},{10,26},{12,28},{14,30},{16,0},... | collective-permute-start | bytes 995336 | tf_op jit(solution)/shard_map/ppermute | solution.py:596
  868.8 71.4 %collective-permute-start.56 = (f32[64,1729]{1,0:T(8,128)}, f32[64,1729]{1,0:T(8,128)}, u32[]{:S(2)}, u32[]{:S(2)}) collective-permute-start(f32[64,1729]{1,0:T(8,128)} %copy.555), channel_id=1, source_target_pairs={{0,16},{2,18},{4,20},{6,22},{8,24},{10,26},{12,28},{14,30},{16,0},... | collective-permute-start | bytes 1327880 | tf_op jit(solution)/shard_map/ppermute | solution.py:596
  871.7 71.3 %collective-permute-start.55 = (f32[2,72,1152]{2,1,0:T(8,128)}, f32[2,72,1152]{2,1,0:T(8,128)S(1)}, u32[]{:S(2)}, u32[]{:S(2)}) collective-permute-start(f32[2,72,1152]{2,1,0:T(8,128)} %fusion.18), channel_id=1, source_target_pairs={{0,8},{2,10},{4,12},{6,14},{8,0},{10,2},{12,4},{14,6},{16,24},{18,... | collective-permute-start | bytes 1990664 | tf_op jit(solution)/shard_map/ppermute | solution.py:596
  971.9 36.7 %collective-permute-start.59 = (f32[792,128]{1,0:T(8,128)}, f32[792,128]{1,0:T(8,128)}, u32[]{:S(2)}, u32[]{:S(2)}) collective-permute-start(f32[792,128]{1,0:T(8,128)} %pad_bitcast_fusion), channel_id=1, source_target_pairs={{0,2},{2,0},{4,6},{6,4},{8,10},{10,8},{12,14},{14,12},{16,18},{18,... | collective-permute-start | bytes 1216520 | tf_op jit(solution)/shard_map/ppermute | solution.py:596
  (89 other events, 1370.9 us)
Sparse Core Ops, SparseCore 0:
  30.5 56.6 all-gather.6
  104.6 53.7 all-gather.8
  162.8 60.0 all-gather.10
  698.9 108.9 all-gather.12
  813.2 139.5 all-gather.14
  972.0 98.0 all-gather.16

commit v3 on v2

--- a/solution.py
+++ b/solution.py
@@ -513,7 +513,8 @@
     )(core, *lefts, *rights)
 
 
-def first_kernel(parts, *refs):
+def first_kernel(parts, aliased, *refs):
+    refs = refs[1:] if aliased else refs
     tokens_ref, d_middle_ref, gain_ref = refs[:3]
     d_proj_refs = refs[3 : 3 + parts]
     weight_refs = refs[3 + parts : 3 + 2 * parts]
@@ -532,7 +533,7 @@
     sums_ref[1:2, :] += jnp.sum(first, 0, keepdims=True)
 
 
-def first_backward(tokens, d_middle, gain, d_projs, weights, begin, images):
+def first_backward(tokens, d_middle, gain, d_projs, weights, begin, images, previous=()):
     dim = tokens.shape[1]
     count = images * PATCHES
 
@@ -541,17 +542,85 @@
 
     parts = len(d_projs)
     return pl.pallas_call(
-        functools.partial(first_kernel, parts),
-        grid=(count // PATCHES,),
-        in_specs=[some(dim)] * 2
+        functools.partial(first_kernel, parts, len(previous) > 0),
+        grid=(images,),
+        in_specs=[pl.BlockSpec(memory_space=pl.ANY) for _ in previous]
+        + [some(dim)] * 2
         + [fixed((1, dim))]
         + [some(d.shape[1]) for d in d_projs]
         + [fixed(w.shape) for w in weights],
-        out_specs=[rows(PATCHES, dim), fixed((8, dim))],
-        out_shape=[jax.ShapeDtypeStruct((count, dim), jnp.float32), jax.ShapeDtypeStruct((8, dim), jnp.float32)],
+        out_specs=[some(dim), fixed((8, dim))],
+        out_shape=[jax.ShapeDtypeStruct(tokens.shape, jnp.float32), jax.ShapeDtypeStruct((8, dim), jnp.float32)],
+        input_output_aliases={0: 0} if previous else {},
         compiler_params=params(60),
         cost_estimate=cost(18 * count * dim * dim, 4 * (3 * dim * dim + 6 * count * dim)),
-    )(tokens, d_middle, gain, *d_projs, *weights)
+    )(*previous, tokens, d_middle, gain, *d_projs, *weights)
+
+
+def settle_units_kernel(first, scale_ref, one_ref, two_ref, hidden_ref, return_ref):
+    step = pl.program_id(0)
+
+    def put(ref):
+        hidden_ref[...] = (ref[:, 0, 0].reshape(BLOCK, -1) * scale_ref[0]).T
+        return_ref[...] = ref[:, 1, 0].reshape(BLOCK, -1) * scale_ref[0]
+
+    pl.when(step < first)(lambda: put(one_ref))
+    pl.when(step >= first)(lambda: put(two_ref))
+
+
+def settle_units(scale, one, two):
+    first, second, dim = one.shape[2], two.shape[2], one.shape[4]
+    units = (first + second) * BLOCK
+    block = (16, 2, 1, PIECE, dim)
+    return pl.pallas_call(
+        functools.partial(settle_units_kernel, first),
+        grid=(first + second,),
+        in_specs=[
+            scalars(),
+            pl.BlockSpec(block, lambda i: (0, 0, jnp.minimum(i, first - 1), 0, 0)),
+            pl.BlockSpec(block, lambda i: (0, 0, jnp.maximum(i - first, 0), 0, 0)),
+        ],
+        out_specs=[pl.BlockSpec((dim, BLOCK), lambda i: (0, i)), rows(BLOCK, dim)],
+        out_shape=[
+            jax.ShapeDtypeStruct((dim, units), jnp.float32),
+            jax.ShapeDtypeStruct((units, dim), jnp.float32),
+        ],
+        compiler_params=params(40),
+        cost_estimate=cost(0, 16 * units * dim),
+    )(scale, one, two)
+
+
+def settle_attend_kernel(scale_ref, value_ref, attend_ref, output_ref):
+    step = pl.program_id(0)
+    size, dim = attend_ref.shape
+
+    @pl.when(step < 3)
+    def _():
+        attend_ref[...] = value_ref[:, 0].reshape(size, dim) * scale_ref[0]
+
+    @pl.when(step == 3)
+    def _():
+        output_ref[...] = value_ref[:, 0].reshape(size, dim) * scale_ref[0]
+
+
+def settle_attend(scale, value):
+    piece, dim = value.shape[2:]
+    size = 8 * piece
+    return pl.pallas_call(
+        settle_attend_kernel,
+        grid=(4,),
+        in_specs=[scalars(), pl.BlockSpec((8, 1, piece, dim), lambda i: (i % 2, i // 2, 0, 0))],
+        out_specs=[
+            pl.BlockSpec((size, dim), lambda i: (jnp.minimum(i, 2), 0)),
+            pl.BlockSpec((size, dim), lambda i: (0, 0)),
+        ],
+        out_shape=[
+            jax.ShapeDtypeStruct((3 * size, dim), jnp.float32),
+            jax.ShapeDtypeStruct((size, dim), jnp.float32),
+        ],
+        compiler_params=params(40),
+        cost_estimate=cost(0, 16 * size * dim),
+    )(scale, value)
 
 
 def offset_matrix():
@@ -609,13 +678,6 @@
 
     def spread(self, part):
         return lax.all_gather(part, "dp", axis=0, tiled=True)
-
-    def all_sum(self, value):
-        value = value + self.along(value, 0)
-        value = value + self.across(value)
-        for bit in (1, 2, 3):
-            value = value + self.along(value, bit)
-        return value
 
     def rows_step(self, value, bit):
         return self.ordered(value, self.along(value, bit), bit)
@@ -725,34 +787,34 @@
         bias_other = row(ring.across(hidden_bias))
         hidden_shares = [ring.share(hidden_weight, dim, first * BLOCK, blocks * BLOCK) for first, blocks in cuts]
         qk = ring.across(ring.share(attend_own, 2 * width, 0, dim))
-        hidden_share, hidden_share_2 = [ring.across(share) for share in hidden_shares]
         values_half = ring.core_half(attend_own, 2 * width, width)
-        output_half = ring.core_half(output_weight, 0, width)
-        qk, table_other, bias_other, values_half, output_half, time_proj, strips_own = join(
-            qk, table_other, bias_other, values_half, output_half, time_proj, make_strips(bias_table)
+        qk, table_other, bias_other, values_half, time_proj, strips_own = join(
+            qk, table_other, bias_other, values_half, time_proj, make_strips(bias_table)
         )
         attend_qk = ring.spread(qk)
         values_mine = ring.across(values_half)
-        output_mine = ring.across(output_half)
+        hidden_share = ring.across(hidden_shares[0])
         time_mine = lax.dynamic_slice_in_dim(time_proj, first_own, own_images, 0)
         time_theirs = lax.dynamic_slice_in_dim(time_proj, (1 - rank) * own_images, own_images, 0)
         time_other = ring.across(time_theirs)
         own = attend_forward(tokens2, *norm_first, attend_own, times_of(time_mine), strips_own)
         return_halves = [ring.core_half(return_weight, first * BLOCK, blocks * BLOCK) for first, blocks in cuts]
-        own, values_mine, output_mine, time_other, return_half, hidden_share, hidden_share_2 = join(
-            own, values_mine, output_mine, time_other, return_halves[0], hidden_share, hidden_share_2
-        )
-        hidden_other = [ring.spread(hidden_share), ring.spread(hidden_share_2)]
+        own, values_mine, time_other, return_half, output_half, hidden_share, share_2 = join(
+            own, values_mine, time_other, return_halves[0], ring.core_half(output_weight, 0, width), hidden_share,
+            hidden_shares[1],
+        )
+        output_mine = ring.across(output_half)
+        hidden_other = [ring.spread(hidden_share), ring.spread(ring.across(share_2))]
         strips_other = make_strips(table_other)
         values_full = ring.ordered(values_mine, ring.along(values_mine, 0), 0)
-        output_other = ring.ordered(output_mine, ring.along(output_mine, 0), 0)
         attend_other = jnp.concatenate([attend_qk, values_full], 0)
         return_mine = ring.across(return_half)
         other = attend_forward(tokens2, *norm_first, attend_other, times_of(time_other), strips_other)
         attend = [attend_own, attend_other]
+        other, return_mine, output_mine = join(other, return_mine, output_mine)
+        output_other = ring.ordered(output_mine, ring.along(output_mine, 0), 0)
+        return_theirs = ring.along(return_mine, 0)
         output = [output_weight, output_other]
-        other, return_mine = join(other, return_mine)
-        return_theirs = ring.along(return_mine, 0)
         middle, *forms = output_forward(
             live, tokens2, cotangent2, [own[3], other[3]], output, row(output_bias), *norm_second
         )
@@ -875,17 +937,15 @@
         qb.pass_on("own", b)
         units_2 = ring.spread(c)
         packed = ring.rows_step(packed, 2)
-        tokens_b, sums_b = first_backward(
-            tokens2, d_middle, row(first_gain), d_projs, attend, half, own_images - half
-        )
-        tokens_b, sums_b, a, b, packed = join(tokens_b, sums_b, qa.send("own"), qb.send("own"), packed)
+        tokens_grad, sums_b = first_backward(
+            tokens2, d_middle, row(first_gain), d_projs, attend, half, own_images - half, (tokens_a,)
+        )
+        tokens_grad, sums_b, a, b, packed, strips_a, strips_b, d_time = join(
+            tokens_grad, sums_b, qa.send("own"), qb.send("own"), packed, attended_own[2], attended_other[2], d_time
+        )
         qa.pass_on("own", a)
         qb.pass_on("own", b)
         packed = ring.rows_step(packed, 3)
-        a, packed, strips_a, strips_b, d_time, tokens_a, units_1 = join(
-            qa.send("own"), packed, attended_own[2], attended_other[2], d_time, tokens_a, units_1
-        )
-        qa.pass_on("own", a)
         d_time_vec = jnp.einsum("sce,ced->sd", d_time, time_weight.transpose(0, 2, 1), precision=HIGH)
         time_table_part = jnp.dot(onehot.T, d_time_vec, precision=HIGHEST)
         table_full = absolute(table_gradient(strips_a), table_gradient(strips_b))
@@ -898,25 +958,23 @@
         ]
         flat = jnp.concatenate([v.reshape(-1) for v in small]) * inv_total
         flat = jnp.pad(flat, (0, -flat.shape[0] % 1024)).reshape(-1, 128)
+        a, packed, flat = join(qa.send("own"), packed, flat)
+        qa.pass_on("own", a)
+        flat = flat + ring.along(flat, 0)
+        time_weight_grad = time_gradient(packed)
         last = jnp.stack([qa.value("own"), qb.value("own")]).reshape(1, -1, dim)
-        last, flat, packed, units_1, units_2, tokens_a = join(last, flat, packed, units_1, units_2, tokens_a)
+        last, flat, time_weight_grad, units_1, units_2 = join(last, flat, time_weight_grad, units_1, units_2)
         attend_all = ring.spread(last).reshape(16, 2, -1, dim)
-        flat = ring.all_sum(flat)
-        time_weight_grad = time_gradient(packed)
-        tokens_grad = jnp.concatenate([tokens_a, tokens_b], 0)
-
-        def units_of(index):
-            found = [
-                g.reshape(16, 2, -1, PIECE, dim)[:, index].transpose(1, 0, 2, 3).reshape(-1, dim)
-                for g in (units_1, units_2)
-            ]
-            return jnp.concatenate(found, 0) * inv_total
-
-        hidden_grad = units_of(0).T
-        return_grad = units_of(1)
-        attend_all = attend_all.transpose(1, 0, 2, 3).reshape(4, width, dim) * inv_total
-        attend_weight_grad = attend_all[:3].transpose(0, 2, 1)
-        output_weight_grad = attend_all[3]
+        flat = flat + ring.across(flat)
+        scale = inv_total.reshape(1)
+        hidden_grad, return_grad = settle_units(
+            scale, *(g.reshape(16, 2, -1, PIECE, dim) for g in (units_1, units_2))
+        )
+        flat, hidden_grad, return_grad = join(flat, hidden_grad, return_grad)
+        for bit in (1, 2, 3):
+            flat = flat + ring.along(flat, bit)
+        attend_weight_grad, output_weight_grad = settle_attend(scale, attend_all)
+        attend_weight_grad = attend_weight_grad.reshape(3, width, dim).transpose(0, 2, 1)
     else:
         attend = [lax.all_gather(attend_weight, "mp", axis=2, tiled=True).transpose(0, 2, 1).reshape(-1, dim)]
         output = [lax.all_gather(output_weight, "mp", axis=0, tiled=True)]

time: 1130 us -> 1110 us (0.982)
  local copies, waits for them, and re-layouts: 127 us -> 83.1 us
  waiting for transfers between devices: 202 us -> 232 us
  other arithmetic: 137 us -> 112 us
  Pallas kernels: 559 us -> 579 us
    transpose x7 -> x0, local copies, waits for them, and re-layouts: 33.5 us -> none  [the longest x6 26.5 us: units_of(): g.reshape(16, 2, -1, PIECE, dim)[:, index].transpose(1, 0, 2, 3)]
    pallas_call x2 -> x4, Pallas kernels: 50.5 us -> 70.6 us  [the longest x2 50.5 us: first_backward(): pl.pallas_call(functools.partial(first_kernel, parts, len(previous) > 0),...]
    all_gather x6, waiting for transfers between devices: 0.03 us -> 14.6 us  [spread(): return lax.all_gather(part, 'dp', axis=0, tiled=True)]
    mul x2 -> x0, other arithmetic: 13.6 us -> none  [the longest x1 8.92 us: units_of(): return jnp.concatenate(found, 0) * inv_total]
    add x18 -> x17, other arithmetic: 39.3 us -> 36.1 us  [send(): out = out + pick(cut, 1 - bit, axis + 1)]
  transfers between devices with their start and end apart: 70 -> 70, of which waited for: 16 -> 16; matrix products, arithmetic and copies ran while one was open for 23% -> 18% of each run, Pallas kernels for 50% -> 52%
where the time goes in v3:
time: 1110 us; the launch traced here: 1100 us
  Pallas kernels  579 us (52%)
  waiting for transfers between devices  232 us (21%)
  other arithmetic  112 us (10%)
  local copies, waits for them, and re-layouts  83.1 us (7%)
  starting transfers between devices  54.7 us (5%)
  matrix products  23.7 us (2%)
  between operations  16.5 us (1%)
    pallas_call x4, Pallas kernels, feed(): pl.pallas_call(functools.partial(feed_kernel, split), grid=(blocks,), in_...  269 us
    ppermute x45, waiting for transfers between devices, along(): return lax.ppermute(value, 'dp', [(i, i ^ 1 << bit) for i in range(16)])  176 us
    pallas_call x2, Pallas kernels, attend_forward(): pl.pallas_call(functools.partial(attend_forward_kernel, heads), grid=(ima...  66.3 us
    pallas_call x4, Pallas kernels, attend_weights(): pl.pallas_call(functools.partial(attend_weights_kernel, split, steps), gr...  63.3 us
    pallas_call x2, Pallas kernels, attend_backward(): pl.pallas_call(functools.partial(attend_backward_kernel, heads), grid=(im...  61.1 us
    pallas_call x2, Pallas kernels, first_backward(): pl.pallas_call(functools.partial(first_kernel, parts, len(previous) > 0),...  50.5 us
    ppermute x19, waiting for transfers between devices, across(): return lax.ppermute(value, 'mp', [(0, 1), (1, 0)])  41.7 us
    add x17, other arithmetic, send(): out = out + pick(cut, 1 - bit, axis + 1)  36.1 us
  transfers between devices with their start and end apart: 70, of which 16 were waited for; matrix products, arithmetic and copies ran while one was open for 18% of the time, Pallas kernels for 52%

profile of v3, /device:TPU:0, one launch (start us, length us, event | category | flops | bytes accessed | tf_op | source)
XLA Modules:
  0.0 1100.8 jit_solution(9950548476032098572)
XLA Ops:
  17.7 6.6 fusion.2
  36.6 3.2 constant_dynamic-slice_fusion.32
  43.7 33.1 %shard_map.297 = (f32[1024,576]{1,0:T(8,128)}, f32[1024,576]{1,0:T(8,128)}, f32[1024,576]{1,0:T(8,128)}, f32[1024,576]{1,0:T(8,128)}, f32[576,1024]{1,0:T(8,128)...) custom-call(f32[1024,1152]{1,0:T(8,128)} %bitcast.386, f32[1,1152]{1,0:T(1,128)} %reshape.1151.gain_ref.refs_2_.refs_3_, ...), custom_call_target="tpu_custom_call" | custom-call | flops 18673040 | bytes 22118 | tf_op jit(solution)/shard_map/pallas_call | solution.py:142
  88.0 6.3 pad_maximum_fusion.weight_ref.refs_6_.refs_7_
  94.3 33.3 %shard_map.298 = (f32[1024,576]{1,0:T(8,128)}, f32[1024,576]{1,0:T(8,128)}, f32[1024,576]{1,0:T(8,128)}, f32[1024,576]{1,0:T(8,128)}, f32[576,1024]{1,0:T(8,128)...) custom-call(f32[1024,1152]{1,0:T(8,128)} %bitcast.387, f32[1,1152]{1,0:T(1,128)} %reshape.1151.gain_ref.refs_2_.refs_3_, ...), custom_call_target="tpu_custom_call" | custom-call | flops 18673040 | bytes 22118 | tf_op jit(solution)/shard_map/pallas_call | solution.py:142
  127.5 32.9 %collective-permute-done.8 = f32[288,1152]{1,0:T(8,128)} collective-permute-done((f32[288,1152]{1,0:T(8,128)}, f32[288,1152]{1,0:T(8,128)}, u32[]{:S(2)}, u32[]{:S(2)}) %collective-permute-start.8) | collective-permute-done | bytes 1327136 | tf_op jit(solution)/shard_map/ppermute | solution.py:662
  166.1 6.3 collective-permute-done.13
  178.3 21.0 %shard_map.299 = (f32[1024,1152]{1,0:T(8,128)}, bf16[1024,2304]{1,0:T(8,128)(2,1)}, bf16[1024,2304]{1,0:T(8,128)(2,1)}) custom-call(f32[4]{0:T(128)S(1)} %compare_convert_fusion.refs_0_, f32[1024,1152]{1,0:T(8,128)} %bitcast.388, f32[1024,1152]{1,0:T(8,128)} %bitcast.396, f32[1024,576]{1,0:T(8,128)S(1)} %copy-done.2, f32[1024,576]{1,0:T(8,128)S(1)} %copy-done.3, ...), custom_call_target="tpu_custom_call" | custom-call | flops 8153726 | bytes 28901 | tf_op jit(solution)/shard_map/pallas_call | solution.py:188
  201.6 3.4 broadcast_select_fusion.3
  207.5 60.6 %shard_map.300 = (f32[1024,1152]{1,0:T(8,128)}, f32[1024,1152]{1,0:T(8,128)}, f32[1,1024]{1,0:T(1,128)}, f32[4,8,16,1152]{3,2,1,0:T(8,128)}, f32[4,8,16,1152]{3,...) custom-call(s32[1]{0:T(128)} %bitcast.14.core_ref, ...), custom_call_target="tpu_custom_call" | custom-call | flops 43486544 | bytes 42467 | tf_op jit(solution)/shard_map/pallas_call | solution.py:305
  268.3 5.6 collective-permute-done.12
  280.1 73.4 %shard_map.301 = (f32[1024,1152]{1,0:T(8,128)}, f32[1024,1152]{1,0:T(8,128)}, f32[1,1280]{1,0:T(1,128)}, f32[5,8,16,1152]{3,2,1,0:T(8,128)}, f32[5,8,16,1152]{3,...) custom-call(s32[1]{0:T(128)} %bitcast.14.core_ref, ...), custom_call_target="tpu_custom_call" | custom-call | flops 54358180 | bytes 47185 | tf_op jit(solution)/shard_map/pallas_call | solution.py:305
  361.9 60.9 %shard_map.302 = (f32[1024,1152]{1,0:T(8,128)}, f32[1024,1152]{1,0:T(8,128)}, f32[1,1024]{1,0:T(1,128)}, f32[4,8,16,1152]{3,2,1,0:T(8,128)}, f32[4,8,16,1152]{3,...) custom-call(s32[1]{0:T(128)} %bitcast.14.core_ref, ...), custom_call_target="tpu_custom_call" | custom-call | flops 43486544 | bytes 42467 | tf_op jit(solution)/shard_map/pallas_call | solution.py:305
  424.3 4.9 add.1246
  435.5 73.6 %shard_map.303 = (f32[1024,1152]{1,0:T(8,128)}, f32[1024,1152]{1,0:T(8,128)}, f32[1,1280]{1,0:T(1,128)}, f32[5,8,16,1152]{3,2,1,0:T(8,128)}, f32[5,8,16,1152]{3,...) custom-call(s32[1]{0:T(128)} %bitcast.14.core_ref, ...), custom_call_target="tpu_custom_call" | custom-call | flops 54358180 | bytes 47185 | tf_op jit(solution)/shard_map/pallas_call | solution.py:305
  517.4 3.4 bitcast_add_fusion.3
  524.4 4.3 constant_dynamic-slice_fusion.21
  528.7 28.4 %shard_map.304 = (f32[1024,1152]{1,0:T(8,128)}, f32[1024,1152]{1,0:T(8,128)}, f32[8,1152]{1,0:T(8,128)}, f32[1024,576]{1,0:T(8,128)}, f32[1024,576]{1,0:T(8,128)}) custom-call(f32[4]{0:T(128)} %copy-done.6, f32[1024,1152]{1,0:T(8,128)} %get-tuple-element.340.refs_1_, f32[1024,1152]{1,0:T(8,128)} %bitcast.397, f32[1,1152]{1,0:T(1,128)} %copy-done.5, ...), custom_call_target="tpu_custom_call" | custom-call | flops 8153726 | bytes 47775 | tf_op jit(solution)/shard_map/pallas_call | solution.py:366
  563.7 30.7 %shard_map.305 = (f32[1024,1728]{1,0:T(8,128)}, f32[1728,1024]{1,0:T(8,128)}, f32[8,16,512]{2,1,0:T(8,128)}, f32[4,1,1728]{2,1,0:T(1,128)}) custom-call(f32[1024,576]{1,0:T(8,128)} %get-tuple-element.354.query_ref, f32[1024,576]{1,0:T(8,128)} %get-tuple-element.355.keys_ref, f32[1024,576]{1,0:T(8,128)} %get-tuple-element.356.values_ref, ...), custom_call_target="tpu_custom_call" | custom-call | flops 16106127 | bytes 21233 | tf_op jit(solution)/shard_map/pallas_call | solution.py:437
  599.9 3.3 fusion.7
  603.3 14.6 %shard_map.306 = (f32[8,72,1152]{2,1,0:T(8,128)}, f32[8,72,1152]{2,1,0:T(8,128)}) custom-call(s32[1]{0:T(128)} %bitcast.14.core_ref, f32[1728,1024]{1,0:T(8,128)} %get-tuple-element.376.refs_0_, f32[1024,1152]{1,0:T(8,128)} %get-tuple-element.411.refs_1_.refs_2_), custom_call_target="tpu_custom_call" | custom-call | flops 8153726 | bytes 19464 | tf_op jit(solution)/shard_map/pallas_call | solution.py:503
  619.7 3.4 constant_dynamic-slice_fusion.9
  626.2 3.9 constant_dynamic-slice_fusion.3
  632.2 16.7 %shard_map.307 = (f32[8,72,1152]{2,1,0:T(8,128)}, f32[8,72,1152]{2,1,0:T(8,128)}) custom-call(s32[1]{0:T(128)} %bitcast.14.core_ref, f32[1728,1024]{1,0:T(8,128)} %get-tuple-element.376.refs_0_, f32[576,1024]{1,0:T(8,128)} %get-tuple-element.377.refs_1_, f32[1024,1152]{1,0:T(8,128)} %get-tuple-element.411.refs_1_.refs_2_, ...), custom_call_target="tpu_custom_call" | custom-call | flops 8153726 | bytes 19464 | tf_op jit(solution)/shard_map/pallas_call | solution.py:503
  667.1 30.4 %shard_map.308 = (f32[1024,1728]{1,0:T(8,128)}, f32[1728,1024]{1,0:T(8,128)}, f32[8,16,512]{2,1,0:T(8,128)}, f32[4,1,1728]{2,1,0:T(1,128)}) custom-call(f32[1024,576]{1,0:T(8,128)} %get-tuple-element.351.query_ref, f32[1024,576]{1,0:T(8,128)} %get-tuple-element.352.keys_ref, f32[1024,576]{1,0:T(8,128)} %get-tuple-element.353.values_ref, ...), custom_call_target="tpu_custom_call" | custom-call | flops 16106127 | bytes 21233 | tf_op jit(solution)/shard_map/pallas_call | solution.py:437
  710.8 17.3 %shard_map.309 = (f32[8,72,1152]{2,1,0:T(8,128)}, f32[8,72,1152]{2,1,0:T(8,128)}) custom-call(s32[1]{0:T(128)} %bitcast.14.core_ref, f32[1728,1024]{1,0:T(8,128)} %get-tuple-element.406.refs_0_, f32[576,1024]{1,0:T(8,128)} %get-tuple-element.407.refs_1_, f32[1024,1152]{1,0:T(8,128)} %get-tuple-element.411.refs_1_.refs_2_, ...), custom_call_target="tpu_custom_call" | custom-call | flops 8153726 | bytes 19464 | tf_op jit(solution)/shard_map/pallas_call | solution.py:503
  730.7 14.6 %shard_map.310 = (f32[8,72,1152]{2,1,0:T(8,128)}, f32[8,72,1152]{2,1,0:T(8,128)}) custom-call(s32[1]{0:T(128)} %bitcast.14.core_ref, f32[1728,1024]{1,0:T(8,128)} %get-tuple-element.406.refs_0_, f32[1024,1152]{1,0:T(8,128)} %get-tuple-element.411.refs_1_.refs_2_), custom_call_target="tpu_custom_call" | custom-call | flops 8153726 | bytes 19464 | tf_op jit(solution)/shard_map/pallas_call | solution.py:503
  745.6 19.8 %collective-permute-done.43 = f32[5,2,16,1152]{3,2,0,1:T(8,128)} collective-permute-done((f32[5,2,16,1152]{3,2,0,1:T(8,128)}, f32[5,2,16,1152]{3,2,0,1:T(8,128)}, u32[]{:S(2)}, u32[]{:S(2)}) %collective-permute-start.43) | collective-permute-done | bytes 737312 | tf_op jit(solution)/shard_map/ppermute | solution.py:665
  767.6 3.3 bitcast_add_fusion.5
  770.9 3.8 constant_dynamic-slice_fusion.15
  785.6 25.1 %shard_map.311 = (f32[1024,1152]{1,0:T(8,128)}, f32[8,1152]{1,0:T(8,128)}) custom-call(f32[1024,1152]{1,0:T(8,128)} %bitcast.389, f32[1024,1152]{1,0:T(8,128)} %get-tuple-element.350.refs_3_.refs_1_.refs_2_, f32[1,1152]{1,0:T(1,128)} %reshape.1151.gain_ref.refs_2_.refs_3_, f32[1024,1728]{1,0:T(8,128)} %get-tuple-element.436.refs_3_.refs_4_, ...), custom_call_target="tpu_custom_call" | custom-call | flops 12230590 | bytes 30081 | tf_op jit(solution)/shard_map/pallas_call | solution.py:544
  810.8 5.7 collective-permute-done.50
  821.6 4.4 constant_dynamic-slice_fusion.6
  832.0 25.4 %shard_map.312 = (f32[1024,1152]{1,0:T(8,128)}, f32[8,1152]{1,0:T(8,128)}) custom-call(f32[1024,1152]{1,0:T(8,128)} %get-tuple-element.435.refs_0_, f32[1024,1152]{1,0:T(8,128)} %bitcast.390, f32[1024,1152]{1,0:T(8,128)} %get-tuple-element.350.refs_3_.refs_1_.refs_2_, f32[1,1152]{1,0:T(1,128)} %reshape.1151.gain_ref.refs_2_.refs_3_, ...), custom_call_target="tpu_custom_call", output_to_operand_aliasing={{0}: (0, {})} | custom-call | flops 12230590 | bytes 30081 | tf_op jit(solution)/shard_map/pallas_call | solution.py:544
  858.3 15.4 %collective-permute-done.53 = f32[2,72,1152]{2,1,0:T(8,128)} collective-permute-done((f32[2,72,1152]{2,1,0:T(8,128)}, f32[2,72,1152]{2,1,0:T(8,128)}, u32[]{:S(2)}, u32[]{:S(2)}) %collective-permute-start.53) | collective-permute-done | bytes 663584 | tf_op jit(solution)/shard_map/ppermute | solution.py:665
  878.2 5.4 fusion.4
  903.2 27.1 %collective-permute-done.58 = f32[1,72,1152]{2,1,0:T(8,128)} collective-permute-done((f32[1,72,1152]{2,1,0:T(8,128)}, f32[1,72,1152]{2,1,0:T(8,128)}, u32[]{:S(2)}, u32[]{:S(2)}) %collective-permute-start.58) | collective-permute-done | bytes 331808 | tf_op jit(solution)/shard_map/ppermute | solution.py:665
  932.6 26.3 %collective-permute-done.56 = f32[64,1729]{1,0:T(8,128)} collective-permute-done((f32[64,1729]{1,0:T(8,128)}, f32[64,1729]{1,0:T(8,128)}, u32[]{:S(2)}, u32[]{:S(2)}) %collective-permute-start.56) | collective-permute-done | bytes 442656 | tf_op jit(solution)/shard_map/ppermute | solution.py:665
  964.2 5.4 convolution_bitcast_fusion
  969.6 9.9 collective-permute-done.57
  981.9 3.7 copy-done.4
  985.5 14.6 %shard_map.313 = (f32[1152,2304]{1,0:T(8,128)}, f32[2304,1152]{1,0:T(8,128)}) custom-call(f32[1]{0:T(128)} %bitcast.115.scale_ref, f32[16,2,4,16,1152]{4,3,2,1,0:T(8,128)S(1)} %bitcast.385, f32[16,2,5,16,1152]{4,3,2,1,0:T(8,128)} %bitcast.398), custom_call_target="tpu_custom_call" | custom-call | bytes 42467 | tf_op jit(solution)/shard_map/pallas_call | solution.py:575
  1000.3 11.2 %collective-permute-done.61 = f32[792,128]{1,0:T(8,128)S(1)} collective-permute-done((f32[792,128]{1,0:T(8,128)S(1)}, f32[792,128]{1,0:T(8,128)S(1)}, u32[]{:S(2)}, u32[]{:S(2)}) %collective-permute-start.61) | collective-permute-done | bytes 405536 | tf_op jit(solution)/shard_map/ppermute | solution.py:665
  1011.6 13.6 %collective-permute-done.62 = f32[792,128]{1,0:T(8,128)S(1)} collective-permute-done((f32[792,128]{1,0:T(8,128)S(1)}, f32[792,128]{1,0:T(8,128)S(1)}, u32[]{:S(2)}, u32[]{:S(2)}) %collective-permute-start.62) | collective-permute-done | bytes 405536 | tf_op jit(solution)/shard_map/ppermute | solution.py:665
  1028.1 40.1 %collective-permute-done.63 = f32[792,128]{1,0:T(8,128)S(1)} collective-permute-done((f32[792,128]{1,0:T(8,128)S(1)}, f32[792,128]{1,0:T(8,128)S(1)}, u32[]{:S(2)}, u32[]{:S(2)}) %collective-permute-start.63) | collective-permute-done | bytes 405536 | tf_op jit(solution)/shard_map/ppermute | solution.py:665
  1071.1 13.1 %all-gather.17.cloned.1.call-done = f32[16,144,1152]{2,1,0:T(8,128)} async-done(((f32[1,144,1152]{2,1,0:T(8,128)}), f32[16,144,1152]{2,1,0:T(8,128)}) %all-gather.17.cloned.1.call-update) | async-done | bytes 10616848 | tf_op jit(solution)/shard_map/all_gather | solution.py:680
  1084.3 4.0 copy-done.1
  1088.3 5.5 shard_map.314
  (429 shorter events, 205.6 us)
Async XLA Ops:
  7.2 80.8 %all-gather.7.cloned.1.call-start = ((), (), s32[]{:S(2)}) async-start(), calls=%async_computation | async-start | bytes 5640192 | tf_op jit(solution)/shard_map/all_gather | solution.py:680
  31.1 176.4 %all-gather.9.cloned.1.call-start = ((), (), s32[]{:S(2)}) async-start(), calls=%async_computation.1 | async-start | bytes 5013504 | tf_op jit(solution)/shard_map/all_gather | solution.py:680
  31.7 45.2 %collective-permute-start.3 = (f32[288,1152]{1,0:T(8,128)}, f32[288,1152]{1,0:T(8,128)}, u32[]{:S(2)}, u32[]{:S(2)}) collective-permute-start(f32[288,1152]{1,0:T(8,128)} %constant_dynamic-slice_fusion.35), channel_id=1, source_target_pairs={{0,1},{1,0},{2,3},{3,2},{4,5},{5,4},{6,7},{7,6},{8,9},{9,8},{10,11... | collective-permute-start | bytes 3981320 | tf_op jit(solution)/shard_map/ppermute | solution.py:662
  33.5 43.3 %collective-permute-start.5 = (f32[72,1024]{1,0:T(8,128)}, f32[72,1024]{1,0:T(8,128)S(1)}, u32[]{:S(2)}, u32[]{:S(2)}) collective-permute-start(f32[72,1024]{1,0:T(8,128)} %constant_dynamic-slice_fusion.30), channel_id=1, source_target_pairs={{0,1},{1,0},{2,3},{3,2},{4,5},{5,4},{6,7},{7,6},{8,9},{9,8},{10,11... | collective-permute-start | bytes 884744 | tf_op jit(solution)/shard_map/ppermute | solution.py:662
  39.9 37.0 %collective-permute-start.4 = (f32[4,3,576]{2,0,1:T(4,128)S(1)}, f32[4,3,576]{2,0,1:T(4,128)S(1)}, u32[]{:S(2)}, u32[]{:S(2)}) collective-permute-start(f32[4,3,576]{2,0,1:T(4,128)S(1)} %get-tuple-element.524), channel_id=1, source_target_pairs={{0,1},{1,0},{2,3},{3,2},{4,5},{5,4},{6,7},{7,6},{8,9},{9,8},{10,11... | collective-permute-start | bytes 82952 | tf_op jit(solution)/shard_map/ppermute | solution.py:662
  77.6 202.6 %all-gather.11.cloned.1.call-start = ((), (), s32[]{:S(2)}) async-start(), calls=%async_computation.2 | async-start | bytes 6266880 | tf_op jit(solution)/shard_map/all_gather | solution.py:680
  77.9 82.6 %collective-permute-start.7 = (f32[512,1152]{1,0:T(8,128)}, f32[512,1152]{1,0:T(8,128)}, u32[]{:S(2)}, u32[]{:S(2)}) collective-permute-start(f32[512,1152]{1,0:T(8,128)} %constant_dynamic-slice_fusion.32), channel_id=1, source_target_pairs={{0,1},{1,0},{2,3},{3,2},{4,5},{5,4},{6,7},{7,6},{8,9},{9,8},{10,11... | collective-permute-start | bytes 7077896 | tf_op jit(solution)/shard_map/ppermute | solution.py:662
  84.6 75.9 %collective-permute-start.8 = (f32[288,1152]{1,0:T(8,128)}, f32[288,1152]{1,0:T(8,128)}, u32[]{:S(2)}, u32[]{:S(2)}) collective-permute-start(f32[288,1152]{1,0:T(8,128)} %constant_dynamic-slice_fusion.31), channel_id=1, source_target_pairs={{0,1},{1,0},{2,3},{3,2},{4,5},{5,4},{6,7},{7,6},{8,9},{9,8},{10,11... | collective-permute-start | bytes 3981320 | tf_op jit(solution)/shard_map/ppermute | solution.py:662
  160.5 38.8 %collective-permute-start.10 = (f32[512,1152]{1,0:T(8,128)}, f32[512,1152]{1,0:T(8,128)}, u32[]{:S(2)}, u32[]{:S(2)}) collective-permute-start(f32[512,1152]{1,0:T(8,128)} %collective-permute-done.7), channel_id=1, source_target_pairs={{0,2},{2,0},{4,6},{6,4},{8,10},{10,8},{12,14},{14,12},{16,18},{18,... | collective-permute-start | bytes 7077896 | tf_op jit(solution)/shard_map/ppermute | solution.py:665
  172.4 809.3 %all-gather.13.cloned.1.call-start = ((), (), s32[]{:S(2)}) async-start(), calls=%async_computation.3 | async-start | bytes 10027008 | tf_op jit(solution)/shard_map/all_gather | solution.py:680
  199.2 68.9 %collective-permute-start.11 = (f32[640,1152]{1,0:T(8,128)S(1)}, f32[640,1152]{1,0:T(8,128)}, u32[]{:S(2)}, u32[]{:S(2)}) collective-permute-start(f32[640,1152]{1,0:T(8,128)S(1)} %constant_dynamic-slice_fusion.29), channel_id=1, source_target_pairs={{0,1},{1,0},{2,3},{3,2},{4,5},{5,4},{6,7},{7,6},{8,9},{9,8},{10,11... | collective-permute-start | bytes 8847368 | tf_op jit(solution)/shard_map/ppermute | solution.py:662
  279.0 74.5 %collective-permute-start.15 = (f32[4,8,16,1152]{3,2,1,0:T(8,128)}, f32[4,8,16,1152]{3,2,1,0:T(8,128)}, u32[]{:S(2)}, u32[]{:S(2)}) collective-permute-start(f32[4,8,16,1152]{3,2,1,0:T(8,128)} %get-tuple-element.309), channel_id=1, source_target_pairs={{0,2},{2,0},{4,6},{6,4},{8,10},{10,8},{12,14},{14,12},{16,18},{18,... | collective-permute-start | bytes 7077896 | tf_op jit(solution)/shard_map/ppermute | solution.py:665
  279.1 77.4 %collective-permute-start.14 = (f32[4,8,16,1152]{3,2,1,0:T(8,128)}, f32[4,8,16,1152]{3,2,1,0:T(8,128)S(1)}, u32[]{:S(2)}, u32[]{:S(2)}) collective-permute-start(f32[4,8,16,1152]{3,2,1,0:T(8,128)} %get-tuple-element.307), channel_id=1, source_target_pairs={{0,2},{2,0},{4,6},{6,4},{8,10},{10,8},{12,14},{14,12},{16,18},{18,... | collective-permute-start | bytes 7077896 | tf_op jit(solution)/shard_map/ppermute | solution.py:665
  358.2 66.0 %collective-permute-start.16 = (f32[5,8,16,1152]{3,2,1,0:T(8,128)}, f32[5,8,16,1152]{3,2,1,0:T(8,128)}, u32[]{:S(2)}, u32[]{:S(2)}) collective-permute-start(f32[5,8,16,1152]{3,2,1,0:T(8,128)} %get-tuple-element.320), channel_id=1, source_target_pairs={{0,2},{2,0},{4,6},{6,4},{8,10},{10,8},{12,14},{14,12},{16,18},{18,... | collective-permute-start | bytes 8847368 | tf_op jit(solution)/shard_map/ppermute | solution.py:665
  358.4 70.7 %collective-permute-start.17 = (f32[5,8,16,1152]{3,2,1,0:T(8,128)}, f32[5,8,16,1152]{3,2,1,0:T(8,128)}, u32[]{:S(2)}, u32[]{:S(2)}) collective-permute-start(f32[5,8,16,1152]{3,2,1,0:T(8,128)} %get-tuple-element.322), channel_id=1, source_target_pairs={{0,2},{2,0},{4,6},{6,4},{8,10},{10,8},{12,14},{14,12},{16,18},{18,... | collective-permute-start | bytes 8847368 | tf_op jit(solution)/shard_map/ppermute | solution.py:665
  358.7 73.2 %collective-permute-start.18 = (f32[4,8,16,1152]{3,2,1,0:T(8,128)}, f32[4,8,16,1152]{3,2,1,0:T(8,128)}, u32[]{:S(2)}, u32[]{:S(2)}) collective-permute-start(f32[4,8,16,1152]{3,2,1,0:T(8,128)} %add.1242), channel_id=1, source_target_pairs={{0,1},{1,0},{2,3},{3,2},{4,5},{5,4},{6,7},{7,6},{8,9},{9,8},{10,11... | collective-permute-start | bytes 7077896 | tf_op jit(solution)/shard_map/ppermute | solution.py:662
  358.7 73.1 %collective-permute-start.19 = (f32[4,4,16,1152]{3,2,1,0:T(8,128)}, f32[4,4,16,1152]{3,2,1,0:T(8,128)}, u32[]{:S(2)}, u32[]{:S(2)}) collective-permute-start(f32[4,4,16,1152]{3,2,1,0:T(8,128)} %fusion.11), channel_id=1, source_target_pairs={{0,4},{2,6},{4,0},{6,2},{8,12},{10,14},{12,8},{14,10},{16,20},{18,... | collective-permute-start | bytes 3538952 | tf_op jit(solution)/shard_map/ppermute | solution.py:665
  431.9 84.1 %collective-permute-start.21 = (f32[5,8,16,1152]{3,2,1,0:T(8,128)}, f32[5,8,16,1152]{3,2,1,0:T(8,128)}, u32[]{:S(2)}, u32[]{:S(2)}) collective-permute-start(f32[5,8,16,1152]{3,2,1,0:T(8,128)} %add.1246), channel_id=1, source_target_pairs={{0,1},{1,0},{2,3},{3,2},{4,5},{5,4},{6,7},{7,6},{8,9},{9,8},{10,11... | collective-permute-start | bytes 8847368 | tf_op jit(solution)/shard_map/ppermute | solution.py:662
  433.9 79.5 %collective-permute-start.20 = (f32[4,8,16,1152]{3,2,1,0:T(8,128)}, f32[4,8,16,1152]{3,2,1,0:T(8,128)}, u32[]{:S(2)}, u32[]{:S(2)}) collective-permute-start(f32[4,8,16,1152]{3,2,1,0:T(8,128)} %get-tuple-element.335), channel_id=1, source_target_pairs={{0,2},{2,0},{4,6},{6,4},{8,10},{10,8},{12,14},{14,12},{16,18},{18,... | collective-permute-start | bytes 7077896 | tf_op jit(solution)/shard_map/ppermute | solution.py:665
  433.9 83.5 %collective-permute-start.23 = (f32[5,4,16,1152]{3,2,1,0:T(8,128)}, f32[5,4,16,1152]{3,2,1,0:T(8,128)}, u32[]{:S(2)}, u32[]{:S(2)}) collective-permute-start(f32[5,4,16,1152]{3,2,1,0:T(8,128)} %fusion.8), channel_id=1, source_target_pairs={{0,4},{2,6},{4,0},{6,2},{8,12},{10,14},{12,8},{14,10},{16,20},{18,... | collective-permute-start | bytes 4423688 | tf_op jit(solution)/shard_map/ppermute | solution.py:665
  434.6 88.4 %collective-permute-start.22 = (f32[4,8,16,1152]{3,2,1,0:T(8,128)}, f32[4,8,16,1152]{3,2,1,0:T(8,128)}, u32[]{:S(2)}, u32[]{:S(2)}) collective-permute-start(f32[4,8,16,1152]{3,2,1,0:T(8,128)} %get-tuple-element.359), channel_id=1, source_target_pairs={{0,2},{2,0},{4,6},{6,4},{8,10},{10,8},{12,14},{14,12},{16,18},{18,... | collective-permute-start | bytes 7077896 | tf_op jit(solution)/shard_map/ppermute | solution.py:665
  516.0 41.1 %collective-permute-start.24 = (f32[4,4,16,1152]{3,2,1,0:T(8,128)}, f32[4,4,16,1152]{3,2,1,0:T(8,128)}, u32[]{:S(2)}, u32[]{:S(2)}) collective-permute-start(f32[4,4,16,1152]{3,2,1,0:T(8,128)} %fusion.10), channel_id=1, source_target_pairs={{0,4},{2,6},{4,0},{6,2},{8,12},{10,14},{12,8},{14,10},{16,20},{18,... | collective-permute-start | bytes 3538952 | tf_op jit(solution)/shard_map/ppermute | solution.py:665
  517.3 39.9 %collective-permute-start.25 = (f32[4,4,16,1152]{3,2,1,0:T(8,128)}, f32[4,4,16,1152]{3,2,1,0:T(8,128)}, u32[]{:S(2)}, u32[]{:S(2)}) collective-permute-start(f32[4,4,16,1152]{3,2,1,0:T(8,128)} %add_add_fusion), channel_id=1, source_target_pairs={{0,1},{1,0},{2,3},{3,2},{4,5},{5,4},{6,7},{7,6},{8,9},{9,8},{10,11... | collective-permute-start | bytes 3538952 | tf_op jit(solution)/shard_map/ppermute | solution.py:662
  520.7 77.9 %collective-permute-start.28 = (f32[5,8,16,1152]{3,2,1,0:T(8,128)}, f32[5,8,16,1152]{3,2,1,0:T(8,128)}, u32[]{:S(2)}, u32[]{:S(2)}) collective-permute-start(f32[5,8,16,1152]{3,2,1,0:T(8,128)} %get-tuple-element.373), channel_id=1, source_target_pairs={{0,2},{2,0},{4,6},{6,4},{8,10},{10,8},{12,14},{14,12},{16,18},{18,... | collective-permute-start | bytes 8847368 | tf_op jit(solution)/shard_map/ppermute | solution.py:665
  559.5 36.5 %collective-permute-start.26 = (f32[4,4,16,1152]{3,2,1,0:T(8,128)}, f32[4,4,16,1152]{3,2,1,0:T(8,128)}, u32[]{:S(2)}, u32[]{:S(2)}) collective-permute-start(f32[4,4,16,1152]{3,2,1,0:T(8,128)} %get-tuple-element.370), channel_id=1, source_target_pairs={{0,4},{2,6},{4,0},{6,2},{8,12},{10,14},{12,8},{14,10},{16,20},{18,... | collective-permute-start | bytes 3538952 | tf_op jit(solution)/shard_map/ppermute | solution.py:665
  560.1 66.1 %collective-permute-start.32 = (f32[5,8,16,1152]{3,2,1,0:T(8,128)}, f32[5,8,16,1152]{3,2,1,0:T(8,128)}, u32[]{:S(2)}, u32[]{:S(2)}) collective-permute-start(f32[5,8,16,1152]{3,2,1,0:T(8,128)} %get-tuple-element.389), channel_id=1, source_target_pairs={{0,2},{2,0},{4,6},{6,4},{8,10},{10,8},{12,14},{14,12},{16,18},{18,... | collective-permute-start | bytes 8847368 | tf_op jit(solution)/shard_map/ppermute | solution.py:665
  561.7 41.6 %collective-permute-start.29 = (f32[5,4,16,1152]{3,2,1,0:T(8,128)}, f32[5,4,16,1152]{3,2,1,0:T(8,128)}, u32[]{:S(2)}, u32[]{:S(2)}) collective-permute-start(f32[5,4,16,1152]{3,2,1,0:T(8,128)} %bitcast_add_fusion.3), channel_id=1, source_target_pairs={{0,1},{1,0},{2,3},{3,2},{4,5},{5,4},{6,7},{7,6},{8,9},{9,8},{10,11... | collective-permute-start | bytes 4423688 | tf_op jit(solution)/shard_map/ppermute | solution.py:662
  617.9 37.5 %collective-permute-start.30 = (f32[8,72,1152]{2,1,0:T(8,128)}, f32[8,72,1152]{2,1,0:T(8,128)}, u32[]{:S(2)}, u32[]{:S(2)}) collective-permute-start(f32[8,72,1152]{2,1,0:T(8,128)} %get-tuple-element.386), channel_id=1, source_target_pairs={{0,2},{2,0},{4,6},{6,4},{8,10},{10,8},{12,14},{14,12},{16,18},{18,... | collective-permute-start | bytes 7962632 | tf_op jit(solution)/shard_map/ppermute | solution.py:665
  657.4 47.3 %collective-permute-start.35 = (f32[8,72,1152]{2,1,0:T(8,128)}, f32[8,72,1152]{2,1,0:T(8,128)}, u32[]{:S(2)}, u32[]{:S(2)}) collective-permute-start(f32[8,72,1152]{2,1,0:T(8,128)} %get-tuple-element.399), channel_id=1, source_target_pairs={{0,2},{2,0},{4,6},{6,4},{8,10},{10,8},{12,14},{14,12},{16,18},{18,... | collective-permute-start | bytes 7962632 | tf_op jit(solution)/shard_map/ppermute | solution.py:665
  660.7 36.8 %collective-permute-start.36 = (f32[4,1,16,1152]{3,2,0,1:T(8,128)S(1)}, f32[4,1,16,1152]{3,2,0,1:T(8,128)}, u32[]{:S(2)}, u32[]{:S(2)}) collective-permute-start(f32[4,1,16,1152]{3,2,0,1:T(8,128)S(1)} %fusion.44), channel_id=1, source_target_pairs={{0,16},{2,18},{4,20},{6,22},{8,24},{10,26},{12,28},{14,30},{16,0},... | collective-permute-start | bytes 884744 | tf_op jit(solution)/shard_map/ppermute | solution.py:665
  663.4 36.4 %collective-permute-start.38 = (f32[5,2,16,1152]{3,2,0,1:T(8,128)}, f32[5,2,16,1152]{3,2,0,1:T(8,128)}, u32[]{:S(2)}, u32[]{:S(2)}) collective-permute-start(f32[5,2,16,1152]{3,2,0,1:T(8,128)} %fusion.15), channel_id=1, source_target_pairs={{0,8},{2,10},{4,12},{6,14},{8,0},{10,2},{12,4},{14,6},{16,24},{18,... | collective-permute-start | bytes 2211848 | tf_op jit(solution)/shard_map/ppermute | solution.py:665
  663.7 38.1 %collective-permute-start.37 = (f32[5,4,16,1152]{3,2,1,0:T(8,128)}, f32[5,4,16,1152]{3,2,1,0:T(8,128)}, u32[]{:S(2)}, u32[]{:S(2)}) collective-permute-start(f32[5,4,16,1152]{3,2,1,0:T(8,128)} %get-tuple-element.402), channel_id=1, source_target_pairs={{0,4},{2,6},{4,0},{6,2},{8,12},{10,14},{12,8},{14,10},{16,20},{18,... | collective-permute-start | bytes 4423688 | tf_op jit(solution)/shard_map/ppermute | solution.py:665
  667.0 41.5 %collective-permute-start.39 = (f32[4,72,1152]{2,1,0:T(8,128)}, f32[4,72,1152]{2,1,0:T(8,128)}, u32[]{:S(2)}, u32[]{:S(2)}) collective-permute-start(f32[4,72,1152]{2,1,0:T(8,128)} %get-tuple-element.496), channel_id=1, source_target_pairs={{0,1},{1,0},{2,3},{3,2},{4,5},{5,4},{6,7},{7,6},{8,9},{9,8},{10,11... | collective-permute-start | bytes 3981320 | tf_op jit(solution)/shard_map/ppermute | solution.py:662
  708.5 273.2 %all-gather.15.cloned.1.call-start = ((), (), s32[]{:S(2)}) async-start(), calls=%async_computation.4 | async-start | bytes 12533760 | tf_op jit(solution)/shard_map/all_gather | solution.py:680
  728.1 42.8 %collective-permute-start.41 = (f32[8,72,1152]{2,1,0:T(8,128)}, f32[8,72,1152]{2,1,0:T(8,128)}, u32[]{:S(2)}, u32[]{:S(2)}) collective-permute-start(f32[8,72,1152]{2,1,0:T(8,128)} %get-tuple-element.417), channel_id=1, source_target_pairs={{0,2},{2,0},{4,6},{6,4},{8,10},{10,8},{12,14},{14,12},{16,18},{18,... | collective-permute-start | bytes 7962632 | tf_op jit(solution)/shard_map/ppermute | solution.py:665
  728.4 37.0 %collective-permute-start.43 = (f32[5,2,16,1152]{3,2,0,1:T(8,128)}, f32[5,2,16,1152]{3,2,0,1:T(8,128)}, u32[]{:S(2)}, u32[]{:S(2)}) collective-permute-start(f32[5,2,16,1152]{3,2,0,1:T(8,128)} %fusion.14), channel_id=1, source_target_pairs={{0,8},{2,10},{4,12},{6,14},{8,0},{10,2},{12,4},{14,6},{16,24},{18,... | collective-permute-start | bytes 2211848 | tf_op jit(solution)/shard_map/ppermute | solution.py:665
  730.2 37.4 %collective-permute-start.42 = (f32[4,72,1152]{2,1,0:T(8,128)}, f32[4,72,1152]{2,1,0:T(8,128)}, u32[]{:S(2)}, u32[]{:S(2)}) collective-permute-start(f32[4,72,1152]{2,1,0:T(8,128)} %fusion.9), channel_id=1, source_target_pairs={{0,4},{2,6},{4,0},{6,2},{8,12},{10,14},{12,8},{14,10},{16,20},{18,... | collective-permute-start | bytes 3981320 | tf_op jit(solution)/shard_map/ppermute | solution.py:665
  730.7 46.5 %collective-permute-start.49 = (f32[5,1,16,1152]{3,2,0,1:T(8,128)}, f32[5,1,16,1152]{3,2,0,1:T(8,128)}, u32[]{:S(2)}, u32[]{:S(2)}) collective-permute-start(f32[5,1,16,1152]{3,2,0,1:T(8,128)} %fusion.30), channel_id=1, source_target_pairs={{0,16},{2,18},{4,20},{6,22},{8,24},{10,26},{12,28},{14,30},{16,0},... | collective-permute-start | bytes 1105928 | tf_op jit(solution)/shard_map/ppermute | solution.py:665
  777.2 44.4 %collective-permute-start.46 = (f32[8,72,1152]{2,1,0:T(8,128)}, f32[8,72,1152]{2,1,0:T(8,128)}, u32[]{:S(2)}, u32[]{:S(2)}) collective-permute-start(f32[8,72,1152]{2,1,0:T(8,128)} %get-tuple-element.427), channel_id=1, source_target_pairs={{0,2},{2,0},{4,6},{6,4},{8,10},{10,8},{12,14},{14,12},{16,18},{18,... | collective-permute-start | bytes 7962632 | tf_op jit(solution)/shard_map/ppermute | solution.py:665
  780.7 35.8 %collective-permute-start.50 = (f32[5,1,16,1152]{3,2,0,1:T(8,128)}, f32[5,1,16,1152]{3,2,0,1:T(8,128)}, u32[]{:S(2)}, u32[]{:S(2)}) collective-permute-start(f32[5,1,16,1152]{3,2,0,1:T(8,128)} %fusion.28), channel_id=1, source_target_pairs={{0,16},{2,18},{4,20},{6,22},{8,24},{10,26},{12,28},{14,30},{16,0},... | collective-permute-start | bytes 1105928 | tf_op jit(solution)/shard_map/ppermute | solution.py:665
  783.3 35.7 %collective-permute-start.47 = (f32[4,72,1152]{2,1,0:T(8,128)}, f32[4,72,1152]{2,1,0:T(8,128)}, u32[]{:S(2)}, u32[]{:S(2)}) collective-permute-start(f32[4,72,1152]{2,1,0:T(8,128)} %get-tuple-element.430), channel_id=1, source_target_pairs={{0,4},{2,6},{4,0},{6,2},{8,12},{10,14},{12,8},{14,10},{16,20},{18,... | collective-permute-start | bytes 3981320 | tf_op jit(solution)/shard_map/ppermute | solution.py:665
  826.1 258.2 %all-gather.17.cloned.1.call-start = ((), (), s32[]{:S(2)}) async-start(), calls=%async_computation.5 | async-start | bytes 11280384 | tf_op jit(solution)/shard_map/all_gather | solution.py:680
  826.1 49.8 %collective-permute-start.52 = (f32[4,72,1152]{2,1,0:T(8,128)}, f32[4,72,1152]{2,1,0:T(8,128)}, u32[]{:S(2)}, u32[]{:S(2)}) collective-permute-start(f32[4,72,1152]{2,1,0:T(8,128)} %get-tuple-element.440), channel_id=1, source_target_pairs={{0,4},{2,6},{4,0},{6,2},{8,12},{10,14},{12,8},{14,10},{16,20},{18,... | collective-permute-start | bytes 3981320 | tf_op jit(solution)/shard_map/ppermute | solution.py:665
  830.0 43.8 %collective-permute-start.53 = (f32[2,72,1152]{2,1,0:T(8,128)}, f32[2,72,1152]{2,1,0:T(8,128)}, u32[]{:S(2)}, u32[]{:S(2)}) collective-permute-start(f32[2,72,1152]{2,1,0:T(8,128)} %add_bitcast_fusion.5), channel_id=1, source_target_pairs={{0,8},{2,10},{4,12},{6,14},{8,0},{10,2},{12,4},{14,6},{16,24},{18,... | collective-permute-start | bytes 1990664 | tf_op jit(solution)/shard_map/ppermute | solution.py:665
  884.7 45.6 %collective-permute-start.58 = (f32[1,72,1152]{2,1,0:T(8,128)}, f32[1,72,1152]{2,1,0:T(8,128)}, u32[]{:S(2)}, u32[]{:S(2)}) collective-permute-start(f32[1,72,1152]{2,1,0:T(8,128)} %bitcast_add_fusion.17), channel_id=1, source_target_pairs={{0,16},{2,18},{4,20},{6,22},{8,24},{10,26},{12,28},{14,30},{16,0},... | collective-permute-start | bytes 995336 | tf_op jit(solution)/shard_map/ppermute | solution.py:665
  886.9 72.0 %collective-permute-start.56 = (f32[64,1729]{1,0:T(8,128)}, f32[64,1729]{1,0:T(8,128)}, u32[]{:S(2)}, u32[]{:S(2)}) collective-permute-start(f32[64,1729]{1,0:T(8,128)} %copy.469), channel_id=1, source_target_pairs={{0,16},{2,18},{4,20},{6,22},{8,24},{10,26},{12,28},{14,30},{16,0},... | collective-permute-start | bytes 1327880 | tf_op jit(solution)/shard_map/ppermute | solution.py:665
  888.7 72.0 %collective-permute-start.55 = (f32[2,72,1152]{2,1,0:T(8,128)}, f32[2,72,1152]{2,1,0:T(8,128)}, u32[]{:S(2)}, u32[]{:S(2)}) collective-permute-start(f32[2,72,1152]{2,1,0:T(8,128)} %add_bitcast_fusion.4), channel_id=1, source_target_pairs={{0,8},{2,10},{4,12},{6,14},{8,0},{10,2},{12,4},{14,6},{16,24},{18,... | collective-permute-start | bytes 1990664 | tf_op jit(solution)/shard_map/ppermute | solution.py:665
  1025.2 42.9 %collective-permute-start.63 = (f32[792,128]{1,0:T(8,128)S(1)}, f32[792,128]{1,0:T(8,128)S(1)}, u32[]{:S(2)}, u32[]{:S(2)}) collective-permute-start(f32[792,128]{1,0:T(8,128)S(1)} %add.1374), channel_id=1, source_target_pairs={{0,16},{2,18},{4,20},{6,22},{8,24},{10,26},{12,28},{14,30},{16,0},... | collective-permute-start | bytes 1216520 | tf_op jit(solution)/shard_map/ppermute | solution.py:665
  (97 other events, 1400.0 us)
Sparse Core Ops, SparseCore 0:
  31.3 56.6 all-gather.6
  90.8 51.9 all-gather.8
  172.5 61.2 all-gather.10
  708.6 110.4 all-gather.12
  826.2 136.9 all-gather.14
  981.9 102.3 all-gather.16

commit v4 on v3

--- a/solution.py
+++ b/solution.py
@@ -788,31 +788,31 @@
         hidden_shares = [ring.share(hidden_weight, dim, first * BLOCK, blocks * BLOCK) for first, blocks in cuts]
         qk = ring.across(ring.share(attend_own, 2 * width, 0, dim))
         values_half = ring.core_half(attend_own, 2 * width, width)
-        qk, table_other, bias_other, values_half, time_proj, strips_own = join(
-            qk, table_other, bias_other, values_half, time_proj, make_strips(bias_table)
+        output_half = ring.core_half(output_weight, 0, width)
+        qk, table_other, bias_other, values_half, output_half, time_proj, strips_own = join(
+            qk, table_other, bias_other, values_half, output_half, time_proj, make_strips(bias_table)
         )
         attend_qk = ring.spread(qk)
         values_mine = ring.across(values_half)
-        hidden_share = ring.across(hidden_shares[0])
+        output_mine = ring.across(output_half)
         time_mine = lax.dynamic_slice_in_dim(time_proj, first_own, own_images, 0)
         time_theirs = lax.dynamic_slice_in_dim(time_proj, (1 - rank) * own_images, own_images, 0)
         time_other = ring.across(time_theirs)
         own = attend_forward(tokens2, *norm_first, attend_own, times_of(time_mine), strips_own)
         return_halves = [ring.core_half(return_weight, first * BLOCK, blocks * BLOCK) for first, blocks in cuts]
-        own, values_mine, time_other, return_half, output_half, hidden_share, share_2 = join(
-            own, values_mine, time_other, return_halves[0], ring.core_half(output_weight, 0, width), hidden_share,
-            hidden_shares[1],
-        )
-        output_mine = ring.across(output_half)
-        hidden_other = [ring.spread(hidden_share), ring.spread(ring.across(share_2))]
+        own, values_mine, output_mine, time_other, return_half, share_1, share_2 = join(
+            own, values_mine, output_mine, time_other, return_halves[0], *hidden_shares
+        )
+        hidden_other = [ring.spread(ring.across(share_1)), ring.spread(ring.across(share_2))]
+        output_theirs = ring.along(output_mine, 0)
         strips_other = make_strips(table_other)
         values_full = ring.ordered(values_mine, ring.along(values_mine, 0), 0)
         attend_other = jnp.concatenate([attend_qk, values_full], 0)
         return_mine = ring.across(return_half)
         other = attend_forward(tokens2, *norm_first, attend_other, times_of(time_other), strips_other)
         attend = [attend_own, attend_other]
-        other, return_mine, output_mine = join(other, return_mine, output_mine)
-        output_other = ring.ordered(output_mine, ring.along(output_mine, 0), 0)
+        other, return_mine, output_mine, output_theirs = join(other, return_mine, output_mine, output_theirs)
+        output_other = ring.ordered(output_mine, output_theirs, 0)
         return_theirs = ring.along(return_mine, 0)
         output = [output_weight, output_other]
         middle, *forms = output_forward(
@@ -886,30 +886,30 @@
             return attend_weights(True, core, [attended[1], flipped_mixed], [normed, d_middle], [2, 0], [1, 1])
 
         normed_first = own[6]
-        part = weights_a(attended_other, normed_first)
-        part, normed_first = join(part, normed_first)
-        qa.begin("other", *part)
-        part = weights_b(attended_other, normed_first, other[4])
-        part, d_mixed_own, a, b, c, d, e = join(
-            part, d_mixed_own, qa.value("other"), h1.send("own"), r2.send("own"), h2.send("own"), r1.value("own")
-        )
-        qb.begin("other", *part)
-        qa_first = ring.across(a[:4])
+        part = attend_weights(
+            True, core, [attended_other[1], other[4]], [normed_first, d_middle], [0, 0], [3, 1]
+        )
+        part, normed_first, d_mixed_own, b, c, d, return_1 = join(
+            part, normed_first, d_mixed_own, h1.send("own"), r2.send("own"), h2.send("own"), r1.value("own")
+        )
+        got = ring.along(part[1], 0)
+        for reduction, begin in ((qa, 0), (qb, 8)):
+            reduction.terms["other"] = [part[0][begin : begin + 8], got[begin : begin + 8]]
+            reduction.level["other"] = 1
         h1.pass_on("own", b)
         r2.pass_on("own", c)
         r2.terms["own"].append(r2_crossed)
         h2.pass_on("own", d)
-        return_1 = e
         attended_own = attend_backward(*own[:4], d_mixed_own, own[5], strips_own)
-        attended_own, a, b, c, d, e, qa_first = join(
-            attended_own, qb.send("other"), pair_up(h1.value("own"), return_1), r2.send("own"), h2.send("own"), a[4:],
-            qa_first,
+        attended_own, a, b, c, d, e = join(
+            attended_own, qb.send("other"), pair_up(h1.value("own"), return_1), r2.send("own"), h2.send("own"),
+            qa.value("other"),
         )
         qb.pass_on("other", a)
         units_1 = ring.spread(b)
         r2.pass_on("own", c)
         h2.pass_on("own", d)
-        qa_second = ring.across(e)
+        qa_first = ring.across(e[:4])
         d_time_got = ring.across(attended_other[3].reshape(own_images, 3, width))
         part = weights_b(attended_own, normed_first, own[4])
         part, normed_first, d_time_got = join(part, normed_first, d_time_got)
@@ -918,21 +918,24 @@
         packed = ring.rows_step(packed, 0)
         qb.begin("own", *part)
         part = weights_a(attended_own, normed_first)
-        part, d_projs, a, b, c, qa_second, packed = join(
+        part, d_projs, a, b, c, qa_first, packed, e = join(
             part, [attended_own[0], attended_other[0]], qb.send("own"), qb.value("other"), r2.send("own"),
-            qa_second, packed,
+            qa_first, packed, e[4:],
         )
         qa.begin("own", *part)
-        qa.terms["own"].append(jnp.concatenate([qa_first, qa_second], 0))
+        qa_second = ring.across(e)
         qb.pass_on("own", a)
         qb.cross(b)
         r2.pass_on("own", c)
         packed = ring.rows_step(packed, 1)
         half = own_images // 2
         tokens_a, sums_a = first_backward(tokens2, d_middle, row(first_gain), d_projs, attend, 0, half)
-        tokens_a, d_projs, a, b, c, packed = join(
-            tokens_a, d_projs, qa.send("own"), qb.send("own"), pair_up(h2.value("own"), r2.value("own")), packed
-        )
+        tokens_a, d_projs, qa_second, qa.terms["own"], b, c, packed = join(
+            tokens_a, d_projs, qa_second, qa.terms["own"], qb.send("own"),
+            pair_up(h2.value("own"), r2.value("own")), packed,
+        )
+        qa.terms["own"].append(jnp.concatenate([qa_first, qa_second], 0))
+        d_projs, a = join(d_projs, qa.send("own"))
         qa.pass_on("own", a)
         qb.pass_on("own", b)
         units_2 = ring.spread(c)

time: 1110 us -> 1140 us (1.027)
  waiting for transfers between devices: 232 us -> 277 us
    ppermute x19, waiting for transfers between devices: 41.7 us -> 73.7 us  [across(): return lax.ppermute(value, 'mp', [(0, 1), (1, 0)])]
    ppermute x45 -> x44, waiting for transfers between devices: 176 us -> 190 us  [along(): return lax.ppermute(value, 'dp', [(i, i ^ 1 << bit) for i in range(16)])]
    ppermute x45 -> x44, starting transfers between devices: 33.8 us -> 27.3 us  [along(): return lax.ppermute(value, 'dp', [(i, i ^ 1 << bit) for i in range(16)])]
    pallas_call x4 -> x3, Pallas kernels: 63.3 us -> 58.5 us  [attend_weights(): pl.pallas_call(functools.partial(attend_weights_kernel, split, steps), gr...]
  transfers between devices with their start and end apart: 70 -> 69, of which waited for: 16 -> 17; matrix products, arithmetic and copies ran while one was open for 18% -> 17% of each run, Pallas kernels for 52% -> 50%
where the time goes in v4:
time: 1140 us; the launch traced here: 1130 us
  Pallas kernels  575 us (50%)
  waiting for transfers between devices  277 us (24%)
  other arithmetic  115 us (10%)
  local copies, waits for them, and re-layouts  78.7 us (7%)
  starting transfers between devices  45.7 us (4%)
  matrix products  25.9 us (2%)
  between operations  16.3 us (1%)
    pallas_call x4, Pallas kernels, feed(): pl.pallas_call(functools.partial(feed_kernel, split), grid=(blocks,), in_...  269 us
    ppermute x44, waiting for transfers between devices, along(): return lax.ppermute(value, 'dp', [(i, i ^ 1 << bit) for i in range(16)])  190 us
    ppermute x19, waiting for transfers between devices, across(): return lax.ppermute(value, 'mp', [(0, 1), (1, 0)])  73.7 us
    pallas_call x2, Pallas kernels, attend_forward(): pl.pallas_call(functools.partial(attend_forward_kernel, heads), grid=(ima...  66.1 us
    pallas_call x2, Pallas kernels, attend_backward(): pl.pallas_call(functools.partial(attend_backward_kernel, heads), grid=(im...  61.9 us
    pallas_call x3, Pallas kernels, attend_weights(): pl.pallas_call(functools.partial(attend_weights_kernel, split, steps), gr...  58.5 us
    pallas_call x2, Pallas kernels, first_backward(): pl.pallas_call(functools.partial(first_kernel, parts, len(previous) > 0),...  50.3 us
    add x17, other arithmetic, send(): out = out + pick(cut, 1 - bit, axis + 1)  35.9 us
  transfers between devices with their start and end apart: 69, of which 17 were waited for; matrix products, arithmetic and copies ran while one was open for 17% of the time, Pallas kernels for 50%

profile of v4, /device:TPU:0, one launch (start us, length us, event | category | flops | bytes accessed | tf_op | source)
XLA Modules:
  0.0 1133.1 jit_solution(16546743085386525684)
XLA Ops:
  15.9 6.8 fusion.2
  34.5 3.2 constant_dynamic-slice_fusion.31
  40.8 33.1 %shard_map.297 = (f32[1024,576]{1,0:T(8,128)}, f32[1024,576]{1,0:T(8,128)}, f32[1024,576]{1,0:T(8,128)}, f32[1024,576]{1,0:T(8,128)}, f32[576,1024]{1,0:T(8,128)...) custom-call(f32[1024,1152]{1,0:T(8,128)} %bitcast.386, f32[1,1152]{1,0:T(1,128)} %reshape.1151.gain_ref.refs_2_.refs_3_, ...), custom_call_target="tpu_custom_call" | custom-call | flops 18673040 | bytes 22118 | tf_op jit(solution)/shard_map/pallas_call | solution.py:142
  73.9 16.1 %collective-permute-done.5 = f32[4,3,576]{2,0,1:T(4,128)S(1)} collective-permute-done((f32[4,3,576]{2,0,1:T(4,128)S(1)}, f32[4,3,576]{2,0,1:T(4,128)S(1)}, u32[]{:S(2)}, u32[]{:S(2)}) %collective-permute-start.5) | collective-permute-done | bytes 27680 | tf_op jit(solution)/shard_map/ppermute | solution.py:662
  90.4 6.6 collective-permute-done.10
  106.0 6.4 pad_maximum_fusion.weight_ref.refs_6_.refs_7_
  112.4 33.1 %shard_map.298 = (f32[1024,576]{1,0:T(8,128)}, f32[1024,576]{1,0:T(8,128)}, f32[1024,576]{1,0:T(8,128)}, f32[1024,576]{1,0:T(8,128)}, f32[576,1024]{1,0:T(8,128)...) custom-call(f32[1024,1152]{1,0:T(8,128)} %bitcast.387, f32[1,1152]{1,0:T(1,128)} %reshape.1151.gain_ref.refs_2_.refs_3_, ...), custom_call_target="tpu_custom_call" | custom-call | flops 18673040 | bytes 22118 | tf_op jit(solution)/shard_map/pallas_call | solution.py:142
  145.4 6.9 collective-permute-done.7
  156.4 7.9 collective-permute-done.13
  169.9 21.1 %shard_map.299 = (f32[1024,1152]{1,0:T(8,128)}, bf16[1024,2304]{1,0:T(8,128)(2,1)}, bf16[1024,2304]{1,0:T(8,128)(2,1)}) custom-call(f32[4]{0:T(128)S(1)} %compare_convert_fusion.refs_0_, f32[1024,1152]{1,0:T(8,128)} %bitcast.388, f32[1024,1152]{1,0:T(8,128)} %bitcast.396, f32[1024,576]{1,0:T(8,128)S(1)} %copy-done.2, f32[1024,576]{1,0:T(8,128)S(1)} %copy-done.3, ...), custom_call_target="tpu_custom_call" | custom-call | flops 8153726 | bytes 28901 | tf_op jit(solution)/shard_map/pallas_call | solution.py:188
  192.2 3.2 broadcast_select_fusion.3
  197.9 60.6 %shard_map.300 = (f32[1024,1152]{1,0:T(8,128)}, f32[1024,1152]{1,0:T(8,128)}, f32[1,1024]{1,0:T(1,128)}, f32[4,8,16,1152]{3,2,1,0:T(8,128)}, f32[4,8,16,1152]{3,...) custom-call(s32[1]{0:T(128)} %bitcast.14.core_ref, ...), custom_call_target="tpu_custom_call" | custom-call | flops 43486544 | bytes 42467 | tf_op jit(solution)/shard_map/pallas_call | solution.py:305
  258.6 5.6 collective-permute-done.12
  270.5 73.6 %shard_map.301 = (f32[1024,1152]{1,0:T(8,128)}, f32[1024,1152]{1,0:T(8,128)}, f32[1,1280]{1,0:T(1,128)}, f32[5,8,16,1152]{3,2,1,0:T(8,128)}, f32[5,8,16,1152]{3,...) custom-call(s32[1]{0:T(128)} %bitcast.14.core_ref, ...), custom_call_target="tpu_custom_call" | custom-call | flops 54358180 | bytes 47185 | tf_op jit(solution)/shard_map/pallas_call | solution.py:305
  354.1 60.7 %shard_map.302 = (f32[1024,1152]{1,0:T(8,128)}, f32[1024,1152]{1,0:T(8,128)}, f32[1,1024]{1,0:T(1,128)}, f32[4,8,16,1152]{3,2,1,0:T(8,128)}, f32[4,8,16,1152]{3,...) custom-call(s32[1]{0:T(128)} %bitcast.14.core_ref, ...), custom_call_target="tpu_custom_call" | custom-call | flops 43486544 | bytes 42467 | tf_op jit(solution)/shard_map/pallas_call | solution.py:305
  416.2 4.8 add.1246
  426.1 73.8 %shard_map.303 = (f32[1024,1152]{1,0:T(8,128)}, f32[1024,1152]{1,0:T(8,128)}, f32[1,1280]{1,0:T(1,128)}, f32[5,8,16,1152]{3,2,1,0:T(8,128)}, f32[5,8,16,1152]{3,...) custom-call(s32[1]{0:T(128)} %bitcast.14.core_ref, ...), custom_call_target="tpu_custom_call" | custom-call | flops 54358180 | bytes 47185 | tf_op jit(solution)/shard_map/pallas_call | solution.py:305
  508.3 3.3 bitcast_add_fusion.3
  514.2 4.3 constant_dynamic-slice_fusion.21
  518.5 28.4 %shard_map.304 = (f32[1024,1152]{1,0:T(8,128)}, f32[1024,1152]{1,0:T(8,128)}, f32[8,1152]{1,0:T(8,128)}, f32[1024,576]{1,0:T(8,128)}, f32[1024,576]{1,0:T(8,128)}) custom-call(f32[4]{0:T(128)} %copy-done.6, f32[1024,1152]{1,0:T(8,128)} %get-tuple-element.344.refs_1_, f32[1024,1152]{1,0:T(8,128)} %bitcast.397, f32[1,1152]{1,0:T(1,128)} %copy-done.5, ...), custom_call_target="tpu_custom_call" | custom-call | flops 8153726 | bytes 47775 | tf_op jit(solution)/shard_map/pallas_call | solution.py:366
  553.1 30.8 %shard_map.305 = (f32[1024,1728]{1,0:T(8,128)}, f32[1728,1024]{1,0:T(8,128)}, f32[8,16,512]{2,1,0:T(8,128)}, f32[4,1,1728]{2,1,0:T(1,128)}) custom-call(f32[1024,576]{1,0:T(8,128)} %get-tuple-element.358.query_ref, f32[1024,576]{1,0:T(8,128)} %get-tuple-element.359.keys_ref, f32[1024,576]{1,0:T(8,128)} %get-tuple-element.360.values_ref, ...), custom_call_target="tpu_custom_call" | custom-call | flops 16106127 | bytes 21233 | tf_op jit(solution)/shard_map/pallas_call | solution.py:437
  599.8 4.1 constant_dynamic-slice_fusion.3
  606.6 26.7 %shard_map.306 = (f32[16,72,1152]{2,1,0:T(8,128)}, f32[16,72,1152]{2,1,0:T(8,128)}) custom-call(s32[1]{0:T(128)} %bitcast.14.core_ref, f32[1728,1024]{1,0:T(8,128)} %get-tuple-element.380.refs_0_, f32[576,1024]{1,0:T(8,128)} %get-tuple-element.381.refs_1_, f32[1024,1152]{1,0:T(8,128)} %get-tuple-element.410.refs_2_.refs_1_, ...), custom_call_target="tpu_custom_call" | custom-call | flops 16307453 | bytes 24772 | tf_op jit(solution)/shard_map/pallas_call | solution.py:503
  642.3 31.0 %shard_map.307 = (f32[1024,1728]{1,0:T(8,128)}, f32[1728,1024]{1,0:T(8,128)}, f32[8,16,512]{2,1,0:T(8,128)}, f32[4,1,1728]{2,1,0:T(1,128)}) custom-call(f32[1024,576]{1,0:T(8,128)} %get-tuple-element.355.query_ref, f32[1024,576]{1,0:T(8,128)} %get-tuple-element.356.keys_ref, f32[1024,576]{1,0:T(8,128)} %get-tuple-element.357.values_ref, ...), custom_call_target="tpu_custom_call" | custom-call | flops 16106127 | bytes 21233 | tf_op jit(solution)/shard_map/pallas_call | solution.py:437
  681.2 6.2 slice_add_fusion
  693.7 17.1 %shard_map.308 = (f32[8,72,1152]{2,1,0:T(8,128)}, f32[8,72,1152]{2,1,0:T(8,128)}) custom-call(s32[1]{0:T(128)} %bitcast.14.core_ref, f32[1728,1024]{1,0:T(8,128)} %get-tuple-element.404.refs_0_, f32[576,1024]{1,0:T(8,128)} %get-tuple-element.405.refs_1_, f32[1024,1152]{1,0:T(8,128)} %get-tuple-element.410.refs_2_.refs_1_, ...), custom_call_target="tpu_custom_call" | custom-call | flops 8153726 | bytes 19464 | tf_op jit(solution)/shard_map/pallas_call | solution.py:503
  711.7 3.4 fusion.71
  715.0 14.7 %shard_map.309 = (f32[8,72,1152]{2,1,0:T(8,128)}, f32[8,72,1152]{2,1,0:T(8,128)}) custom-call(s32[1]{0:T(128)} %bitcast.14.core_ref, f32[1728,1024]{1,0:T(8,128)} %get-tuple-element.404.refs_0_, f32[1024,1152]{1,0:T(8,128)} %get-tuple-element.410.refs_2_.refs_1_), custom_call_target="tpu_custom_call" | custom-call | flops 8153726 | bytes 19464 | tf_op jit(solution)/shard_map/pallas_call | solution.py:503
  738.3 8.1 collective-permute-done.42
  749.4 37.9 %collective-permute-done.48 = f32[5,1,16,1152]{3,2,0,1:T(8,128)} collective-permute-done((f32[5,1,16,1152]{3,2,0,1:T(8,128)}, f32[5,1,16,1152]{3,2,0,1:T(8,128)}, u32[]{:S(2)}, u32[]{:S(2)}) %collective-permute-start.48) | collective-permute-done | bytes 368672 | tf_op jit(solution)/shard_map/ppermute | solution.py:665
  790.5 25.0 %shard_map.310 = (f32[1024,1152]{1,0:T(8,128)}, f32[8,1152]{1,0:T(8,128)}) custom-call(f32[1024,1152]{1,0:T(8,128)} %bitcast.389, f32[1024,1152]{1,0:T(8,128)} %get-tuple-element.354.refs_3_.refs_1_.refs_2_, f32[1,1152]{1,0:T(1,128)} %reshape.1151.gain_ref.refs_2_.refs_3_, f32[1024,1728]{1,0:T(8,128)} %get-tuple-element.440.refs_3_.refs_4_, ...), custom_call_target="tpu_custom_call" | custom-call | flops 12230590 | bytes 30081 | tf_op jit(solution)/shard_map/pallas_call | solution.py:544
  820.7 28.0 %collective-permute-done.47 = f32[4,72,1152]{2,1,0:T(8,128)S(1)} collective-permute-done((f32[4,72,1152]{2,1,0:T(8,128)}, f32[4,72,1152]{2,1,0:T(8,128)S(1)}, u32[]{:S(2)}, u32[]{:S(2)}) %collective-permute-start.47) | collective-permute-done | bytes 1327136 | tf_op jit(solution)/shard_map/ppermute | solution.py:662
  854.0 4.4 constant_dynamic-slice_fusion.6
  864.0 25.3 %shard_map.311 = (f32[1024,1152]{1,0:T(8,128)}, f32[8,1152]{1,0:T(8,128)}) custom-call(f32[1024,1152]{1,0:T(8,128)} %get-tuple-element.433.refs_0_, f32[1024,1152]{1,0:T(8,128)} %bitcast.390, f32[1024,1152]{1,0:T(8,128)} %get-tuple-element.354.refs_3_.refs_1_.refs_2_, f32[1,1152]{1,0:T(1,128)} %reshape.1151.gain_ref.refs_2_.refs_3_, ...), custom_call_target="tpu_custom_call", output_to_operand_aliasing={{0}: (0, {})} | custom-call | flops 12230590 | bytes 30081 | tf_op jit(solution)/shard_map/pallas_call | solution.py:544
  891.1 13.4 %collective-permute-done.52 = f32[2,72,1152]{2,1,0:T(8,128)} collective-permute-done((f32[2,72,1152]{2,1,0:T(8,128)}, f32[2,72,1152]{2,1,0:T(8,128)}, u32[]{:S(2)}, u32[]{:S(2)}) %collective-permute-start.52) | collective-permute-done | bytes 663584 | tf_op jit(solution)/shard_map/ppermute | solution.py:665
  908.7 6.7 fusion.4
  934.2 27.3 %collective-permute-done.57 = f32[1,72,1152]{2,1,0:T(8,128)} collective-permute-done((f32[1,72,1152]{2,1,0:T(8,128)}, f32[1,72,1152]{2,1,0:T(8,128)}, u32[]{:S(2)}, u32[]{:S(2)}) %collective-permute-start.57) | collective-permute-done | bytes 331808 | tf_op jit(solution)/shard_map/ppermute | solution.py:665
  963.8 27.0 %collective-permute-done.55 = f32[64,1729]{1,0:T(8,128)} collective-permute-done((f32[64,1729]{1,0:T(8,128)}, f32[64,1729]{1,0:T(8,128)}, u32[]{:S(2)}, u32[]{:S(2)}) %collective-permute-start.55) | collective-permute-done | bytes 442656 | tf_op jit(solution)/shard_map/ppermute | solution.py:665
  996.3 5.4 convolution_bitcast_fusion
  1001.7 10.4 collective-permute-done.56
  1014.4 3.7 copy-done.4
  1018.1 14.7 %shard_map.312 = (f32[1152,2304]{1,0:T(8,128)}, f32[2304,1152]{1,0:T(8,128)}) custom-call(f32[1]{0:T(128)} %bitcast.115.scale_ref, f32[16,2,4,16,1152]{4,3,2,1,0:T(8,128)S(1)} %bitcast.385, f32[16,2,5,16,1152]{4,3,2,1,0:T(8,128)} %bitcast.398), custom_call_target="tpu_custom_call" | custom-call | bytes 42467 | tf_op jit(solution)/shard_map/pallas_call | solution.py:575
  1033.4 10.8 collective-permute-done.60
  1044.3 16.0 %collective-permute-done.61 = f32[792,128]{1,0:T(8,128)S(1)} collective-permute-done((f32[792,128]{1,0:T(8,128)S(1)}, f32[792,128]{1,0:T(8,128)S(1)}, u32[]{:S(2)}, u32[]{:S(2)}) %collective-permute-start.61) | collective-permute-done | bytes 405536 | tf_op jit(solution)/shard_map/ppermute | solution.py:665
  1060.8 40.6 %collective-permute-done.62 = f32[792,128]{1,0:T(8,128)S(1)} collective-permute-done((f32[792,128]{1,0:T(8,128)S(1)}, f32[792,128]{1,0:T(8,128)S(1)}, u32[]{:S(2)}, u32[]{:S(2)}) %collective-permute-start.62) | collective-permute-done | bytes 405536 | tf_op jit(solution)/shard_map/ppermute | solution.py:665
  1104.3 12.3 %all-gather.17.cloned.1.call-done = f32[16,144,1152]{2,1,0:T(8,128)} async-done(((f32[1,144,1152]{2,1,0:T(8,128)}), f32[16,144,1152]{2,1,0:T(8,128)}) %all-gather.17.cloned.1.call-update) | async-done | bytes 10616848 | tf_op jit(solution)/shard_map/all_gather | solution.py:680
  1116.6 4.0 copy-done.1
  1120.6 5.5 shard_map.313
  (425 shorter events, 196.5 us)
Async XLA Ops:
  7.2 98.8 %all-gather.7.cloned.1.call-start = ((), (), s32[]{:S(2)}) async-start(), calls=%async_computation | async-start | bytes 5640192 | tf_op jit(solution)/shard_map/all_gather | solution.py:680
  30.3 167.6 %all-gather.9.cloned.1.call-start = ((), (), s32[]{:S(2)}) async-start(), calls=%async_computation.1 | async-start | bytes 5013504 | tf_op jit(solution)/shard_map/all_gather | solution.py:680
  30.6 59.4 %collective-permute-start.3 = (f32[288,1152]{1,0:T(8,128)}, f32[288,1152]{1,0:T(8,128)}, u32[]{:S(2)}, u32[]{:S(2)}) collective-permute-start(f32[288,1152]{1,0:T(8,128)} %get-tuple-element.257), channel_id=1, source_target_pairs={{0,1},{1,0},{2,3},{3,2},{4,5},{5,4},{6,7},{7,6},{8,9},{9,8},{10,11... | collective-permute-start | bytes 3981320 | tf_op jit(solution)/shard_map/ppermute | solution.py:662
  30.8 59.3 %collective-permute-start.4 = (f32[288,1152]{1,0:T(8,128)}, f32[288,1152]{1,0:T(8,128)S(1)}, u32[]{:S(2)}, u32[]{:S(2)}) collective-permute-start(f32[288,1152]{1,0:T(8,128)} %get-tuple-element.258), channel_id=1, source_target_pairs={{0,1},{1,0},{2,3},{3,2},{4,5},{5,4},{6,7},{7,6},{8,9},{9,8},{10,11... | collective-permute-start | bytes 3981320 | tf_op jit(solution)/shard_map/ppermute | solution.py:662
  37.7 52.3 %collective-permute-start.5 = (f32[4,3,576]{2,0,1:T(4,128)S(1)}, f32[4,3,576]{2,0,1:T(4,128)S(1)}, u32[]{:S(2)}, u32[]{:S(2)}) collective-permute-start(f32[4,3,576]{2,0,1:T(4,128)S(1)} %get-tuple-element.531), channel_id=1, source_target_pairs={{0,1},{1,0},{2,3},{3,2},{4,5},{5,4},{6,7},{7,6},{8,9},{9,8},{10,11... | collective-permute-start | bytes 82952 | tf_op jit(solution)/shard_map/ppermute | solution.py:662
  97.8 172.7 %all-gather.11.cloned.1.call-start = ((), (), s32[]{:S(2)}) async-start(), calls=%async_computation.2 | async-start | bytes 6266880 | tf_op jit(solution)/shard_map/all_gather | solution.py:680
  98.4 54.0 %collective-permute-start.7 = (f32[512,1152]{1,0:T(8,128)}, f32[512,1152]{1,0:T(8,128)}, u32[]{:S(2)}, u32[]{:S(2)}) collective-permute-start(f32[512,1152]{1,0:T(8,128)} %constant_dynamic-slice_fusion.31), channel_id=1, source_target_pairs={{0,1},{1,0},{2,3},{3,2},{4,5},{5,4},{6,7},{7,6},{8,9},{9,8},{10,11... | collective-permute-start | bytes 7077896 | tf_op jit(solution)/shard_map/ppermute | solution.py:662
  103.8 41.6 %collective-permute-start.8 = (f32[288,1152]{1,0:T(8,128)}, f32[288,1152]{1,0:T(8,128)}, u32[]{:S(2)}, u32[]{:S(2)}) collective-permute-start(f32[288,1152]{1,0:T(8,128)} %copy-done.42), channel_id=1, source_target_pairs={{0,2},{2,0},{4,6},{6,4},{8,10},{10,8},{12,14},{14,12},{16,18},{18,... | collective-permute-start | bytes 3981320 | tf_op jit(solution)/shard_map/ppermute | solution.py:665
  152.4 38.7 %collective-permute-start.9 = (f32[512,1152]{1,0:T(8,128)}, f32[512,1152]{1,0:T(8,128)}, u32[]{:S(2)}, u32[]{:S(2)}) collective-permute-start(f32[512,1152]{1,0:T(8,128)} %collective-permute-done.7), channel_id=1, source_target_pairs={{0,2},{2,0},{4,6},{6,4},{8,10},{10,8},{12,14},{14,12},{16,18},{18,... | collective-permute-start | bytes 7077896 | tf_op jit(solution)/shard_map/ppermute | solution.py:665
  164.3 850.0 %all-gather.13.cloned.1.call-start = ((), (), s32[]{:S(2)}) async-start(), calls=%async_computation.3 | async-start | bytes 10027008 | tf_op jit(solution)/shard_map/all_gather | solution.py:680
  191.1 67.5 %collective-permute-start.11 = (f32[640,1152]{1,0:T(8,128)S(1)}, f32[640,1152]{1,0:T(8,128)}, u32[]{:S(2)}, u32[]{:S(2)}) collective-permute-start(f32[640,1152]{1,0:T(8,128)S(1)} %constant_dynamic-slice_fusion.29), channel_id=1, source_target_pairs={{0,1},{1,0},{2,3},{3,2},{4,5},{5,4},{6,7},{7,6},{8,9},{9,8},{10,11... | collective-permute-start | bytes 8847368 | tf_op jit(solution)/shard_map/ppermute | solution.py:662
  269.4 74.7 %collective-permute-start.15 = (f32[4,8,16,1152]{3,2,1,0:T(8,128)}, f32[4,8,16,1152]{3,2,1,0:T(8,128)}, u32[]{:S(2)}, u32[]{:S(2)}) collective-permute-start(f32[4,8,16,1152]{3,2,1,0:T(8,128)} %get-tuple-element.313), channel_id=1, source_target_pairs={{0,2},{2,0},{4,6},{6,4},{8,10},{10,8},{12,14},{14,12},{16,18},{18,... | collective-permute-start | bytes 7077896 | tf_op jit(solution)/shard_map/ppermute | solution.py:665
  269.5 77.6 %collective-permute-start.14 = (f32[4,8,16,1152]{3,2,1,0:T(8,128)}, f32[4,8,16,1152]{3,2,1,0:T(8,128)S(1)}, u32[]{:S(2)}, u32[]{:S(2)}) collective-permute-start(f32[4,8,16,1152]{3,2,1,0:T(8,128)} %get-tuple-element.311), channel_id=1, source_target_pairs={{0,2},{2,0},{4,6},{6,4},{8,10},{10,8},{12,14},{14,12},{16,18},{18,... | collective-permute-start | bytes 7077896 | tf_op jit(solution)/shard_map/ppermute | solution.py:665
  348.8 67.4 %collective-permute-start.16 = (f32[5,8,16,1152]{3,2,1,0:T(8,128)}, f32[5,8,16,1152]{3,2,1,0:T(8,128)}, u32[]{:S(2)}, u32[]{:S(2)}) collective-permute-start(f32[5,8,16,1152]{3,2,1,0:T(8,128)} %get-tuple-element.324), channel_id=1, source_target_pairs={{0,2},{2,0},{4,6},{6,4},{8,10},{10,8},{12,14},{14,12},{16,18},{18,... | collective-permute-start | bytes 8847368 | tf_op jit(solution)/shard_map/ppermute | solution.py:665
  349.0 72.0 %collective-permute-start.17 = (f32[5,8,16,1152]{3,2,1,0:T(8,128)}, f32[5,8,16,1152]{3,2,1,0:T(8,128)}, u32[]{:S(2)}, u32[]{:S(2)}) collective-permute-start(f32[5,8,16,1152]{3,2,1,0:T(8,128)} %get-tuple-element.326), channel_id=1, source_target_pairs={{0,2},{2,0},{4,6},{6,4},{8,10},{10,8},{12,14},{14,12},{16,18},{18,... | collective-permute-start | bytes 8847368 | tf_op jit(solution)/shard_map/ppermute | solution.py:665
  349.4 74.4 %collective-permute-start.18 = (f32[4,8,16,1152]{3,2,1,0:T(8,128)}, f32[4,8,16,1152]{3,2,1,0:T(8,128)}, u32[]{:S(2)}, u32[]{:S(2)}) collective-permute-start(f32[4,8,16,1152]{3,2,1,0:T(8,128)} %add.1242), channel_id=1, source_target_pairs={{0,1},{1,0},{2,3},{3,2},{4,5},{5,4},{6,7},{7,6},{8,9},{9,8},{10,11... | collective-permute-start | bytes 7077896 | tf_op jit(solution)/shard_map/ppermute | solution.py:662
  350.7 73.1 %collective-permute-start.19 = (f32[4,4,16,1152]{3,2,1,0:T(8,128)}, f32[4,4,16,1152]{3,2,1,0:T(8,128)}, u32[]{:S(2)}, u32[]{:S(2)}) collective-permute-start(f32[4,4,16,1152]{3,2,1,0:T(8,128)} %fusion.11), channel_id=1, source_target_pairs={{0,4},{2,6},{4,0},{6,2},{8,12},{10,14},{12,8},{14,10},{16,20},{18,... | collective-permute-start | bytes 3538952 | tf_op jit(solution)/shard_map/ppermute | solution.py:665
  423.7 81.5 %collective-permute-start.21 = (f32[5,8,16,1152]{3,2,1,0:T(8,128)}, f32[5,8,16,1152]{3,2,1,0:T(8,128)}, u32[]{:S(2)}, u32[]{:S(2)}) collective-permute-start(f32[5,8,16,1152]{3,2,1,0:T(8,128)} %add.1246), channel_id=1, source_target_pairs={{0,1},{1,0},{2,3},{3,2},{4,5},{5,4},{6,7},{7,6},{8,9},{9,8},{10,11... | collective-permute-start | bytes 8847368 | tf_op jit(solution)/shard_map/ppermute | solution.py:662
  423.9 78.7 %collective-permute-start.20 = (f32[4,8,16,1152]{3,2,1,0:T(8,128)}, f32[4,8,16,1152]{3,2,1,0:T(8,128)}, u32[]{:S(2)}, u32[]{:S(2)}) collective-permute-start(f32[4,8,16,1152]{3,2,1,0:T(8,128)} %get-tuple-element.339), channel_id=1, source_target_pairs={{0,2},{2,0},{4,6},{6,4},{8,10},{10,8},{12,14},{14,12},{16,18},{18,... | collective-permute-start | bytes 7077896 | tf_op jit(solution)/shard_map/ppermute | solution.py:665
  423.9 90.2 %collective-permute-start.22 = (f32[4,8,16,1152]{3,2,1,0:T(8,128)}, f32[4,8,16,1152]{3,2,1,0:T(8,128)}, u32[]{:S(2)}, u32[]{:S(2)}) collective-permute-start(f32[4,8,16,1152]{3,2,1,0:T(8,128)} %get-tuple-element.363), channel_id=1, source_target_pairs={{0,2},{2,0},{4,6},{6,4},{8,10},{10,8},{12,14},{14,12},{16,18},{18,... | collective-permute-start | bytes 7077896 | tf_op jit(solution)/shard_map/ppermute | solution.py:665
  424.4 83.8 %collective-permute-start.23 = (f32[5,4,16,1152]{3,2,1,0:T(8,128)}, f32[5,4,16,1152]{3,2,1,0:T(8,128)}, u32[]{:S(2)}, u32[]{:S(2)}) collective-permute-start(f32[5,4,16,1152]{3,2,1,0:T(8,128)} %fusion.8), channel_id=1, source_target_pairs={{0,4},{2,6},{4,0},{6,2},{8,12},{10,14},{12,8},{14,10},{16,20},{18,... | collective-permute-start | bytes 4423688 | tf_op jit(solution)/shard_map/ppermute | solution.py:665
  505.3 83.5 %collective-permute-start.28 = (f32[5,8,16,1152]{3,2,1,0:T(8,128)}, f32[5,8,16,1152]{3,2,1,0:T(8,128)}, u32[]{:S(2)}, u32[]{:S(2)}) collective-permute-start(f32[5,8,16,1152]{3,2,1,0:T(8,128)} %get-tuple-element.377), channel_id=1, source_target_pairs={{0,2},{2,0},{4,6},{6,4},{8,10},{10,8},{12,14},{14,12},{16,18},{18,... | collective-permute-start | bytes 8847368 | tf_op jit(solution)/shard_map/ppermute | solution.py:665
  505.4 41.5 %collective-permute-start.24 = (f32[4,4,16,1152]{3,2,1,0:T(8,128)}, f32[4,4,16,1152]{3,2,1,0:T(8,128)}, u32[]{:S(2)}, u32[]{:S(2)}) collective-permute-start(f32[4,4,16,1152]{3,2,1,0:T(8,128)} %fusion.10), channel_id=1, source_target_pairs={{0,4},{2,6},{4,0},{6,2},{8,12},{10,14},{12,8},{14,10},{16,20},{18,... | collective-permute-start | bytes 3538952 | tf_op jit(solution)/shard_map/ppermute | solution.py:665
  506.4 40.5 %collective-permute-start.25 = (f32[4,4,16,1152]{3,2,1,0:T(8,128)}, f32[4,4,16,1152]{3,2,1,0:T(8,128)}, u32[]{:S(2)}, u32[]{:S(2)}) collective-permute-start(f32[4,4,16,1152]{3,2,1,0:T(8,128)} %add_add_fusion), channel_id=1, source_target_pairs={{0,1},{1,0},{2,3},{3,2},{4,5},{5,4},{6,7},{7,6},{8,9},{9,8},{10,11... | collective-permute-start | bytes 3538952 | tf_op jit(solution)/shard_map/ppermute | solution.py:662
  508.3 91.5 %collective-permute-start.31 = (f32[5,8,16,1152]{3,2,1,0:T(8,128)}, f32[5,8,16,1152]{3,2,1,0:T(8,128)}, u32[]{:S(2)}, u32[]{:S(2)}) collective-permute-start(f32[5,8,16,1152]{3,2,1,0:T(8,128)} %get-tuple-element.388), channel_id=1, source_target_pairs={{0,2},{2,0},{4,6},{6,4},{8,10},{10,8},{12,14},{14,12},{16,18},{18,... | collective-permute-start | bytes 8847368 | tf_op jit(solution)/shard_map/ppermute | solution.py:665
  549.3 36.7 %collective-permute-start.26 = (f32[4,4,16,1152]{3,2,1,0:T(8,128)}, f32[4,4,16,1152]{3,2,1,0:T(8,128)}, u32[]{:S(2)}, u32[]{:S(2)}) collective-permute-start(f32[4,4,16,1152]{3,2,1,0:T(8,128)} %get-tuple-element.374), channel_id=1, source_target_pairs={{0,4},{2,6},{4,0},{6,2},{8,12},{10,14},{12,8},{14,10},{16,20},{18,... | collective-permute-start | bytes 3538952 | tf_op jit(solution)/shard_map/ppermute | solution.py:665
  549.7 43.5 %collective-permute-start.29 = (f32[5,4,16,1152]{3,2,1,0:T(8,128)}, f32[5,4,16,1152]{3,2,1,0:T(8,128)}, u32[]{:S(2)}, u32[]{:S(2)}) collective-permute-start(f32[5,4,16,1152]{3,2,1,0:T(8,128)} %bitcast_add_fusion.3), channel_id=1, source_target_pairs={{0,1},{1,0},{2,3},{3,2},{4,5},{5,4},{6,7},{7,6},{8,9},{9,8},{10,11... | collective-permute-start | bytes 4423688 | tf_op jit(solution)/shard_map/ppermute | solution.py:662
  593.2 43.2 %collective-permute-start.32 = (f32[5,4,16,1152]{3,2,1,0:T(8,128)}, f32[5,4,16,1152]{3,2,1,0:T(8,128)}, u32[]{:S(2)}, u32[]{:S(2)}) collective-permute-start(f32[5,4,16,1152]{3,2,1,0:T(8,128)} %fusion.7), channel_id=1, source_target_pairs={{0,4},{2,6},{4,0},{6,2},{8,12},{10,14},{12,8},{14,10},{16,20},{18,... | collective-permute-start | bytes 4423688 | tf_op jit(solution)/shard_map/ppermute | solution.py:665
  596.5 36.8 %collective-permute-start.33 = (f32[4,1,16,1152]{3,2,0,1:T(8,128)}, f32[4,1,16,1152]{3,2,0,1:T(8,128)S(1)}, u32[]{:S(2)}, u32[]{:S(2)}) collective-permute-start(f32[4,1,16,1152]{3,2,0,1:T(8,128)} %fusion.46), channel_id=1, source_target_pairs={{0,16},{2,18},{4,20},{6,22},{8,24},{10,26},{12,28},{14,30},{16,0},... | collective-permute-start | bytes 884744 | tf_op jit(solution)/shard_map/ppermute | solution.py:665
  599.3 35.5 %collective-permute-start.30 = (f32[4,2,16,1152]{3,2,0,1:T(8,128)}, f32[4,2,16,1152]{3,2,0,1:T(8,128)S(1)}, u32[]{:S(2)}, u32[]{:S(2)}) collective-permute-start(f32[4,2,16,1152]{3,2,0,1:T(8,128)} %fusion.17), channel_id=1, source_target_pairs={{0,8},{2,10},{4,12},{6,14},{8,0},{10,2},{12,4},{14,6},{16,24},{18,... | collective-permute-start | bytes 1769480 | tf_op jit(solution)/shard_map/ppermute | solution.py:665
  638.7 42.5 %collective-permute-start.34 = (f32[16,72,1152]{2,1,0:T(8,128)}, f32[16,72,1152]{2,1,0:T(8,128)}, u32[]{:S(2)}, u32[]{:S(2)}) collective-permute-start(f32[16,72,1152]{2,1,0:T(8,128)} %get-tuple-element.398), channel_id=1, source_target_pairs={{0,2},{2,0},{4,6},{6,4},{8,10},{10,8},{12,14},{14,12},{16,18},{18,... | collective-permute-start | bytes 15925256 | tf_op jit(solution)/shard_map/ppermute | solution.py:665
  638.7 39.2 %collective-permute-start.36 = (f32[5,4,16,1152]{3,2,1,0:T(8,128)}, f32[5,4,16,1152]{3,2,1,0:T(8,128)}, u32[]{:S(2)}, u32[]{:S(2)}) collective-permute-start(f32[5,4,16,1152]{3,2,1,0:T(8,128)} %get-tuple-element.401), channel_id=1, source_target_pairs={{0,4},{2,6},{4,0},{6,2},{8,12},{10,14},{12,8},{14,10},{16,20},{18,... | collective-permute-start | bytes 4423688 | tf_op jit(solution)/shard_map/ppermute | solution.py:665
  639.0 34.3 %collective-permute-start.35 = (f32[4,1,16,1152]{3,2,0,1:T(8,128)S(1)}, f32[4,1,16,1152]{3,2,0,1:T(8,128)}, u32[]{:S(2)}, u32[]{:S(2)}) collective-permute-start(f32[4,1,16,1152]{3,2,0,1:T(8,128)S(1)} %fusion.44), channel_id=1, source_target_pairs={{0,16},{2,18},{4,20},{6,22},{8,24},{10,26},{12,28},{14,30},{16,0},... | collective-permute-start | bytes 884744 | tf_op jit(solution)/shard_map/ppermute | solution.py:665
  639.7 36.0 %collective-permute-start.37 = (f32[5,2,16,1152]{3,2,0,1:T(8,128)}, f32[5,2,16,1152]{3,2,0,1:T(8,128)S(1)}, u32[]{:S(2)}, u32[]{:S(2)}) collective-permute-start(f32[5,2,16,1152]{3,2,0,1:T(8,128)} %fusion.15), channel_id=1, source_target_pairs={{0,8},{2,10},{4,12},{6,14},{8,0},{10,2},{12,4},{14,6},{16,24},{18,... | collective-permute-start | bytes 2211848 | tf_op jit(solution)/shard_map/ppermute | solution.py:665
  689.3 325.0 %all-gather.15.cloned.1.call-start = ((), (), s32[]{:S(2)}) async-start(), calls=%async_computation.4 | async-start | bytes 12533760 | tf_op jit(solution)/shard_map/all_gather | solution.py:680
  691.6 38.3 %collective-permute-start.41 = (f32[5,2,16,1152]{3,2,0,1:T(8,128)}, f32[5,2,16,1152]{3,2,0,1:T(8,128)}, u32[]{:S(2)}, u32[]{:S(2)}) collective-permute-start(f32[5,2,16,1152]{3,2,0,1:T(8,128)} %fusion.14), channel_id=1, source_target_pairs={{0,8},{2,10},{4,12},{6,14},{8,0},{10,2},{12,4},{14,6},{16,24},{18,... | collective-permute-start | bytes 2211848 | tf_op jit(solution)/shard_map/ppermute | solution.py:665
  692.2 40.1 %collective-permute-start.40 = (f32[4,72,1152]{2,1,0:T(8,128)}, f32[4,72,1152]{2,1,0:T(8,128)}, u32[]{:S(2)}, u32[]{:S(2)}) collective-permute-start(f32[4,72,1152]{2,1,0:T(8,128)} %fusion.9), channel_id=1, source_target_pairs={{0,4},{2,6},{4,0},{6,2},{8,12},{10,14},{12,8},{14,10},{16,20},{18,... | collective-permute-start | bytes 3981320 | tf_op jit(solution)/shard_map/ppermute | solution.py:665
  746.4 104.9 %collective-permute-start.45 = (f32[8,72,1152]{2,1,0:T(8,128)}, f32[8,72,1152]{2,1,0:T(8,128)}, u32[]{:S(2)}, u32[]{:S(2)}) collective-permute-start(f32[8,72,1152]{2,1,0:T(8,128)} %get-tuple-element.427), channel_id=1, source_target_pairs={{0,2},{2,0},{4,6},{6,4},{8,10},{10,8},{12,14},{14,12},{16,18},{18,... | collective-permute-start | bytes 7962632 | tf_op jit(solution)/shard_map/ppermute | solution.py:665
  746.4 40.9 %collective-permute-start.48 = (f32[5,1,16,1152]{3,2,0,1:T(8,128)}, f32[5,1,16,1152]{3,2,0,1:T(8,128)}, u32[]{:S(2)}, u32[]{:S(2)}) collective-permute-start(f32[5,1,16,1152]{3,2,0,1:T(8,128)} %fusion.30), channel_id=1, source_target_pairs={{0,16},{2,18},{4,20},{6,22},{8,24},{10,26},{12,28},{14,30},{16,0},... | collective-permute-start | bytes 1105928 | tf_op jit(solution)/shard_map/ppermute | solution.py:665
  749.2 66.3 %collective-permute-start.50 = (f32[16,1729]{1,0:T(8,128)S(1)}, f32[16,1729]{1,0:T(8,128)S(1)}, u32[]{:S(2)}, u32[]{:S(2)}) collective-permute-start(f32[16,1729]{1,0:T(8,128)S(1)} %pad_maximum_fusion.11), channel_id=1, source_target_pairs={{0,4},{2,6},{4,0},{6,2},{8,12},{10,14},{12,8},{14,10},{16,20},{18,... | collective-permute-start | bytes 331976 | tf_op jit(solution)/shard_map/ppermute | solution.py:665
  789.0 62.3 %collective-permute-start.44 = (f32[4,72,1152]{2,1,0:T(8,128)}, f32[4,72,1152]{2,1,0:T(8,128)}, u32[]{:S(2)}, u32[]{:S(2)}) collective-permute-start(f32[4,72,1152]{2,1,0:T(8,128)} %get-tuple-element.425), channel_id=1, source_target_pairs={{0,1},{1,0},{2,3},{3,2},{4,5},{5,4},{6,7},{7,6},{8,9},{9,8},{10,11... | collective-permute-start | bytes 3981320 | tf_op jit(solution)/shard_map/ppermute | solution.py:662
  851.3 265.2 %all-gather.17.cloned.1.call-start = ((), (), s32[]{:S(2)}) async-start(), calls=%async_computation.5 | async-start | bytes 11280384 | tf_op jit(solution)/shard_map/all_gather | solution.py:680
  858.4 48.2 %collective-permute-start.51 = (f32[4,72,1152]{2,1,0:T(8,128)}, f32[4,72,1152]{2,1,0:T(8,128)}, u32[]{:S(2)}, u32[]{:S(2)}) collective-permute-start(f32[4,72,1152]{2,1,0:T(8,128)} %get-tuple-element.444), channel_id=1, source_target_pairs={{0,4},{2,6},{4,0},{6,2},{8,12},{10,14},{12,8},{14,10},{16,20},{18,... | collective-permute-start | bytes 3981320 | tf_op jit(solution)/shard_map/ppermute | solution.py:665
  863.9 40.6 %collective-permute-start.52 = (f32[2,72,1152]{2,1,0:T(8,128)}, f32[2,72,1152]{2,1,0:T(8,128)}, u32[]{:S(2)}, u32[]{:S(2)}) collective-permute-start(f32[2,72,1152]{2,1,0:T(8,128)} %add_bitcast_fusion.5), channel_id=1, source_target_pairs={{0,8},{2,10},{4,12},{6,14},{8,0},{10,2},{12,4},{14,6},{16,24},{18,... | collective-permute-start | bytes 1990664 | tf_op jit(solution)/shard_map/ppermute | solution.py:665
  916.5 45.0 %collective-permute-start.57 = (f32[1,72,1152]{2,1,0:T(8,128)}, f32[1,72,1152]{2,1,0:T(8,128)}, u32[]{:S(2)}, u32[]{:S(2)}) collective-permute-start(f32[1,72,1152]{2,1,0:T(8,128)} %bitcast_add_fusion.17), channel_id=1, source_target_pairs={{0,16},{2,18},{4,20},{6,22},{8,24},{10,26},{12,28},{14,30},{16,0},... | collective-permute-start | bytes 995336 | tf_op jit(solution)/shard_map/ppermute | solution.py:665
  917.6 73.3 %collective-permute-start.55 = (f32[64,1729]{1,0:T(8,128)}, f32[64,1729]{1,0:T(8,128)}, u32[]{:S(2)}, u32[]{:S(2)}) collective-permute-start(f32[64,1729]{1,0:T(8,128)} %copy.469), channel_id=1, source_target_pairs={{0,16},{2,18},{4,20},{6,22},{8,24},{10,26},{12,28},{14,30},{16,0},... | collective-permute-start | bytes 1327880 | tf_op jit(solution)/shard_map/ppermute | solution.py:665
  920.5 72.1 %collective-permute-start.54 = (f32[2,72,1152]{2,1,0:T(8,128)}, f32[2,72,1152]{2,1,0:T(8,128)}, u32[]{:S(2)}, u32[]{:S(2)}) collective-permute-start(f32[2,72,1152]{2,1,0:T(8,128)} %add_bitcast_fusion.4), channel_id=1, source_target_pairs={{0,8},{2,10},{4,12},{6,14},{8,0},{10,2},{12,4},{14,6},{16,24},{18,... | collective-permute-start | bytes 1990664 | tf_op jit(solution)/shard_map/ppermute | solution.py:665
  1060.3 41.0 %collective-permute-start.62 = (f32[792,128]{1,0:T(8,128)S(1)}, f32[792,128]{1,0:T(8,128)S(1)}, u32[]{:S(2)}, u32[]{:S(2)}) collective-permute-start(f32[792,128]{1,0:T(8,128)S(1)} %add.1374), channel_id=1, source_target_pairs={{0,16},{2,18},{4,20},{6,22},{8,24},{10,26},{12,28},{14,30},{16,0},... | collective-permute-start | bytes 1216520 | tf_op jit(solution)/shard_map/ppermute | solution.py:665
  (97 other events, 1688.2 us)
Sparse Core Ops, SparseCore 0:
  30.5 56.9 all-gather.6
  97.9 53.7 all-gather.8
  164.4 60.0 all-gather.10
  689.4 103.5 all-gather.12
  851.5 144.2 all-gather.14
  1014.5 102.0 all-gather.16

commit v5 on v3

--- a/solution.py
+++ b/solution.py
@@ -788,31 +788,31 @@
         hidden_shares = [ring.share(hidden_weight, dim, first * BLOCK, blocks * BLOCK) for first, blocks in cuts]
         qk = ring.across(ring.share(attend_own, 2 * width, 0, dim))
         values_half = ring.core_half(attend_own, 2 * width, width)
-        qk, table_other, bias_other, values_half, time_proj, strips_own = join(
-            qk, table_other, bias_other, values_half, time_proj, make_strips(bias_table)
+        output_half = ring.core_half(output_weight, 0, width)
+        qk, table_other, bias_other, values_half, output_half, time_proj, strips_own = join(
+            qk, table_other, bias_other, values_half, output_half, time_proj, make_strips(bias_table)
         )
         attend_qk = ring.spread(qk)
         values_mine = ring.across(values_half)
-        hidden_share = ring.across(hidden_shares[0])
+        output_mine = ring.across(output_half)
         time_mine = lax.dynamic_slice_in_dim(time_proj, first_own, own_images, 0)
         time_theirs = lax.dynamic_slice_in_dim(time_proj, (1 - rank) * own_images, own_images, 0)
         time_other = ring.across(time_theirs)
         own = attend_forward(tokens2, *norm_first, attend_own, times_of(time_mine), strips_own)
         return_halves = [ring.core_half(return_weight, first * BLOCK, blocks * BLOCK) for first, blocks in cuts]
-        own, values_mine, time_other, return_half, output_half, hidden_share, share_2 = join(
-            own, values_mine, time_other, return_halves[0], ring.core_half(output_weight, 0, width), hidden_share,
-            hidden_shares[1],
-        )
-        output_mine = ring.across(output_half)
-        hidden_other = [ring.spread(hidden_share), ring.spread(ring.across(share_2))]
+        own, values_mine, output_mine, time_other, return_half, share_1, share_2 = join(
+            own, values_mine, output_mine, time_other, return_halves[0], *hidden_shares
+        )
+        hidden_other = [ring.spread(ring.across(share_1)), ring.spread(ring.across(share_2))]
+        output_theirs = ring.along(output_mine, 0)
         strips_other = make_strips(table_other)
         values_full = ring.ordered(values_mine, ring.along(values_mine, 0), 0)
         attend_other = jnp.concatenate([attend_qk, values_full], 0)
         return_mine = ring.across(return_half)
         other = attend_forward(tokens2, *norm_first, attend_other, times_of(time_other), strips_other)
         attend = [attend_own, attend_other]
-        other, return_mine, output_mine = join(other, return_mine, output_mine)
-        output_other = ring.ordered(output_mine, ring.along(output_mine, 0), 0)
+        other, return_mine, output_mine, output_theirs = join(other, return_mine, output_mine, output_theirs)
+        output_other = ring.ordered(output_mine, output_theirs, 0)
         return_theirs = ring.along(return_mine, 0)
         output = [output_weight, output_other]
         middle, *forms = output_forward(

time: 1110 us -> 1100 us (level)
  transfers between devices with their start and end apart: 70 -> 70, of which waited for: 16 -> 17; matrix products, arithmetic and copies ran while one was open for 18% -> 18% of each run, Pallas kernels for 52% -> 53%
where the time goes in v5:
time: 1100 us; the launch traced here: 1090 us
  Pallas kernels  580 us (53%)
  waiting for transfers between devices  230 us (21%)
  other arithmetic  111 us (10%)
  local copies, waits for them, and re-layouts  77.1 us (7%)
  starting transfers between devices  53 us (5%)
  matrix products  25 us (2%)
  between operations  16.4 us (1%)
    pallas_call x4, Pallas kernels, feed(): pl.pallas_call(functools.partial(feed_kernel, split), grid=(blocks,), in_...  269 us
    ppermute x45, waiting for transfers between devices, along(): return lax.ppermute(value, 'dp', [(i, i ^ 1 << bit) for i in range(16)])  176 us
    pallas_call x2, Pallas kernels, attend_forward(): pl.pallas_call(functools.partial(attend_forward_kernel, heads), grid=(ima...  66.1 us
    pallas_call x4, Pallas kernels, attend_weights(): pl.pallas_call(functools.partial(attend_weights_kernel, split, steps), gr...  63.3 us
    pallas_call x2, Pallas kernels, attend_backward(): pl.pallas_call(functools.partial(attend_backward_kernel, heads), grid=(im...  61.1 us
    pallas_call x2, Pallas kernels, first_backward(): pl.pallas_call(functools.partial(first_kernel, parts, len(previous) > 0),...  50.8 us
    ppermute x19, waiting for transfers between devices, across(): return lax.ppermute(value, 'mp', [(0, 1), (1, 0)])  38.4 us
    add x17, other arithmetic, send(): out = out + pick(cut, 1 - bit, axis + 1)  35.2 us
  transfers between devices with their start and end apart: 70, of which 17 were waited for; matrix products, arithmetic and copies ran while one was open for 18% of the time, Pallas kernels for 53%

profile of v5, /device:TPU:0, one launch (start us, length us, event | category | flops | bytes accessed | tf_op | source)
XLA Modules:
  0.0 1091.9 jit_solution(7135564100953742457)
XLA Ops:
  15.9 6.8 fusion.2
  34.7 3.2 constant_dynamic-slice_fusion.31
  41.0 33.0 %shard_map.297 = (f32[1024,576]{1,0:T(8,128)}, f32[1024,576]{1,0:T(8,128)}, f32[1024,576]{1,0:T(8,128)}, f32[1024,576]{1,0:T(8,128)}, f32[576,1024]{1,0:T(8,128)...) custom-call(f32[1024,1152]{1,0:T(8,128)} %bitcast.386, f32[1,1152]{1,0:T(1,128)} %reshape.1151.gain_ref.refs_2_.refs_3_, ...), custom_call_target="tpu_custom_call" | custom-call | flops 18673040 | bytes 22118 | tf_op jit(solution)/shard_map/pallas_call | solution.py:142
  74.1 16.2 %collective-permute-done.5 = f32[4,3,576]{2,0,1:T(4,128)S(1)} collective-permute-done((f32[4,3,576]{2,0,1:T(4,128)S(1)}, f32[4,3,576]{2,0,1:T(4,128)S(1)}, u32[]{:S(2)}, u32[]{:S(2)}) %collective-permute-start.5) | collective-permute-done | bytes 27680 | tf_op jit(solution)/shard_map/ppermute | solution.py:662
  90.7 6.6 collective-permute-done.10
  105.9 6.4 pad_maximum_fusion.weight_ref.refs_6_.refs_7_
  112.3 33.1 %shard_map.298 = (f32[1024,576]{1,0:T(8,128)}, f32[1024,576]{1,0:T(8,128)}, f32[1024,576]{1,0:T(8,128)}, f32[1024,576]{1,0:T(8,128)}, f32[576,1024]{1,0:T(8,128)...) custom-call(f32[1024,1152]{1,0:T(8,128)} %bitcast.387, f32[1,1152]{1,0:T(1,128)} %reshape.1151.gain_ref.refs_2_.refs_3_, ...), custom_call_target="tpu_custom_call" | custom-call | flops 18673040 | bytes 22118 | tf_op jit(solution)/shard_map/pallas_call | solution.py:142
  145.4 6.9 collective-permute-done.7
  156.3 7.9 collective-permute-done.13
  170.1 21.2 %shard_map.299 = (f32[1024,1152]{1,0:T(8,128)}, bf16[1024,2304]{1,0:T(8,128)(2,1)}, bf16[1024,2304]{1,0:T(8,128)(2,1)}) custom-call(f32[4]{0:T(128)S(1)} %compare_convert_fusion.refs_0_, f32[1024,1152]{1,0:T(8,128)} %bitcast.388, f32[1024,1152]{1,0:T(8,128)} %bitcast.396, f32[1024,576]{1,0:T(8,128)S(1)} %copy-done.2, f32[1024,576]{1,0:T(8,128)S(1)} %copy-done.3, ...), custom_call_target="tpu_custom_call" | custom-call | flops 8153726 | bytes 28901 | tf_op jit(solution)/shard_map/pallas_call | solution.py:188
  192.4 3.4 broadcast_select_fusion.3
  198.3 60.6 %shard_map.300 = (f32[1024,1152]{1,0:T(8,128)}, f32[1024,1152]{1,0:T(8,128)}, f32[1,1024]{1,0:T(1,128)}, f32[4,8,16,1152]{3,2,1,0:T(8,128)}, f32[4,8,16,1152]{3,...) custom-call(s32[1]{0:T(128)} %bitcast.14.core_ref, ...), custom_call_target="tpu_custom_call" | custom-call | flops 43486544 | bytes 42467 | tf_op jit(solution)/shard_map/pallas_call | solution.py:305
  259.0 5.6 collective-permute-done.12
  270.8 73.4 %shard_map.301 = (f32[1024,1152]{1,0:T(8,128)}, f32[1024,1152]{1,0:T(8,128)}, f32[1,1280]{1,0:T(1,128)}, f32[5,8,16,1152]{3,2,1,0:T(8,128)}, f32[5,8,16,1152]{3,...) custom-call(s32[1]{0:T(128)} %bitcast.14.core_ref, ...), custom_call_target="tpu_custom_call" | custom-call | flops 54358180 | bytes 47185 | tf_op jit(solution)/shard_map/pallas_call | solution.py:305
  354.3 61.0 %shard_map.302 = (f32[1024,1152]{1,0:T(8,128)}, f32[1024,1152]{1,0:T(8,128)}, f32[1,1024]{1,0:T(1,128)}, f32[4,8,16,1152]{3,2,1,0:T(8,128)}, f32[4,8,16,1152]{3,...) custom-call(s32[1]{0:T(128)} %bitcast.14.core_ref, ...), custom_call_target="tpu_custom_call" | custom-call | flops 43486544 | bytes 42467 | tf_op jit(solution)/shard_map/pallas_call | solution.py:305
  416.7 4.9 add.1246
  426.5 73.6 %shard_map.303 = (f32[1024,1152]{1,0:T(8,128)}, f32[1024,1152]{1,0:T(8,128)}, f32[1,1280]{1,0:T(1,128)}, f32[5,8,16,1152]{3,2,1,0:T(8,128)}, f32[5,8,16,1152]{3,...) custom-call(s32[1]{0:T(128)} %bitcast.14.core_ref, ...), custom_call_target="tpu_custom_call" | custom-call | flops 54358180 | bytes 47185 | tf_op jit(solution)/shard_map/pallas_call | solution.py:305
  509.6 3.4 bitcast_add_fusion.3
  515.5 4.3 constant_dynamic-slice_fusion.21
  519.9 28.4 %shard_map.304 = (f32[1024,1152]{1,0:T(8,128)}, f32[1024,1152]{1,0:T(8,128)}, f32[8,1152]{1,0:T(8,128)}, f32[1024,576]{1,0:T(8,128)}, f32[1024,576]{1,0:T(8,128)}) custom-call(f32[4]{0:T(128)} %copy-done.6, f32[1024,1152]{1,0:T(8,128)} %get-tuple-element.344.refs_1_, f32[1024,1152]{1,0:T(8,128)} %bitcast.397, f32[1,1152]{1,0:T(1,128)} %copy-done.5, ...), custom_call_target="tpu_custom_call" | custom-call | flops 8153726 | bytes 47775 | tf_op jit(solution)/shard_map/pallas_call | solution.py:366
  552.2 30.7 %shard_map.305 = (f32[1024,1728]{1,0:T(8,128)}, f32[1728,1024]{1,0:T(8,128)}, f32[8,16,512]{2,1,0:T(8,128)}, f32[4,1,1728]{2,1,0:T(1,128)}) custom-call(f32[1024,576]{1,0:T(8,128)} %get-tuple-element.358.query_ref, f32[1024,576]{1,0:T(8,128)} %get-tuple-element.359.keys_ref, f32[1024,576]{1,0:T(8,128)} %get-tuple-element.360.values_ref, ...), custom_call_target="tpu_custom_call" | custom-call | flops 16106127 | bytes 21233 | tf_op jit(solution)/shard_map/pallas_call | solution.py:437
  588.3 3.3 fusion.7
  591.6 14.6 %shard_map.306 = (f32[8,72,1152]{2,1,0:T(8,128)}, f32[8,72,1152]{2,1,0:T(8,128)}) custom-call(s32[1]{0:T(128)} %bitcast.14.core_ref, f32[1728,1024]{1,0:T(8,128)} %get-tuple-element.380.refs_0_, f32[1024,1152]{1,0:T(8,128)} %get-tuple-element.415.refs_1_.refs_2_), custom_call_target="tpu_custom_call" | custom-call | flops 8153726 | bytes 19464 | tf_op jit(solution)/shard_map/pallas_call | solution.py:503
  614.5 4.1 constant_dynamic-slice_fusion.3
  621.2 16.7 %shard_map.307 = (f32[8,72,1152]{2,1,0:T(8,128)}, f32[8,72,1152]{2,1,0:T(8,128)}) custom-call(s32[1]{0:T(128)} %bitcast.14.core_ref, f32[1728,1024]{1,0:T(8,128)} %get-tuple-element.380.refs_0_, f32[576,1024]{1,0:T(8,128)} %get-tuple-element.381.refs_1_, f32[1024,1152]{1,0:T(8,128)} %get-tuple-element.415.refs_1_.refs_2_, ...), custom_call_target="tpu_custom_call" | custom-call | flops 8153726 | bytes 19464 | tf_op jit(solution)/shard_map/pallas_call | solution.py:503
  657.5 30.3 %shard_map.308 = (f32[1024,1728]{1,0:T(8,128)}, f32[1728,1024]{1,0:T(8,128)}, f32[8,16,512]{2,1,0:T(8,128)}, f32[4,1,1728]{2,1,0:T(1,128)}) custom-call(f32[1024,576]{1,0:T(8,128)} %get-tuple-element.355.query_ref, f32[1024,576]{1,0:T(8,128)} %get-tuple-element.356.keys_ref, f32[1024,576]{1,0:T(8,128)} %get-tuple-element.357.values_ref, ...), custom_call_target="tpu_custom_call" | custom-call | flops 16106127 | bytes 21233 | tf_op jit(solution)/shard_map/pallas_call | solution.py:437
  699.6 17.3 %shard_map.309 = (f32[8,72,1152]{2,1,0:T(8,128)}, f32[8,72,1152]{2,1,0:T(8,128)}) custom-call(s32[1]{0:T(128)} %bitcast.14.core_ref, f32[1728,1024]{1,0:T(8,128)} %get-tuple-element.410.refs_0_, f32[576,1024]{1,0:T(8,128)} %get-tuple-element.411.refs_1_, f32[1024,1152]{1,0:T(8,128)} %get-tuple-element.415.refs_1_.refs_2_, ...), custom_call_target="tpu_custom_call" | custom-call | flops 8153726 | bytes 19464 | tf_op jit(solution)/shard_map/pallas_call | solution.py:503
  719.4 14.6 %shard_map.310 = (f32[8,72,1152]{2,1,0:T(8,128)}, f32[8,72,1152]{2,1,0:T(8,128)}) custom-call(s32[1]{0:T(128)} %bitcast.14.core_ref, f32[1728,1024]{1,0:T(8,128)} %get-tuple-element.410.refs_0_, f32[1024,1152]{1,0:T(8,128)} %get-tuple-element.415.refs_1_.refs_2_), custom_call_target="tpu_custom_call" | custom-call | flops 8153726 | bytes 19464 | tf_op jit(solution)/shard_map/pallas_call | solution.py:503
  736.1 19.7 %collective-permute-done.43 = f32[5,2,16,1152]{3,2,0,1:T(8,128)} collective-permute-done((f32[5,2,16,1152]{3,2,0,1:T(8,128)}, f32[5,2,16,1152]{3,2,0,1:T(8,128)}, u32[]{:S(2)}, u32[]{:S(2)}) %collective-permute-start.43) | collective-permute-done | bytes 737312 | tf_op jit(solution)/shard_map/ppermute | solution.py:665
  761.3 3.8 constant_dynamic-slice_fusion.15
  776.4 25.2 %shard_map.311 = (f32[1024,1152]{1,0:T(8,128)}, f32[8,1152]{1,0:T(8,128)}) custom-call(f32[1024,1152]{1,0:T(8,128)} %bitcast.389, f32[1024,1152]{1,0:T(8,128)} %get-tuple-element.354.refs_3_.refs_1_.refs_2_, f32[1,1152]{1,0:T(1,128)} %reshape.1151.gain_ref.refs_2_.refs_3_, f32[1024,1728]{1,0:T(8,128)} %get-tuple-element.440.refs_3_.refs_4_, ...), custom_call_target="tpu_custom_call" | custom-call | flops 12230590 | bytes 30081 | tf_op jit(solution)/shard_map/pallas_call | solution.py:544
  801.7 4.2 collective-permute-done.50
  810.9 4.4 constant_dynamic-slice_fusion.6
  821.0 25.6 %shard_map.312 = (f32[1024,1152]{1,0:T(8,128)}, f32[8,1152]{1,0:T(8,128)}) custom-call(f32[1024,1152]{1,0:T(8,128)} %get-tuple-element.439.refs_0_, f32[1024,1152]{1,0:T(8,128)} %bitcast.390, f32[1024,1152]{1,0:T(8,128)} %get-tuple-element.354.refs_3_.refs_1_.refs_2_, f32[1,1152]{1,0:T(1,128)} %reshape.1151.gain_ref.refs_2_.refs_3_, ...), custom_call_target="tpu_custom_call", output_to_operand_aliasing={{0}: (0, {})} | custom-call | flops 12230590 | bytes 30081 | tf_op jit(solution)/shard_map/pallas_call | solution.py:544
  847.4 15.1 %collective-permute-done.53 = f32[2,72,1152]{2,1,0:T(8,128)} collective-permute-done((f32[2,72,1152]{2,1,0:T(8,128)}, f32[2,72,1152]{2,1,0:T(8,128)}, u32[]{:S(2)}, u32[]{:S(2)}) %collective-permute-start.53) | collective-permute-done | bytes 663584 | tf_op jit(solution)/shard_map/ppermute | solution.py:665
  866.8 5.7 fusion.4
  892.3 26.8 %collective-permute-done.58 = f32[1,72,1152]{2,1,0:T(8,128)} collective-permute-done((f32[1,72,1152]{2,1,0:T(8,128)}, f32[1,72,1152]{2,1,0:T(8,128)}, u32[]{:S(2)}, u32[]{:S(2)}) %collective-permute-start.58) | collective-permute-done | bytes 331808 | tf_op jit(solution)/shard_map/ppermute | solution.py:665
  921.4 26.8 %collective-permute-done.56 = f32[64,1729]{1,0:T(8,128)} collective-permute-done((f32[64,1729]{1,0:T(8,128)}, f32[64,1729]{1,0:T(8,128)}, u32[]{:S(2)}, u32[]{:S(2)}) %collective-permute-start.56) | collective-permute-done | bytes 442656 | tf_op jit(solution)/shard_map/ppermute | solution.py:665
  953.6 5.4 convolution_bitcast_fusion
  959.0 10.2 collective-permute-done.57
  973.1 3.7 copy-done.4
  976.8 14.7 %shard_map.313 = (f32[1152,2304]{1,0:T(8,128)}, f32[2304,1152]{1,0:T(8,128)}) custom-call(f32[1]{0:T(128)} %bitcast.115.scale_ref, f32[16,2,4,16,1152]{4,3,2,1,0:T(8,128)S(1)} %bitcast.385, f32[16,2,5,16,1152]{4,3,2,1,0:T(8,128)} %bitcast.398), custom_call_target="tpu_custom_call" | custom-call | bytes 42467 | tf_op jit(solution)/shard_map/pallas_call | solution.py:575
  991.7 11.0 %collective-permute-done.61 = f32[792,128]{1,0:T(8,128)S(1)} collective-permute-done((f32[792,128]{1,0:T(8,128)S(1)}, f32[792,128]{1,0:T(8,128)S(1)}, u32[]{:S(2)}, u32[]{:S(2)}) %collective-permute-start.61) | collective-permute-done | bytes 405536 | tf_op jit(solution)/shard_map/ppermute | solution.py:665
  1002.8 12.5 %collective-permute-done.62 = f32[792,128]{1,0:T(8,128)S(1)} collective-permute-done((f32[792,128]{1,0:T(8,128)S(1)}, f32[792,128]{1,0:T(8,128)S(1)}, u32[]{:S(2)}, u32[]{:S(2)}) %collective-permute-start.62) | collective-permute-done | bytes 405536 | tf_op jit(solution)/shard_map/ppermute | solution.py:665
  1015.4 42.0 %collective-permute-done.63 = f32[792,128]{1,0:T(8,128)S(1)} collective-permute-done((f32[792,128]{1,0:T(8,128)S(1)}, f32[792,128]{1,0:T(8,128)S(1)}, u32[]{:S(2)}, u32[]{:S(2)}) %collective-permute-start.63) | collective-permute-done | bytes 405536 | tf_op jit(solution)/shard_map/ppermute | solution.py:665
  1060.4 15.0 %all-gather.17.cloned.1.call-done = f32[16,144,1152]{2,1,0:T(8,128)} async-done(((f32[1,144,1152]{2,1,0:T(8,128)}), f32[16,144,1152]{2,1,0:T(8,128)}) %all-gather.17.cloned.1.call-update) | async-done | bytes 10616848 | tf_op jit(solution)/shard_map/all_gather | solution.py:680
  1075.4 4.0 copy-done.1
  1079.4 5.5 shard_map.314
  (420 shorter events, 202.5 us)
Async XLA Ops:
  7.2 98.7 %all-gather.7.cloned.1.call-start = ((), (), s32[]{:S(2)}) async-start(), calls=%async_computation | async-start | bytes 5640192 | tf_op jit(solution)/shard_map/all_gather | solution.py:680
  30.3 167.9 %all-gather.9.cloned.1.call-start = ((), (), s32[]{:S(2)}) async-start(), calls=%async_computation.1 | async-start | bytes 5013504 | tf_op jit(solution)/shard_map/all_gather | solution.py:680
  30.8 59.4 %collective-permute-start.3 = (f32[288,1152]{1,0:T(8,128)}, f32[288,1152]{1,0:T(8,128)}, u32[]{:S(2)}, u32[]{:S(2)}) collective-permute-start(f32[288,1152]{1,0:T(8,128)} %get-tuple-element.257), channel_id=1, source_target_pairs={{0,1},{1,0},{2,3},{3,2},{4,5},{5,4},{6,7},{7,6},{8,9},{9,8},{10,11... | collective-permute-start | bytes 3981320 | tf_op jit(solution)/shard_map/ppermute | solution.py:662
  31.0 59.3 %collective-permute-start.4 = (f32[288,1152]{1,0:T(8,128)}, f32[288,1152]{1,0:T(8,128)S(1)}, u32[]{:S(2)}, u32[]{:S(2)}) collective-permute-start(f32[288,1152]{1,0:T(8,128)} %get-tuple-element.258), channel_id=1, source_target_pairs={{0,1},{1,0},{2,3},{3,2},{4,5},{5,4},{6,7},{7,6},{8,9},{9,8},{10,11... | collective-permute-start | bytes 3981320 | tf_op jit(solution)/shard_map/ppermute | solution.py:662
  37.9 52.3 %collective-permute-start.5 = (f32[4,3,576]{2,0,1:T(4,128)S(1)}, f32[4,3,576]{2,0,1:T(4,128)S(1)}, u32[]{:S(2)}, u32[]{:S(2)}) collective-permute-start(f32[4,3,576]{2,0,1:T(4,128)S(1)} %get-tuple-element.528), channel_id=1, source_target_pairs={{0,1},{1,0},{2,3},{3,2},{4,5},{5,4},{6,7},{7,6},{8,9},{9,8},{10,11... | collective-permute-start | bytes 82952 | tf_op jit(solution)/shard_map/ppermute | solution.py:662
  98.0 172.8 %all-gather.11.cloned.1.call-start = ((), (), s32[]{:S(2)}) async-start(), calls=%async_computation.2 | async-start | bytes 6266880 | tf_op jit(solution)/shard_map/all_gather | solution.py:680
  98.3 54.0 %collective-permute-start.7 = (f32[512,1152]{1,0:T(8,128)}, f32[512,1152]{1,0:T(8,128)}, u32[]{:S(2)}, u32[]{:S(2)}) collective-permute-start(f32[512,1152]{1,0:T(8,128)} %constant_dynamic-slice_fusion.31), channel_id=1, source_target_pairs={{0,1},{1,0},{2,3},{3,2},{4,5},{5,4},{6,7},{7,6},{8,9},{9,8},{10,11... | collective-permute-start | bytes 7077896 | tf_op jit(solution)/shard_map/ppermute | solution.py:662
  103.8 41.6 %collective-permute-start.8 = (f32[288,1152]{1,0:T(8,128)}, f32[288,1152]{1,0:T(8,128)}, u32[]{:S(2)}, u32[]{:S(2)}) collective-permute-start(f32[288,1152]{1,0:T(8,128)} %copy-done.41), channel_id=1, source_target_pairs={{0,2},{2,0},{4,6},{6,4},{8,10},{10,8},{12,14},{14,12},{16,18},{18,... | collective-permute-start | bytes 3981320 | tf_op jit(solution)/shard_map/ppermute | solution.py:665
  152.3 38.9 %collective-permute-start.9 = (f32[512,1152]{1,0:T(8,128)}, f32[512,1152]{1,0:T(8,128)}, u32[]{:S(2)}, u32[]{:S(2)}) collective-permute-start(f32[512,1152]{1,0:T(8,128)} %collective-permute-done.7), channel_id=1, source_target_pairs={{0,2},{2,0},{4,6},{6,4},{8,10},{10,8},{12,14},{14,12},{16,18},{18,... | collective-permute-start | bytes 7077896 | tf_op jit(solution)/shard_map/ppermute | solution.py:665
  164.3 807.1 %all-gather.13.cloned.1.call-start = ((), (), s32[]{:S(2)}) async-start(), calls=%async_computation.3 | async-start | bytes 10027008 | tf_op jit(solution)/shard_map/all_gather | solution.py:680
  191.3 67.6 %collective-permute-start.11 = (f32[640,1152]{1,0:T(8,128)S(1)}, f32[640,1152]{1,0:T(8,128)}, u32[]{:S(2)}, u32[]{:S(2)}) collective-permute-start(f32[640,1152]{1,0:T(8,128)S(1)} %constant_dynamic-slice_fusion.29), channel_id=1, source_target_pairs={{0,1},{1,0},{2,3},{3,2},{4,5},{5,4},{6,7},{7,6},{8,9},{9,8},{10,11... | collective-permute-start | bytes 8847368 | tf_op jit(solution)/shard_map/ppermute | solution.py:662
  269.7 74.5 %collective-permute-start.15 = (f32[4,8,16,1152]{3,2,1,0:T(8,128)}, f32[4,8,16,1152]{3,2,1,0:T(8,128)}, u32[]{:S(2)}, u32[]{:S(2)}) collective-permute-start(f32[4,8,16,1152]{3,2,1,0:T(8,128)} %get-tuple-element.313), channel_id=1, source_target_pairs={{0,2},{2,0},{4,6},{6,4},{8,10},{10,8},{12,14},{14,12},{16,18},{18,... | collective-permute-start | bytes 7077896 | tf_op jit(solution)/shard_map/ppermute | solution.py:665
  269.9 77.4 %collective-permute-start.14 = (f32[4,8,16,1152]{3,2,1,0:T(8,128)}, f32[4,8,16,1152]{3,2,1,0:T(8,128)S(1)}, u32[]{:S(2)}, u32[]{:S(2)}) collective-permute-start(f32[4,8,16,1152]{3,2,1,0:T(8,128)} %get-tuple-element.311), channel_id=1, source_target_pairs={{0,2},{2,0},{4,6},{6,4},{8,10},{10,8},{12,14},{14,12},{16,18},{18,... | collective-permute-start | bytes 7077896 | tf_op jit(solution)/shard_map/ppermute | solution.py:665
  348.9 67.8 %collective-permute-start.16 = (f32[5,8,16,1152]{3,2,1,0:T(8,128)}, f32[5,8,16,1152]{3,2,1,0:T(8,128)}, u32[]{:S(2)}, u32[]{:S(2)}) collective-permute-start(f32[5,8,16,1152]{3,2,1,0:T(8,128)} %get-tuple-element.324), channel_id=1, source_target_pairs={{0,2},{2,0},{4,6},{6,4},{8,10},{10,8},{12,14},{14,12},{16,18},{18,... | collective-permute-start | bytes 8847368 | tf_op jit(solution)/shard_map/ppermute | solution.py:665
  349.1 72.5 %collective-permute-start.17 = (f32[5,8,16,1152]{3,2,1,0:T(8,128)}, f32[5,8,16,1152]{3,2,1,0:T(8,128)}, u32[]{:S(2)}, u32[]{:S(2)}) collective-permute-start(f32[5,8,16,1152]{3,2,1,0:T(8,128)} %get-tuple-element.326), channel_id=1, source_target_pairs={{0,2},{2,0},{4,6},{6,4},{8,10},{10,8},{12,14},{14,12},{16,18},{18,... | collective-permute-start | bytes 8847368 | tf_op jit(solution)/shard_map/ppermute | solution.py:665
  349.4 74.9 %collective-permute-start.18 = (f32[4,8,16,1152]{3,2,1,0:T(8,128)}, f32[4,8,16,1152]{3,2,1,0:T(8,128)}, u32[]{:S(2)}, u32[]{:S(2)}) collective-permute-start(f32[4,8,16,1152]{3,2,1,0:T(8,128)} %add.1242), channel_id=1, source_target_pairs={{0,1},{1,0},{2,3},{3,2},{4,5},{5,4},{6,7},{7,6},{8,9},{9,8},{10,11... | collective-permute-start | bytes 7077896 | tf_op jit(solution)/shard_map/ppermute | solution.py:662
  350.9 73.4 %collective-permute-start.19 = (f32[4,4,16,1152]{3,2,1,0:T(8,128)}, f32[4,4,16,1152]{3,2,1,0:T(8,128)}, u32[]{:S(2)}, u32[]{:S(2)}) collective-permute-start(f32[4,4,16,1152]{3,2,1,0:T(8,128)} %fusion.11), channel_id=1, source_target_pairs={{0,4},{2,6},{4,0},{6,2},{8,12},{10,14},{12,8},{14,10},{16,20},{18,... | collective-permute-start | bytes 3538952 | tf_op jit(solution)/shard_map/ppermute | solution.py:665
  424.3 81.1 %collective-permute-start.21 = (f32[5,8,16,1152]{3,2,1,0:T(8,128)}, f32[5,8,16,1152]{3,2,1,0:T(8,128)}, u32[]{:S(2)}, u32[]{:S(2)}) collective-permute-start(f32[5,8,16,1152]{3,2,1,0:T(8,128)} %add.1246), channel_id=1, source_target_pairs={{0,1},{1,0},{2,3},{3,2},{4,5},{5,4},{6,7},{7,6},{8,9},{9,8},{10,11... | collective-permute-start | bytes 8847368 | tf_op jit(solution)/shard_map/ppermute | solution.py:662
  424.5 78.3 %collective-permute-start.20 = (f32[4,8,16,1152]{3,2,1,0:T(8,128)}, f32[4,8,16,1152]{3,2,1,0:T(8,128)}, u32[]{:S(2)}, u32[]{:S(2)}) collective-permute-start(f32[4,8,16,1152]{3,2,1,0:T(8,128)} %get-tuple-element.339), channel_id=1, source_target_pairs={{0,2},{2,0},{4,6},{6,4},{8,10},{10,8},{12,14},{14,12},{16,18},{18,... | collective-permute-start | bytes 7077896 | tf_op jit(solution)/shard_map/ppermute | solution.py:665
  424.5 91.0 %collective-permute-start.22 = (f32[4,8,16,1152]{3,2,1,0:T(8,128)}, f32[4,8,16,1152]{3,2,1,0:T(8,128)}, u32[]{:S(2)}, u32[]{:S(2)}) collective-permute-start(f32[4,8,16,1152]{3,2,1,0:T(8,128)} %get-tuple-element.363), channel_id=1, source_target_pairs={{0,2},{2,0},{4,6},{6,4},{8,10},{10,8},{12,14},{14,12},{16,18},{18,... | collective-permute-start | bytes 7077896 | tf_op jit(solution)/shard_map/ppermute | solution.py:665
  425.0 84.6 %collective-permute-start.23 = (f32[5,4,16,1152]{3,2,1,0:T(8,128)}, f32[5,4,16,1152]{3,2,1,0:T(8,128)}, u32[]{:S(2)}, u32[]{:S(2)}) collective-permute-start(f32[5,4,16,1152]{3,2,1,0:T(8,128)} %fusion.8), channel_id=1, source_target_pairs={{0,4},{2,6},{4,0},{6,2},{8,12},{10,14},{12,8},{14,10},{16,20},{18,... | collective-permute-start | bytes 4423688 | tf_op jit(solution)/shard_map/ppermute | solution.py:665
  505.4 81.6 %collective-permute-start.28 = (f32[5,8,16,1152]{3,2,1,0:T(8,128)}, f32[5,8,16,1152]{3,2,1,0:T(8,128)}, u32[]{:S(2)}, u32[]{:S(2)}) collective-permute-start(f32[5,8,16,1152]{3,2,1,0:T(8,128)} %get-tuple-element.377), channel_id=1, source_target_pairs={{0,2},{2,0},{4,6},{6,4},{8,10},{10,8},{12,14},{14,12},{16,18},{18,... | collective-permute-start | bytes 8847368 | tf_op jit(solution)/shard_map/ppermute | solution.py:665
  506.5 41.7 %collective-permute-start.24 = (f32[4,4,16,1152]{3,2,1,0:T(8,128)}, f32[4,4,16,1152]{3,2,1,0:T(8,128)}, u32[]{:S(2)}, u32[]{:S(2)}) collective-permute-start(f32[4,4,16,1152]{3,2,1,0:T(8,128)} %fusion.10), channel_id=1, source_target_pairs={{0,4},{2,6},{4,0},{6,2},{8,12},{10,14},{12,8},{14,10},{16,20},{18,... | collective-permute-start | bytes 3538952 | tf_op jit(solution)/shard_map/ppermute | solution.py:665
  507.7 40.6 %collective-permute-start.25 = (f32[4,4,16,1152]{3,2,1,0:T(8,128)}, f32[4,4,16,1152]{3,2,1,0:T(8,128)}, u32[]{:S(2)}, u32[]{:S(2)}) collective-permute-start(f32[4,4,16,1152]{3,2,1,0:T(8,128)} %add_add_fusion), channel_id=1, source_target_pairs={{0,1},{1,0},{2,3},{3,2},{4,5},{5,4},{6,7},{7,6},{8,9},{9,8},{10,11... | collective-permute-start | bytes 3538952 | tf_op jit(solution)/shard_map/ppermute | solution.py:662
  519.9 94.6 %collective-permute-start.32 = (f32[5,8,16,1152]{3,2,1,0:T(8,128)}, f32[5,8,16,1152]{3,2,1,0:T(8,128)}, u32[]{:S(2)}, u32[]{:S(2)}) collective-permute-start(f32[5,8,16,1152]{3,2,1,0:T(8,128)} %get-tuple-element.393), channel_id=1, source_target_pairs={{0,2},{2,0},{4,6},{6,4},{8,10},{10,8},{12,14},{14,12},{16,18},{18,... | collective-permute-start | bytes 8847368 | tf_op jit(solution)/shard_map/ppermute | solution.py:665
  550.4 41.2 %collective-permute-start.29 = (f32[5,4,16,1152]{3,2,1,0:T(8,128)}, f32[5,4,16,1152]{3,2,1,0:T(8,128)}, u32[]{:S(2)}, u32[]{:S(2)}) collective-permute-start(f32[5,4,16,1152]{3,2,1,0:T(8,128)} %bitcast_add_fusion.3), channel_id=1, source_target_pairs={{0,1},{1,0},{2,3},{3,2},{4,5},{5,4},{6,7},{7,6},{8,9},{9,8},{10,11... | collective-permute-start | bytes 4423688 | tf_op jit(solution)/shard_map/ppermute | solution.py:662
  606.2 39.2 %collective-permute-start.30 = (f32[8,72,1152]{2,1,0:T(8,128)}, f32[8,72,1152]{2,1,0:T(8,128)}, u32[]{:S(2)}, u32[]{:S(2)}) collective-permute-start(f32[8,72,1152]{2,1,0:T(8,128)} %get-tuple-element.390), channel_id=1, source_target_pairs={{0,2},{2,0},{4,6},{6,4},{8,10},{10,8},{12,14},{14,12},{16,18},{18,... | collective-permute-start | bytes 7962632 | tf_op jit(solution)/shard_map/ppermute | solution.py:665
  647.4 48.1 %collective-permute-start.35 = (f32[8,72,1152]{2,1,0:T(8,128)}, f32[8,72,1152]{2,1,0:T(8,128)}, u32[]{:S(2)}, u32[]{:S(2)}) collective-permute-start(f32[8,72,1152]{2,1,0:T(8,128)} %get-tuple-element.403), channel_id=1, source_target_pairs={{0,2},{2,0},{4,6},{6,4},{8,10},{10,8},{12,14},{14,12},{16,18},{18,... | collective-permute-start | bytes 7962632 | tf_op jit(solution)/shard_map/ppermute | solution.py:665
  649.1 38.8 %collective-permute-start.36 = (f32[4,1,16,1152]{3,2,0,1:T(8,128)S(1)}, f32[4,1,16,1152]{3,2,0,1:T(8,128)}, u32[]{:S(2)}, u32[]{:S(2)}) collective-permute-start(f32[4,1,16,1152]{3,2,0,1:T(8,128)S(1)} %fusion.44), channel_id=1, source_target_pairs={{0,16},{2,18},{4,20},{6,22},{8,24},{10,26},{12,28},{14,30},{16,0},... | collective-permute-start | bytes 884744 | tf_op jit(solution)/shard_map/ppermute | solution.py:665
  651.9 38.3 %collective-permute-start.38 = (f32[5,2,16,1152]{3,2,0,1:T(8,128)}, f32[5,2,16,1152]{3,2,0,1:T(8,128)}, u32[]{:S(2)}, u32[]{:S(2)}) collective-permute-start(f32[5,2,16,1152]{3,2,0,1:T(8,128)} %fusion.15), channel_id=1, source_target_pairs={{0,8},{2,10},{4,12},{6,14},{8,0},{10,2},{12,4},{14,6},{16,24},{18,... | collective-permute-start | bytes 2211848 | tf_op jit(solution)/shard_map/ppermute | solution.py:665
  652.3 39.9 %collective-permute-start.37 = (f32[5,4,16,1152]{3,2,1,0:T(8,128)S(1)}, f32[5,4,16,1152]{3,2,1,0:T(8,128)}, u32[]{:S(2)}, u32[]{:S(2)}) collective-permute-start(f32[5,4,16,1152]{3,2,1,0:T(8,128)S(1)} %copy-done.38), channel_id=1, source_target_pairs={{0,4},{2,6},{4,0},{6,2},{8,12},{10,14},{12,8},{14,10},{16,20},{18,... | collective-permute-start | bytes 4423688 | tf_op jit(solution)/shard_map/ppermute | solution.py:665
  655.7 43.2 %collective-permute-start.39 = (f32[4,72,1152]{2,1,0:T(8,128)}, f32[4,72,1152]{2,1,0:T(8,128)}, u32[]{:S(2)}, u32[]{:S(2)}) collective-permute-start(f32[4,72,1152]{2,1,0:T(8,128)} %get-tuple-element.500), channel_id=1, source_target_pairs={{0,1},{1,0},{2,3},{3,2},{4,5},{5,4},{6,7},{7,6},{8,9},{9,8},{10,11... | collective-permute-start | bytes 3981320 | tf_op jit(solution)/shard_map/ppermute | solution.py:662
  699.0 272.3 %all-gather.15.cloned.1.call-start = ((), (), s32[]{:S(2)}) async-start(), calls=%async_computation.4 | async-start | bytes 12533760 | tf_op jit(solution)/shard_map/all_gather | solution.py:680
  716.9 44.4 %collective-permute-start.41 = (f32[8,72,1152]{2,1,0:T(8,128)}, f32[8,72,1152]{2,1,0:T(8,128)}, u32[]{:S(2)}, u32[]{:S(2)}) collective-permute-start(f32[8,72,1152]{2,1,0:T(8,128)} %get-tuple-element.421), channel_id=1, source_target_pairs={{0,2},{2,0},{4,6},{6,4},{8,10},{10,8},{12,14},{14,12},{16,18},{18,... | collective-permute-start | bytes 7962632 | tf_op jit(solution)/shard_map/ppermute | solution.py:665
  717.3 38.5 %collective-permute-start.43 = (f32[5,2,16,1152]{3,2,0,1:T(8,128)}, f32[5,2,16,1152]{3,2,0,1:T(8,128)}, u32[]{:S(2)}, u32[]{:S(2)}) collective-permute-start(f32[5,2,16,1152]{3,2,0,1:T(8,128)} %fusion.14), channel_id=1, source_target_pairs={{0,8},{2,10},{4,12},{6,14},{8,0},{10,2},{12,4},{14,6},{16,24},{18,... | collective-permute-start | bytes 2211848 | tf_op jit(solution)/shard_map/ppermute | solution.py:665
  719.0 39.1 %collective-permute-start.42 = (f32[4,72,1152]{2,1,0:T(8,128)}, f32[4,72,1152]{2,1,0:T(8,128)}, u32[]{:S(2)}, u32[]{:S(2)}) collective-permute-start(f32[4,72,1152]{2,1,0:T(8,128)} %fusion.9), channel_id=1, source_target_pairs={{0,4},{2,6},{4,0},{6,2},{8,12},{10,14},{12,8},{14,10},{16,20},{18,... | collective-permute-start | bytes 3981320 | tf_op jit(solution)/shard_map/ppermute | solution.py:665
  719.4 46.5 %collective-permute-start.49 = (f32[5,1,16,1152]{3,2,0,1:T(8,128)}, f32[5,1,16,1152]{3,2,0,1:T(8,128)}, u32[]{:S(2)}, u32[]{:S(2)}) collective-permute-start(f32[5,1,16,1152]{3,2,0,1:T(8,128)} %fusion.30), channel_id=1, source_target_pairs={{0,16},{2,18},{4,20},{6,22},{8,24},{10,26},{12,28},{14,30},{16,0},... | collective-permute-start | bytes 1105928 | tf_op jit(solution)/shard_map/ppermute | solution.py:665
  765.9 45.0 %collective-permute-start.46 = (f32[8,72,1152]{2,1,0:T(8,128)}, f32[8,72,1152]{2,1,0:T(8,128)}, u32[]{:S(2)}, u32[]{:S(2)}) collective-permute-start(f32[8,72,1152]{2,1,0:T(8,128)} %get-tuple-element.431), channel_id=1, source_target_pairs={{0,2},{2,0},{4,6},{6,4},{8,10},{10,8},{12,14},{14,12},{16,18},{18,... | collective-permute-start | bytes 7962632 | tf_op jit(solution)/shard_map/ppermute | solution.py:665
  770.1 35.8 %collective-permute-start.50 = (f32[5,1,16,1152]{3,2,0,1:T(8,128)}, f32[5,1,16,1152]{3,2,0,1:T(8,128)S(1)}, u32[]{:S(2)}, u32[]{:S(2)}) collective-permute-start(f32[5,1,16,1152]{3,2,0,1:T(8,128)} %fusion.28), channel_id=1, source_target_pairs={{0,16},{2,18},{4,20},{6,22},{8,24},{10,26},{12,28},{14,30},{16,0},... | collective-permute-start | bytes 1105928 | tf_op jit(solution)/shard_map/ppermute | solution.py:665
  772.7 35.7 %collective-permute-start.47 = (f32[4,72,1152]{2,1,0:T(8,128)}, f32[4,72,1152]{2,1,0:T(8,128)}, u32[]{:S(2)}, u32[]{:S(2)}) collective-permute-start(f32[4,72,1152]{2,1,0:T(8,128)} %get-tuple-element.434), channel_id=1, source_target_pairs={{0,4},{2,6},{4,0},{6,2},{8,12},{10,14},{12,8},{14,10},{16,20},{18,... | collective-permute-start | bytes 3981320 | tf_op jit(solution)/shard_map/ppermute | solution.py:665
  772.7 35.7 %collective-permute-start.48 = (f32[4,72,1152]{2,1,0:T(8,128)}, f32[4,72,1152]{2,1,0:T(8,128)}, u32[]{:S(2)}, u32[]{:S(2)}) collective-permute-start(f32[4,72,1152]{2,1,0:T(8,128)} %bitcast_add_fusion.5), channel_id=1, source_target_pairs={{0,1},{1,0},{2,3},{3,2},{4,5},{5,4},{6,7},{7,6},{8,9},{9,8},{10,11... | collective-permute-start | bytes 3981320 | tf_op jit(solution)/shard_map/ppermute | solution.py:662
  815.4 260.0 %all-gather.17.cloned.1.call-start = ((), (), s32[]{:S(2)}) async-start(), calls=%async_computation.5 | async-start | bytes 11280384 | tf_op jit(solution)/shard_map/all_gather | solution.py:680
  815.4 49.3 %collective-permute-start.52 = (f32[4,72,1152]{2,1,0:T(8,128)}, f32[4,72,1152]{2,1,0:T(8,128)}, u32[]{:S(2)}, u32[]{:S(2)}) collective-permute-start(f32[4,72,1152]{2,1,0:T(8,128)} %get-tuple-element.444), channel_id=1, source_target_pairs={{0,4},{2,6},{4,0},{6,2},{8,12},{10,14},{12,8},{14,10},{16,20},{18,... | collective-permute-start | bytes 3981320 | tf_op jit(solution)/shard_map/ppermute | solution.py:665
  818.9 43.6 %collective-permute-start.53 = (f32[2,72,1152]{2,1,0:T(8,128)}, f32[2,72,1152]{2,1,0:T(8,128)}, u32[]{:S(2)}, u32[]{:S(2)}) collective-permute-start(f32[2,72,1152]{2,1,0:T(8,128)} %add_bitcast_fusion.5), channel_id=1, source_target_pairs={{0,8},{2,10},{4,12},{6,14},{8,0},{10,2},{12,4},{14,6},{16,24},{18,... | collective-permute-start | bytes 1990664 | tf_op jit(solution)/shard_map/ppermute | solution.py:665
  873.7 45.4 %collective-permute-start.58 = (f32[1,72,1152]{2,1,0:T(8,128)}, f32[1,72,1152]{2,1,0:T(8,128)}, u32[]{:S(2)}, u32[]{:S(2)}) collective-permute-start(f32[1,72,1152]{2,1,0:T(8,128)} %bitcast_add_fusion.17), channel_id=1, source_target_pairs={{0,16},{2,18},{4,20},{6,22},{8,24},{10,26},{12,28},{14,30},{16,0},... | collective-permute-start | bytes 995336 | tf_op jit(solution)/shard_map/ppermute | solution.py:665
  875.7 72.5 %collective-permute-start.56 = (f32[64,1729]{1,0:T(8,128)}, f32[64,1729]{1,0:T(8,128)}, u32[]{:S(2)}, u32[]{:S(2)}) collective-permute-start(f32[64,1729]{1,0:T(8,128)} %copy.469), channel_id=1, source_target_pairs={{0,16},{2,18},{4,20},{6,22},{8,24},{10,26},{12,28},{14,30},{16,0},... | collective-permute-start | bytes 1327880 | tf_op jit(solution)/shard_map/ppermute | solution.py:665
  877.7 72.3 %collective-permute-start.55 = (f32[2,72,1152]{2,1,0:T(8,128)}, f32[2,72,1152]{2,1,0:T(8,128)}, u32[]{:S(2)}, u32[]{:S(2)}) collective-permute-start(f32[2,72,1152]{2,1,0:T(8,128)} %add_bitcast_fusion.4), channel_id=1, source_target_pairs={{0,8},{2,10},{4,12},{6,14},{8,0},{10,2},{12,4},{14,6},{16,24},{18,... | collective-permute-start | bytes 1990664 | tf_op jit(solution)/shard_map/ppermute | solution.py:665
  1015.4 42.1 %collective-permute-start.63 = (f32[792,128]{1,0:T(8,128)S(1)}, f32[792,128]{1,0:T(8,128)S(1)}, u32[]{:S(2)}, u32[]{:S(2)}) collective-permute-start(f32[792,128]{1,0:T(8,128)S(1)} %add.1374), channel_id=1, source_target_pairs={{0,16},{2,18},{4,20},{6,22},{8,24},{10,26},{12,28},{14,30},{16,0},... | collective-permute-start | bytes 1216520 | tf_op jit(solution)/shard_map/ppermute | solution.py:665
  (94 other events, 1235.8 us)
Sparse Core Ops, SparseCore 0:
  30.4 56.6 all-gather.6
  98.2 53.7 all-gather.8
  164.4 60.0 all-gather.10
  699.1 108.8 all-gather.12
  815.5 137.2 all-gather.14
  971.5 103.8 all-gather.16
